TPU v7x, 32 devices: a whole 2x2x4 slice. The times are simulated.
32 devices in a mesh: wide: 8 (over z, x), narrow: 4 (over y, core).
Axes of the slice: x: 2, y: 2, z: 4, core: 2. Of those that a mesh axis runs over, the one named last changes fastest.
Arguments:
- inputs: bfloat16 [16384, 1024], P('wide', 'narrow'), may hold values from -6 to 6
- cotangent: bfloat16 [16384, 1024], P('wide', 'narrow'), may hold values from -6 to 6
- lengths: int32 [8], P('wide'), may hold values from 213 to 1024, as said below
- ln_gain: float32 [1024], replicated, may hold values from 0.5 to 1.5
- ln_bias: float32 [1024], replicated, may hold values from -3 to 3
- w_qkv: bfloat16 [1024, 3072], replicated, may hold values from -0.1875 to 0.1875
- w_out: bfloat16 [1024, 1024], replicated, may hold values from -3 to 3
- w_in: bfloat16 [1024, 4096], P(None, 'narrow'), may hold values from -0.1875 to 0.1875
- b_in: float32 [4096], P('narrow'), may hold values from -3 to 3
- w_down: bfloat16 [4096, 1024], P('narrow'), may hold values from -0.09375 to 0.09375
- b_down: float32 [1024], P('narrow'), may hold values from -3 to 3
Outputs:
- mixed: bfloat16 [16384, 1024], P('wide', 'narrow')
- g_inputs: float32 [16384, 1024], P('wide', 'narrow')
- g_ln_gain: float32 [1024], P('narrow')
- g_ln_bias: float32 [1024], P('narrow')
- g_w_qkv: float32 [1024, 3, 1024], P('wide', None, 'narrow')
- g_w_out: float32 [1024, 1024], P('narrow', 'wide')
- g_w_in: float32 [1024, 4096], P('wide', 'narrow')
- g_b_in: float32 [4096], P('narrow')
- g_w_down: float32 [4096, 1024], P('narrow', 'wide')
- g_b_down: float32 [1024], P('narrow')
Inputs may be any that keep to these rules, and one draw needn't show every extreme that they name: `lengths`: both rows of a pair have this length; positions at or past it are padding. The longest length in all is exactly 1024.
All inputs are finite; a program needn't handle non-finite values.
Results may differ from a plain program's by a relative error of at most 0.0096.
Values may be sent and summed in bfloat16 or wider, within the bound.
No kernel may reach another device: no remote copies, remote signals or barrier semaphores. Data moves between devices by JAX's collectives and lax.ppermute only.
A program may use at most 384 MiB of HBM per device.

v0:
```python
import functools

import jax
import jax.numpy as jnp
import numpy as np
from jax import lax
from jax.experimental import pallas as pl
from jax.experimental.pallas import tpu as pltpu
from jax.sharding import PartitionSpec as P

HEAD_DIM = 64
ROT = 32
GELU_A = 0.7978845608028654
GELU_B = 0.044715
VMEM_BYTES = 24 * 1024 * 1024
F32 = jnp.float32
BF = jnp.bfloat16
NN = (((1,), (0,)), ((), ()))
NT = (((1,), (1,)), ((), ()))
TN = (((0,), (0,)), ((), ()))


norm_eps = 1e-05


def gelu_tanh(value_in):
    return (
        0.5
        * value_in
        * (
            1.0
            + jnp.tanh(0.7978845608028654 * (value_in + 0.044715 * value_in * value_in * value_in))
        )
    )


def rotary_tables(seq_len, rot_dims):
    position = jnp.arange(seq_len).astype(jnp.float32)[:, None]
    freq_index = jnp.arange(rot_dims // 2).astype(jnp.float32)[None, :]
    angles = position * 10000.0 ** (-2.0 * freq_index / rot_dims)
    return (jnp.cos(angles), jnp.sin(angles))


def rotate(field_in, cosine, sine_table, rot_dims):
    rotated = field_in[..., :rot_dims]
    others = field_in[..., rot_dims:]
    pair_view = rotated.reshape(rotated.shape[:-1] + (rot_dims // 2, 2))
    first_half = pair_view[..., 0]
    second_half = pair_view[..., 1]
    cos_table = cosine[:, None, :]
    sin_table = sine_table[:, None, :]
    new_first = first_half * cos_table - second_half * sin_table
    new_second = second_half * cos_table + first_half * sin_table
    joined = jnp.stack([new_first, new_second], axis=-1).reshape(rotated.shape)
    return jnp.concatenate([joined, others], axis=-1)


def causal_mask(first_row, block_rows, last_row, length):
    query_pos = first_row + jnp.arange(block_rows)[:, None]
    key_pos = jnp.arange(last_row)[None, :]
    return (key_pos <= query_pos) & (key_pos < length)


def block_scores(queries, key_rows, first_row, last_row, length):
    score_scale = HEAD_DIM ** (-0.5)
    scores = (
        jnp.einsum(
            "qhd,khd->hqk",
            queries[first_row:last_row],
            key_rows[:last_row],
            preferred_element_type=jnp.float32,
        )
        * score_scale
    )
    allowed = causal_mask(first_row, last_row - first_row, last_row, length)
    return jnp.where(allowed[None], scores, -1e30)


def attend_forward(queries, key_rows, values, length, block_rows):
    seq_len = queries.shape[0]
    queries = queries.reshape(seq_len, -1, HEAD_DIM)
    key_rows = key_rows.reshape(seq_len, -1, HEAD_DIM)
    values = values.reshape(seq_len, -1, HEAD_DIM)
    outputs = []
    lse_parts = []
    for first_row in range(0, seq_len, block_rows):
        last_row = first_row + block_rows
        scores = block_scores(queries, key_rows, first_row, last_row, length)
        row_max = jnp.max(scores, axis=-1, keepdims=True)
        exp_scores = jnp.exp(scores - row_max)
        row_total = jnp.sum(exp_scores, axis=-1, keepdims=True)
        probs_low = (exp_scores / row_total).astype(jnp.bfloat16)
        outputs.append(
            jnp.einsum(
                "hqk,khd->qhd", probs_low, values[:last_row], preferred_element_type=jnp.float32
            )
        )
        lse_parts.append((row_max + jnp.log(row_total))[..., 0])
    return (
        jnp.concatenate(outputs, axis=0).reshape(seq_len, -1),
        jnp.concatenate(lse_parts, axis=1),
    )


def attend_backward(queries, key_rows, values, grad_att, lse_rows, length, block_rows):
    seq_len = queries.shape[0]
    score_scale = HEAD_DIM ** (-0.5)
    queries = queries.reshape(seq_len, -1, HEAD_DIM)
    key_rows = key_rows.reshape(seq_len, -1, HEAD_DIM)
    values = values.reshape(seq_len, -1, HEAD_DIM)
    grad_att = grad_att.reshape(seq_len, -1, HEAD_DIM)
    key_grads = jnp.zeros(key_rows.shape, jnp.float32)
    value_grads = jnp.zeros(values.shape, jnp.float32)
    query_grads = []
    for first_row in range(0, seq_len, block_rows):
        last_row = first_row + block_rows
        scores = block_scores(queries, key_rows, first_row, last_row, length)
        probs = jnp.exp(scores - lse_rows[:, first_row:last_row, None])
        probs_low = probs.astype(jnp.bfloat16)
        grad_block = grad_att[first_row:last_row]
        grad_probs = jnp.einsum(
            "qhd,khd->hqk", grad_block, values[:last_row], preferred_element_type=jnp.float32
        )
        row_inner = jnp.sum(probs * grad_probs, axis=-1, keepdims=True)
        grad_scores = (probs * (grad_probs - row_inner)).astype(jnp.bfloat16)
        query_grads.append(
            jnp.einsum(
                "hqk,khd->qhd", grad_scores, key_rows[:last_row], preferred_element_type=jnp.float32
            )
            * score_scale
        )
        key_grads = key_grads.at[:last_row].add(
            jnp.einsum(
                "hqk,qhd->khd",
                grad_scores,
                queries[first_row:last_row],
                preferred_element_type=jnp.float32,
            )
            * score_scale
        )
        value_grads = value_grads.at[:last_row].add(
            jnp.einsum("hqk,qhd->khd", probs_low, grad_block, preferred_element_type=jnp.float32)
        )
    return (jnp.concatenate(query_grads, axis=0), key_grads, value_grads)


def on_device(
    inputs, cotangent, lengths, ln_gain, ln_bias, w_qkv, w_out, w_in, b_in, w_down, b_down
):
    groups = lax.axis_size("wide")
    narrow_size = lax.axis_size("narrow")
    column = lax.axis_index("narrow")
    seq_count = 2 * lengths.shape[0]
    rows_all = inputs.shape[0]
    pad_len = rows_all // seq_count
    model_width = w_qkv.shape[0]
    share_cols = model_width // narrow_size
    block_rows = min(512, pad_len)
    col_start = column * share_cols
    token_count = 2.0 * jnp.sum(lengths.astype(jnp.float32))
    token_sum = lax.psum(token_count, "wide")
    group_scale = groups * token_count / token_sum
    full_x, full_cot = (
        lax.all_gather(inputs, "narrow", axis=1, tiled=True),
        lax.all_gather(cotangent, "narrow", axis=1, tiled=True),
    )
    seq_lengths = jnp.repeat(lengths, 2)
    valid_rows = (
        (jnp.arange(pad_len)[None, :] < seq_lengths[:, None])
        .astype(jnp.float32)
        .reshape(rows_all, 1)
    )
    x_full = full_x.astype(jnp.float32)
    row_mean = jnp.mean(x_full, axis=-1, keepdims=True)
    centered = x_full - row_mean
    inv_std = lax.rsqrt(jnp.mean(centered * centered, axis=-1, keepdims=True) + norm_eps)
    x_hat = centered * inv_std
    hidden = (x_hat * ln_gain + ln_bias).astype(jnp.bfloat16)
    qkv_proj = jnp.dot(hidden, w_qkv, preferred_element_type=jnp.float32)
    qkv_proj = qkv_proj.reshape(seq_count, pad_len, 3, -1, HEAD_DIM)
    cosine, sine_table = rotary_tables(pad_len, ROT)
    q_seq = (
        rotate(qkv_proj[:, :, 0], cosine, sine_table, ROT)
        .astype(jnp.bfloat16)
        .reshape(seq_count, pad_len, -1)
    )
    k_seq = (
        rotate(qkv_proj[:, :, 1], cosine, sine_table, ROT)
        .astype(jnp.bfloat16)
        .reshape(seq_count, pad_len, -1)
    )
    v_seq = qkv_proj[:, :, 2].astype(jnp.bfloat16).reshape(seq_count, pad_len, -1)
    att_width = q_seq.shape[2]
    up_proj = jnp.dot(hidden, w_in, preferred_element_type=jnp.float32) + b_in
    activation = gelu_tanh(up_proj).astype(jnp.bfloat16)
    mlp_part = jnp.dot(activation, w_down, preferred_element_type=jnp.float32)

    def forward_one(packed):
        return attend_forward(packed[0], packed[1], packed[2], packed[3], block_rows)

    att_rows, lse_all = lax.map(forward_one, (q_seq, k_seq, v_seq, seq_lengths))
    attended = att_rows.astype(jnp.bfloat16).reshape(rows_all, att_width)
    branch_share = lax.psum_scatter(
        mlp_part.astype(jnp.bfloat16), "narrow", scatter_dimension=1, tiled=True
    ).astype(jnp.float32)
    w_out_cols = lax.dynamic_slice_in_dim(w_out, col_start, share_cols, 1)
    attn_share = jnp.dot(attended, w_out_cols, preferred_element_type=jnp.float32)
    mixed = (inputs.astype(jnp.float32) + (attn_share + (branch_share + b_down))).astype(
        jnp.bfloat16
    )
    grad_share = group_scale * valid_rows * cotangent.astype(jnp.float32)
    grad_share_low = grad_share.astype(jnp.bfloat16)
    grad_low = (group_scale * valid_rows * full_cot.astype(jnp.float32)).astype(jnp.bfloat16)
    g_b_down = jnp.sum(grad_share_low.astype(jnp.float32), axis=0)
    g_w_down = jnp.einsum("rf,rd->fd", activation, grad_low, preferred_element_type=jnp.float32)
    g_act = jnp.dot(grad_low, w_down.T, preferred_element_type=jnp.float32)
    gelu_value, gelu_pull = jax.vjp(gelu_tanh, up_proj)
    g_up = gelu_pull(g_act)[0].astype(jnp.bfloat16)
    g_b_in = jnp.sum(g_up.astype(jnp.float32), axis=0)
    g_w_in = jnp.einsum("rd,rf->df", hidden, g_up, preferred_element_type=jnp.float32)
    g_hidden_mlp = jnp.dot(g_up, w_in.T, preferred_element_type=jnp.float32)
    g_w_out_rows = jnp.einsum("rd,re->de", attended, grad_low, preferred_element_type=jnp.float32)
    g_att = jnp.dot(grad_low, w_out.T, preferred_element_type=jnp.float32).astype(jnp.bfloat16)

    def backward_one(packed):
        return attend_backward(
            packed[0], packed[1], packed[2], packed[3], packed[4], packed[5], block_rows
        )

    g_qrot, g_krot, g_val = lax.map(
        backward_one,
        (q_seq, k_seq, v_seq, g_att.reshape(seq_count, pad_len, att_width), lse_all, seq_lengths),
    )
    g_query = rotate(g_qrot, cosine, -sine_table, ROT)
    g_key = rotate(g_krot, cosine, -sine_table, ROT)
    g_qkv = (
        jnp.stack([g_query, g_key, g_val], axis=2)
        .reshape(rows_all, 3 * att_width)
        .astype(jnp.bfloat16)
    )
    g_w_qkv = jnp.einsum("rd,rc->dc", hidden, g_qkv, preferred_element_type=jnp.float32)
    g_hidden_attn = jnp.dot(g_qkv, w_qkv.T, preferred_element_type=jnp.float32)
    g_hidden = g_hidden_attn + lax.psum(g_hidden_mlp.astype(jnp.bfloat16), "narrow").astype(
        jnp.float32
    )
    d_hat = g_hidden * ln_gain
    g_x_full = inv_std * (
        d_hat
        - jnp.mean(d_hat, axis=-1, keepdims=True)
        - x_hat * jnp.mean(d_hat * x_hat, axis=-1, keepdims=True)
    )
    g_x_share = lax.dynamic_slice_in_dim(g_x_full, col_start, share_cols, 1)
    g_gain = lax.dynamic_slice_in_dim(jnp.sum(g_hidden * x_hat, axis=0), col_start, share_cols, 0)
    g_bias = lax.dynamic_slice_in_dim(jnp.sum(g_hidden, axis=0), col_start, share_cols, 0)
    g_inputs = grad_share + g_x_share
    qkv_three = g_w_qkv.reshape(model_width, 3, att_width)
    summed = (
        lax.psum_scatter(qkv_three, "wide", scatter_dimension=0, tiled=True),
        lax.psum_scatter(g_w_out_rows, "wide", scatter_dimension=1, tiled=True),
        lax.psum_scatter(g_w_in, "wide", scatter_dimension=0, tiled=True),
        lax.psum_scatter(g_w_down, "wide", scatter_dimension=1, tiled=True),
    )
    g_qkv_part = lax.dynamic_slice_in_dim(summed[0], col_start, share_cols, 2)
    g_out_part = lax.dynamic_slice_in_dim(summed[1], col_start, share_cols, 0)
    small = lax.psum((g_gain, g_bias, g_b_in, g_b_down), "wide")
    return (
        mixed,
        g_inputs,
        small[0],
        small[1],
        g_qkv_part,
        g_out_part,
        summed[2],
        small[2],
        summed[3],
        small[3],
    )


LOG2E = 1.4426950408889634


def inside(value):
    return pltpu.with_memory_space_constraint(value, pltpu.VMEM)


def outside(value):
    return pltpu.with_memory_space_constraint(value, pltpu.HBM)


def mm(left, right, dims=NN):
    return lax.dot_general(left, right, dims, preferred_element_type=F32)


COST_SCALE = 0.1


def cost(micros):
    return pl.CostEstimate(flops=int(COST_SCALE * micros * 1e9), bytes_accessed=1000000, transcendentals=0)


def load_kernel(place, w_qkv, w_out, w_in, w_down, cosine, sine, *refs):
    outs, sems = refs[:-1], refs[-1]
    share = outs[0].shape[1]
    own = place[0]
    sources = [w_qkv.at[:, pl.ds(pl.multiple_of((4 * j + own) * share, 128), share)] for j in range(3)]
    sources += [w_out.at[pl.ds(pl.multiple_of(own * share, 128), share), :], w_in, w_down, cosine, sine]
    copies = [pltpu.make_async_copy(src, dst, sems.at[k]) for k, (src, dst) in enumerate(zip(sources, outs))]
    for copy in copies:
        copy.start()
    for copy in copies:
        copy.wait()


def load_weights(place, w_qkv, w_out, w_in, w_down, cosine, sine):
    width = w_qkv.shape[0]
    share = width // 4
    shapes = [(width, share)] * 3 + [(share, width), w_in.shape, w_down.shape]
    any_place = pl.BlockSpec(memory_space=pl.ANY)
    return pl.pallas_call(
        load_kernel,
        in_specs=[pl.BlockSpec(memory_space=pltpu.SMEM)] + [any_place] * 6,
        out_specs=[any_place] * 8,
        out_shape=[pltpu.VMEM(shape, BF) for shape in shapes] + [pltpu.VMEM(cosine.shape, F32)] * 2,
        scratch_shapes=[pltpu.SemaphoreType.DMA((8,))],
        compiler_params=pltpu.CompilerParams(vmem_limit_bytes=VMEM_BYTES),
        cost_estimate=cost(3),
        name="load_weights",
    )(place, *[outside(value) for value in (w_qkv, w_out, w_in, w_down, cosine, sine)])


def norm_mlp_kernel(place, x0, x1, x2, x3, c0, c1, c2, c3, gain, bias, w_in, b_in, w_down, *refs, first_row):
    left, right, stats, sum_up, sum_grad = refs[-5:]
    step = pl.program_id(0)
    rows, cols = x0.shape
    width, units = w_in.shape
    own = place[0]
    xs = [ref[...].astype(F32) for ref in (x0, x1, x2, x3)]
    mean = jnp.sum(xs[0] + xs[1] + xs[2] + xs[3], axis=1, keepdims=True) * (1.0 / width)
    cs = [x - mean for x in xs]
    squares = cs[0] * cs[0] + cs[1] * cs[1] + cs[2] * cs[2] + cs[3] * cs[3]
    inv_std = lax.rsqrt(jnp.sum(squares, axis=1, keepdims=True) * (1.0 / width) + norm_eps)
    row = first_row + step * rows + lax.broadcasted_iota(jnp.int32, (rows, 1), 0)
    for j, (centered, cot) in enumerate(zip(cs, (c0, c1, c2, c3))):
        here = pl.ds(pl.multiple_of((own ^ j) * cols, cols), cols)
        left[0, :, here] = (centered * inv_std * gain[:, here] + bias[:, here]).astype(BF)
        low = jnp.where(row < place[1], cot[...], jnp.zeros_like(cot))
        left[1, :, here] = low
        if j == 0:
            sum_grad[...] = jnp.sum(low.astype(F32).reshape(rows // 8, 8, cols), axis=0)
    lane = lax.broadcasted_iota(jnp.int32, (rows, 128), 1)
    stats[...] = jnp.where(lane == 0, mean, inv_std)
    h = left[0]
    g = left[1]
    part = min(512, units)
    for first in range(0, units, part):
        here = pl.ds(first, part)
        up = mm(h, w_in[:, here]) + b_in[:, here]
        g_act = mm(g, w_down[here, :], NT)
        square = up * up
        tanh = jnp.tanh(up * (GELU_A + GELU_A * GELU_B * square))
        half = 0.5 * up
        plus = 1.0 + tanh
        slope = 0.5 * plus + (half * (1.0 - tanh * tanh)) * (GELU_A + 3.0 * GELU_A * GELU_B * square)
        g_up = slope * g_act
        right[0, :, here] = g_up.astype(BF)
        right[1, :, here] = (half * plus).astype(BF)
        sum_up[:, here] = jnp.sum(g_up.reshape(rows // 8, 8, part), axis=0)


def norm_mlp(place, near, far, gain, bias, w_in, b_in, w_down, start_row, first_row, total, before=None):
    rows, cols = far[0].shape
    rows //= 2
    width, units = w_in.shape
    tile = min(256, rows)
    tiles = rows // tile
    offset = first_row // tile
    begin = start_row // tile

    def part(j):
        return [pl.BlockSpec((tile, cols), lambda i: (i + begin, 0))] * 2 + [pl.BlockSpec((tile, cols), lambda i: (i + j * tiles, 0))] * 2

    def rowed(size):
        return pl.BlockSpec((tile, size), lambda i: (i + offset, 0))

    def paired(size):
        return pl.BlockSpec((2, tile, size), lambda i: (0, i + offset, 0))

    def eight(size):
        return pl.BlockSpec((8, size), lambda i: (i + offset, 0))

    def whole(shape):
        return pl.BlockSpec(memory_space=pltpu.VMEM)

    shape = jax.ShapeDtypeStruct
    outs = [pltpu.VMEM((2, total, width), BF), pltpu.VMEM((2, total, units), BF), shape((total, 128), F32),
            shape((total // tile * 8, units), F32), shape((total // tile * 8, cols), F32)]
    before = [] if before is None else [inside(before[0]), inside(before[1]), *before[2:]]
    return pl.pallas_call(
        functools.partial(norm_mlp_kernel, first_row=first_row),
        grid=(tiles,),
        in_specs=[pl.BlockSpec(memory_space=pltpu.SMEM)]
        + part(0) + part(1)
        + [whole((1, width)), whole((1, width)), whole((width, units)), whole((1, units)), whole((units, width))]
        + [pl.BlockSpec(memory_space=pl.ANY)] * len(before),
        out_specs=[paired(width), paired(units), rowed(128), eight(units), eight(cols)],
        out_shape=outs,
        input_output_aliases={14 + k: k for k in range(len(before))},
        compiler_params=pltpu.CompilerParams(vmem_limit_bytes=VMEM_BYTES),
        cost_estimate=cost(0.010 * rows),
        name="norm_mlp",
    )(place, near[0], near[1], *far, near[2], near[3], *far, gain, bias, inside(w_in), b_in, inside(w_down), *before)


def turn(field, cosine, sine):
    lane = lax.broadcasted_iota(jnp.int32, field.shape, 1)
    size = field.shape[1]
    other = jnp.where(lane % 2 == 0, pltpu.roll(field, size - 1, 1), pltpu.roll(field, 1, 1))
    return field * cosine + other * sine


def attend_kernel(
    place, left, w_q, w_k, w_v, w_o, cosine, sine, cos_all, sin_all, attended, g_qkv,
    k_aug, k_t, v_nat, v_t, q_nat, q_aug, d_out, gk_acc, gv_acc, *, tiles, tile, pairs,
):
    step = pl.program_id(0)
    length = place[1]
    share = 128 * pairs

    @pl.when(step < tiles)
    def project():
        h = left[0]
        cos = cosine[...]
        sin = sine[...]
        q_all = mm(h, w_q[...])
        k_all = mm(h, w_k[...])
        v_all = mm(h, w_v[...])
        g_all = mm(left[1], w_o[...], NT)
        start = pl.multiple_of(step * tile, tile)
        here = pl.ds(start, tile)
        lane = lax.broadcasted_iota(jnp.int32, (tile, 128), 1)
        key_row = start + lax.broadcasted_iota(jnp.int32, (tile, 128), 0)
        closed = jnp.where(key_row < length, 0.0, -1e30)
        first = lane < HEAD_DIM
        sub = lax.broadcasted_iota(jnp.int32, (128, tile), 0)
        for p in range(pairs):
            cut = slice(128 * p, 128 * (p + 1))
            q = turn(q_all[:, cut], cos, sin) * HEAD_DIM ** (-0.5)
            k = turn(k_all[:, cut], cos, sin)
            v = v_all[:, cut]
            q_nat[p, here, :] = q.astype(BF)
            v_nat[p, here, :] = v.astype(BF)
            k_aug[2 * p, here, :] = jnp.where(first, k, jnp.where(lane == HEAD_DIM, closed, 0.0)).astype(BF)
            k_aug[2 * p + 1, here, :] = jnp.where(first, jnp.where(lane == 0, closed, 0.0), k).astype(BF)
            q_t = q.T
            q_aug[2 * p, :, here] = jnp.where(sub < HEAD_DIM, q_t, jnp.where(sub == HEAD_DIM, 1.0, 0.0)).astype(BF)
            q_aug[2 * p + 1, :, here] = jnp.where(sub < HEAD_DIM, jnp.where(sub == 0, 1.0, 0.0), q_t).astype(BF)
            k_t[p, :, here] = k.T.astype(BF)
            v_t[p, :, here] = v.T.astype(BF)
            d_out[p, :, here] = g_all[:, cut].T

    @pl.when(step >= tiles)
    def attend():
        p = step - tiles
        lane = lax.broadcasted_iota(jnp.int32, (tile, 128), 1)
        later = lax.broadcasted_iota(jnp.int32, (tile, tile), 0) > lax.broadcasted_iota(jnp.int32, (tile, tile), 1)
        heads = range(2)
        mine = [lane < HEAD_DIM, lane >= HEAD_DIM]
        cuts = [slice(0, HEAD_DIM), slice(HEAD_DIM, 2 * HEAD_DIM)]

        def cut_of(j):
            return pl.ds(pl.multiple_of(j * share + p * 128, 128), 128)

        def score(i):
            n = (i + 1) * tile
            return [mm(k_aug[2 * p + h, :n, :], q_aug[2 * p + h, :, i * tile : n]) for h in heads]

        for i in range(tiles):
            n = (i + 1) * tile
            here = slice(i * tile, n)
            old = slice(0, i * tile)
            scores = ahead if i else score(0)
            weights, inverses = [], []
            for h in heads:
                s = scores[h]
                tail = jnp.where(later, -1e30, s[n - tile :])
                s = tail if i == 0 else jnp.concatenate([s[: n - tile], tail], axis=0)
                e = jnp.exp(s - jnp.max(s, axis=0, keepdims=True))
                inverses.append(1.0 / jnp.sum(e, axis=0, keepdims=True))
                weights.append(e)
            lows = [e.astype(BF) for e in weights]
            outs = [mm(v_t[p, cuts[h], :n], lows[h]) * inverses[h] for h in heads]
            scaled, inner = [], []
            for h in heads:
                d = d_out[p, cuts[h], here]
                inner.append(jnp.sum(d * outs[h], axis=0, keepdims=True) * inverses[h])
                scaled.append(d * inverses[h])
            g_scores = []
            for h in heads:
                zero = jnp.zeros((HEAD_DIM, tile), BF)
                d_t = scaled[h].astype(BF)
                d_t = jnp.concatenate([d_t, zero] if h == 0 else [zero, d_t], axis=0)
                g_scores.append((weights[h] * (mm(v_nat[p, :n, :], d_t) - inner[h])).astype(BF))
            if i + 1 < tiles:
                ahead = score(i + 1)
            attended[here, cut_of(0)] = jnp.concatenate(outs, axis=0).T.astype(BF)
            d_nat = jnp.concatenate(scaled, axis=0).T
            q_here = q_nat[p, here, :]
            g_q = jnp.concatenate([mm(k_t[p, cuts[h], :n], g_scores[h]) for h in heads], axis=0).T * HEAD_DIM ** (-0.5)
            g_qkv[here, cut_of(0)] = turn(g_q, cos_all[here, :], -sin_all[here, :]).astype(BF)
            add_v = sum(mm(lows[h], jnp.where(mine[h], d_nat, 0.0).astype(BF)) for h in heads)
            add_k = sum(mm(g_scores[h], jnp.where(mine[h], q_here, jnp.zeros_like(q_here))) for h in heads)
            if i > 0:
                gv_acc[old] += add_v[: n - tile]
                gk_acc[old] += add_k[: n - tile]
            gv_acc[here] = add_v[n - tile :]
            gk_acc[here] = add_k[n - tile :]
        g_qkv[:, cut_of(1)] = turn(gk_acc[...], cos_all[...], -sin_all[...]).astype(BF)
        g_qkv[:, cut_of(2)] = gv_acc[...].astype(BF)


def attend(place, left, weights):
    _, rows, width = left.shape
    share = width // 4
    pairs = share // 128
    tile = min(256, rows)
    tiles = rows // tile

    def early(i, _):
        return (jnp.minimum(i, tiles - 1), 0)

    def whole(shape):
        return pl.BlockSpec(shape, lambda i, _: (0, 0), pipeline_mode=pl.Buffered(1))

    w_q, w_k, w_v, w_o, _, _, cosine, sine = [inside(value) for value in weights]
    return pl.pallas_call(
        functools.partial(attend_kernel, tiles=tiles, tile=tile, pairs=pairs),
        grid_spec=pltpu.PrefetchScalarGridSpec(
            num_scalar_prefetch=1,
            grid=(tiles + pairs,),
            in_specs=[
                pl.BlockSpec((2, tile, width), lambda i, _: (0, jnp.minimum(i, tiles - 1), 0)),
                whole(w_q.shape), whole(w_k.shape), whole(w_v.shape), whole(w_o.shape),
                pl.BlockSpec((tile, 128), early),
                pl.BlockSpec((tile, 128), early),
                whole((rows, 128)), whole((rows, 128)),
            ],
            out_specs=[whole((rows, share)), whole((rows, 3 * share))],
            scratch_shapes=[
                pltpu.VMEM((2 * pairs, rows, 128), BF),
                pltpu.VMEM((pairs, 128, rows), BF),
                pltpu.VMEM((pairs, rows, 128), BF),
                pltpu.VMEM((pairs, 128, rows), BF),
                pltpu.VMEM((pairs, rows, 128), BF),
                pltpu.VMEM((2 * pairs, 128, rows), BF),
                pltpu.VMEM((pairs, 128, rows), F32),
                pltpu.VMEM((rows, 128), F32),
                pltpu.VMEM((rows, 128), F32),
            ],
        ),
        out_shape=[pltpu.VMEM((rows, share), BF), pltpu.VMEM((rows, 3 * share), BF)],
        compiler_params=pltpu.CompilerParams(vmem_limit_bytes=VMEM_BYTES),
        cost_estimate=cost(0.014 * rows),
        name="attend",
    )(place, inside(left), w_q, w_k, w_v, w_o, cosine, sine, cosine, sine)


def weight_mlp_kernel(place, scale, left_0, left_1, right_0, right_1, keep, send):
    total = (scale[0] * (mm(left_0[0], right_0[0], TN) + mm(left_1[0], right_1[0], TN))).astype(BF)
    half = total.shape[0] // 2
    odd = place[2] == 1
    keep[0] = jnp.where(odd, total[half:], total[:half])
    send[0] = jnp.where(odd, total[:half], total[half:])


def weight_att_kernel(place, scale, left_0, left_1, qkv_0, qkv_1, att_0, att_1, keep, send):
    odd = place[2] == 1
    size = qkv_0.shape[1]
    first = (scale[0] * (mm(left_0[0], qkv_0[...], TN) + mm(left_1[0], qkv_1[...], TN))).astype(BF)
    second = (scale[0] * (mm(left_0[1], att_0[...], TN) + mm(left_1[1], att_1[...], TN))).astype(BF)
    half = first.shape[0] // 2
    keep[0, :, :size] = jnp.where(odd, first[half:], first[:half])
    send[0, :, :size] = jnp.where(odd, first[:half], first[half:])
    keep[0, :, size:] = jnp.where(odd, second[half:], second[:half])
    send[0, :, size:] = jnp.where(odd, second[:half], second[half:])


def weight_hold_kernel(place, scale, left_0, left_1, right_0, right_1, hold, ship):
    total = (scale[0] * (mm(left_0[0], right_0[0], TN) + mm(left_1[0], right_1[0], TN))).astype(BF)
    half = total.shape[0] // 2
    odd = place[2] == 1
    mine = jnp.where(odd, total[half:], total[:half])
    other = jnp.where(odd, total[:half], total[half:])

    @pl.when(pl.program_id(0) < 2)
    def near():
        hold[0, 0] = mine
        hold[0, 1] = other

    @pl.when(pl.program_id(0) >= 2)
    def far():
        ship[0, 0] = mine
        ship[0, 1] = other


def chip_of(slot, place):
    return (2 * (slot & 1) + (slot >> 1)) ^ place[3]


def weight_mlp(place, scale, lefts, rights, kind):
    _, rows, width = lefts[0].shape
    units = rights[0].shape[2]
    size = width // 8
    column = pl.BlockSpec((1, rows, 2 * size), lambda i, where: (kind, 0, chip_of(i, where)))
    whole = pl.BlockSpec((1, rows, units), lambda i, where: (kind, 0, 0), pipeline_mode=pl.Buffered(1))
    if kind == 0:
        kernel = weight_mlp_kernel
        slot = pl.BlockSpec((1, size, units), lambda i, where: (i, 0, 0))
        outs = [slot, slot]
        out = [pltpu.HBM((4, size, units), BF)] * 2
    else:
        kernel = weight_hold_kernel
        outs = [pl.BlockSpec((1, 2, size, units), lambda i, where: (jnp.minimum(i, 1), 0, 0, 0)),
                pl.BlockSpec((1, 2, size, units), lambda i, where: (jnp.maximum(i - 2, 0), 0, 0, 0))]
        out = [pltpu.HBM((2, 2, size, units), BF)] * 2
    return pl.pallas_call(
        kernel,
        grid_spec=pltpu.PrefetchScalarGridSpec(
            num_scalar_prefetch=1, grid=(4,),
            in_specs=[pl.BlockSpec(memory_space=pltpu.SMEM), column, column, whole, whole], out_specs=outs,
        ),
        out_shape=out,
        compiler_params=pltpu.CompilerParams(vmem_limit_bytes=VMEM_BYTES),
        cost_estimate=cost(0.0065 * rows),
        name="weight_mlp",
    )(place, scale, *[inside(value) for value in (*lefts, *rights)])


def weight_att(place, scale, lefts, qkvs, atts):
    _, rows, width = lefts[0].shape
    units = qkvs[0].shape[1] + atts[0].shape[1]
    size = width // 8
    column = pl.BlockSpec((2, rows, 2 * size), lambda i, where: (0, 0, chip_of(i, where)))

    def whole(ref):
        return pl.BlockSpec(ref.shape, lambda i, where: (0, 0), pipeline_mode=pl.Buffered(1))

    slot = pl.BlockSpec((1, size, units), lambda i, where: (i, 0, 0))
    out = pltpu.HBM((4, size, units), BF)
    return pl.pallas_call(
        weight_att_kernel,
        grid_spec=pltpu.PrefetchScalarGridSpec(
            num_scalar_prefetch=1, grid=(4,),
            in_specs=[pl.BlockSpec(memory_space=pltpu.SMEM), column, column] + [whole(r) for r in (*qkvs, *atts)],
            out_specs=[slot, slot],
        ),
        out_shape=[out, out],
        compiler_params=pltpu.CompilerParams(vmem_limit_bytes=VMEM_BYTES),
        cost_estimate=cost(0.007 * rows),
        name="weight_att",
    )(place, scale, *[inside(value) for value in (*lefts, *qkvs, *atts)])


def branch_kernel(place, left, right, att, g_qkv, w_q, w_k, w_v, w_o, w_in, w_down, gain, bias,
                  keep, near, far_b, far_g, sums, column_sums):
    own = place[0]
    rows, share = att.shape
    total = mm(right[1], w_down[...]) + mm(att[...], w_o[...])
    g_total = mm(right[0], w_in[...], NT)
    for j, w in enumerate((w_q, w_k, w_v)):
        g_total += mm(g_qkv[:, j * share : (j + 1) * share], w[...], NT)
    odd = (own & 1) == 1
    up = (own >> 1) == 1
    for kind, (whole, far) in enumerate(((total, far_b), (g_total, far_g))):
        cuts = [whole[:, j * share : (j + 1) * share].astype(BF) for j in range(4)]
        low = [jnp.where(odd, cuts[2 * y + 1], cuts[2 * y]) for y in range(2)]
        high = [jnp.where(odd, cuts[2 * y], cuts[2 * y + 1]) for y in range(2)]
        keep[0, kind] = jnp.where(up, low[1], low[0])
        keep[1, kind] = jnp.where(up, low[0], low[1])
        near[kind] = jnp.where(up, high[1], high[0])
        far[...] = jnp.where(up, high[0], high[1])
    turned = g_total * (left[0].astype(F32) - bias[...])
    mean_part = jnp.sum(g_total * gain[...], axis=1, keepdims=True)
    inner_part = jnp.sum(turned, axis=1, keepdims=True)
    lane = lax.broadcasted_iota(jnp.int32, (rows, 128), 1)
    sums[...] = jnp.where(lane == 0, mean_part, inner_part).T[:8, :]

    @pl.when(pl.program_id(0) == 0)
    def clear():
        column_sums[...] = jnp.zeros_like(column_sums)

    column_sums[0:1, :] += jnp.sum(g_total, axis=0, keepdims=True)
    column_sums[1:2, :] += jnp.sum(turned, axis=0, keepdims=True)


def branch_parts(place, left, right, att, g_qkv, weights, gain, bias, first_row, rows):
    _, _, width = left.shape
    units = right.shape[2]
    share = att.shape[1]
    tile = min(256, rows)
    tiles = rows // tile
    offset = first_row // tile

    def paired(k, size):
        return pl.BlockSpec((k, tile, size), lambda i, _: (0, i + offset, 0))

    def rowed(size):
        return pl.BlockSpec((tile, size), lambda i, _: (i + offset, 0))

    def whole(shape):
        return pl.BlockSpec(shape, lambda i, _: (0, 0), pipeline_mode=pl.Buffered(1))

    weights = [inside(value) for value in weights[:6]]
    shape = jax.ShapeDtypeStruct
    slots = pl.BlockSpec((2, 2, tile, share), lambda i, _: (0, 0, i, 0))
    sent = pl.BlockSpec((2, tile, share), lambda i, _: (0, i, 0))
    rowed_out = pl.BlockSpec((tile, share), lambda i, _: (i, 0))
    return pl.pallas_call(
        branch_kernel,
        grid_spec=pltpu.PrefetchScalarGridSpec(
            num_scalar_prefetch=1,
            grid=(tiles,),
            in_specs=[
                paired(1, width), paired(2, units), rowed(share), rowed(3 * share),
                *[whole(value.shape) for value in weights],
                whole((1, width)), whole((1, width)),
            ],
            out_specs=[slots, sent, rowed_out, rowed_out, pl.BlockSpec((8, tile), lambda i, _: (0, i)), pl.BlockSpec((8, width), lambda i, _: (0, 0))],
        ),
        out_shape=[pltpu.HBM((2, 2, rows, share), BF)] + [pltpu.HBM((2, rows, share), BF)] + [pltpu.HBM((rows, share), BF)] * 2 + [shape((8, rows), F32),
                   shape((8, width), F32)],
        compiler_params=pltpu.CompilerParams(vmem_limit_bytes=VMEM_BYTES),
        cost_estimate=cost(0.010 * rows),
        name="branch_parts",
    )(place, inside(left), inside(right), inside(att), inside(g_qkv), *weights, gain, bias)


def combine_kernel(count, keep_in, x_in, hold, z_down, kept, core_b, core_g, z_in, low_in, zz_down, low_down, chip):
    size, units = keep_in.shape[1:]
    for k in range(2):
        z_in[k * size : (k + 1) * size] = keep_in[2 + k] + x_in[2 + k]
        low_in[k] = keep_in[k] + x_in[k]
        zz_down[k] = hold[1, k] + z_down[1, k]
        low_down[k] = hold[0, k] + z_down[0, k]
    rows = z_in.shape[0] - 2 * size
    row = lax.broadcasted_iota(jnp.int32, (rows, units), 0)
    value = jnp.full((rows, units), count[0], F32)
    high = value.astype(BF).astype(F32)
    z_in[2 * size :] = jnp.where(row == 0, high, jnp.where(row == 1, value - high, 0.0)).astype(BF)
    chip[0] = kept[1, 0] + core_b[...]
    chip[1] = kept[1, 1] + core_g[...]


def combine(count, keep_in, x_in, hold, z_down, kept, core):
    _, size, units = keep_in.shape
    _, _, rows, cols = kept.shape
    inner = pl.BlockSpec(memory_space=pltpu.VMEM)
    shapes = [(2 * size + 16, units), (2, size, units), (2, size, units), (2, size, units), (2, rows, cols)]
    return pl.pallas_call(
        combine_kernel,
        in_specs=[pl.BlockSpec(memory_space=pltpu.SMEM)] + [inner] * 7,
        out_specs=[inner] * 5,
        out_shape=[pltpu.HBM(shape, BF) for shape in shapes],
        compiler_params=pltpu.CompilerParams(vmem_limit_bytes=VMEM_BYTES),
        cost_estimate=cost(3),
        name="combine",
    )(count, *[outside(value) for value in (keep_in, x_in, hold, z_down, kept, *core)])


def final_kernel(place, scale, keep, near, far, x_ref, cot, stats, sums, gain, bias_down, *refs, first_row):
    mixed, g_x = refs[-2:]
    step = pl.program_id(0)
    rows, cols = x_ref.shape
    width = 4 * cols
    x = x_ref[...].astype(F32)
    branch = keep[0, 0].astype(F32) + near[0].astype(F32) + far[0].astype(F32)
    mixed[...] = (x + (branch + bias_down[...])).astype(BF)
    g = scale[0] * (keep[0, 1].astype(F32) + near[1].astype(F32) + far[1].astype(F32))
    inv_std = stats[:, 1:2]
    x_hat = (x - stats[:, 0:1]) * inv_std
    totals = (scale[0] / width) * jnp.concatenate([sums[...], jnp.zeros((126, rows), F32)], axis=0).T
    row = first_row + step * rows + lax.broadcasted_iota(jnp.int32, (rows, 1), 0)
    weight = jnp.where(row < place[1], scale[0], 0.0)
    g_out = weight * cot[...].astype(F32)
    g_x[...] = g_out + inv_std * (g * gain[...] - totals[:, 0:1] - x_hat * totals[:, 1:2])


def finish_rows(place, scale, keep, near, far, x, cot, stats, sums, gain, bias_down, sequence, first_row, before=None):
    _, rows, cols = far.shape
    tile = min(512, rows)
    tiles = rows // tile
    pad_len = stats.shape[0]
    begin = (sequence * pad_len + first_row) // tile
    inner = first_row // tile
    part = pl.BlockSpec((tile, cols), lambda i: (i + begin, 0))
    cored = pl.BlockSpec((1, tile, cols), lambda i: (0, i, 0))
    kept = pl.BlockSpec((1, 2, tile, cols), lambda i: (0, 0, i, 0))
    both = pl.BlockSpec((2, tile, cols), lambda i: (0, i, 0))
    flat = pl.BlockSpec((1, cols), lambda i: (0, 0))
    scalar = pl.BlockSpec(memory_space=pltpu.SMEM)
    shape = jax.ShapeDtypeStruct
    before = [] if before is None else list(before)
    return pl.pallas_call(
        functools.partial(final_kernel, first_row=first_row),
        grid=(tiles,),
        in_specs=[scalar, scalar, kept, both, both, part, part,
                  pl.BlockSpec((tile, 128), lambda i: (i + inner, 0)), pl.BlockSpec((2, tile), lambda i: (0, i + begin)), flat, flat]
        + [pl.BlockSpec(memory_space=pl.ANY)] * len(before),
        out_specs=[part, part],
        out_shape=[shape(x.shape, BF), shape(x.shape, F32)],
        input_output_aliases={11 + k: k for k in range(len(before))},
        compiler_params=pltpu.CompilerParams(vmem_limit_bytes=VMEM_BYTES),
        cost_estimate=cost(0.003 * rows),
        name="finish_rows",
    )(place, scale, *[outside(value) for value in (keep, near, far, x, cot, stats)], sums, gain, bias_down, *before)


def final_weight_kernel(factor, low_in, far_in, low_down, far_down, low_a, far_a, g_in, g_down, g_qkv, g_out):
    scale = factor[0]
    _, size, cols = g_qkv.shape
    g_in[...] = scale * (low_in[...].astype(F32) + far_in[:size].astype(F32))
    g_down[...] = (scale * (low_down[...].astype(F32) + far_down[...].astype(F32))).T
    for j in range(3):
        cut = slice(j * cols, (j + 1) * cols)
        g_qkv[j] = scale * (low_a[:, cut].astype(F32) + far_a[:size, cut].astype(F32))
    cut = slice(3 * cols, 4 * cols)
    g_out[...] = (scale * (low_a[:, cut].astype(F32) + far_a[:size, cut].astype(F32))).T


def finish_weights(factor, low_in, far_in, low_down, far_down, low_a, far_a):
    size, units = low_in.shape
    cols = low_a.shape[1] // 4
    shape = jax.ShapeDtypeStruct
    return pl.pallas_call(
        final_weight_kernel,
        in_specs=[pl.BlockSpec(memory_space=pltpu.SMEM)] + [pl.BlockSpec(memory_space=pltpu.VMEM)] * 6,
        out_specs=[pl.BlockSpec(memory_space=pltpu.VMEM)] * 4,
        out_shape=[shape((size, units), F32), shape((units, size), F32), shape((3, size, cols), F32), shape((cols, size), F32)],
        compiler_params=pltpu.CompilerParams(vmem_limit_bytes=VMEM_BYTES),
        cost_estimate=cost(3),
        name="finish_weights",
    )(factor, low_in, far_in, low_down, far_down, low_a, far_a)


def swap(value, axis, bit):
    size = lax.axis_size(axis)
    return lax.ppermute(value, axis, [(i, i ^ bit) for i in range(size)])


def sum_small(value, axis):
    bit = 1
    while bit < lax.axis_size(axis):
        value = value + swap(value, axis, bit)
        bit *= 2
    return value


def add_core(kept, core):
    return kept[1] + jnp.stack(core)


def pack(values, units):
    padded = jnp.concatenate([values, jnp.zeros((-values.shape[0] % units,), F32)]).reshape(-1, units)
    high = lax.reduce_precision(padded, 8, 7)
    rows = jnp.concatenate([high, padded - high], axis=0).astype(BF)
    return jnp.concatenate([rows, jnp.zeros((-rows.shape[0] % 16, units), BF)], axis=0)


def unpack(rows, count):
    part = -(-count // rows.shape[1])
    high, low = rows[:part].astype(F32), rows[part : 2 * part].astype(F32)
    return (high + low).reshape(-1)[:count]


def after(value, *others):
    return lax.optimization_barrier((value, *others))[0]


def on_device_fast(inputs, cotangent, lengths, ln_gain, ln_bias, w_qkv, w_out, w_in, b_in, w_down, b_down):
    groups = lax.axis_size("wide")
    column = lax.axis_index("narrow")
    place_wide = lax.axis_index("wide")
    rows_all, cols = inputs.shape
    pad_len = rows_all // 2
    width = w_qkv.shape[0]
    units = w_in.shape[1]
    place = jnp.stack([column, lengths[0], place_wide & 1, place_wide >> 1]).astype(jnp.int32)
    gain = ln_gain.reshape(1, width)
    bias = ln_bias.reshape(1, width)
    b_up = b_in.reshape(1, units)
    half = pad_len // 2
    cuts = ((0, half), (half, pad_len), (pad_len, rows_all))
    own_gain = lax.dynamic_slice_in_dim(ln_gain, column * cols, cols, 0).reshape(1, cols)
    b_row = b_down.reshape(1, cols)

    across = [swap(jnp.concatenate([inputs[low:high], cotangent[low:high]], axis=0), "narrow", 2) for low, high in cuts]
    near = (inputs, swap(inputs, "narrow", 1), cotangent, swap(cotangent, "narrow", 1))
    count = (2.0 * jnp.sum(lengths.astype(F32))).reshape(1)
    count_x = count + swap(count, "wide", 1)
    weights = load_weights(place, w_qkv, w_out, w_in, w_down, *turn_tables(pad_len))
    up_in, up_down = weights[4:6]

    def far(k, *earlier):
        rows = after(across[k], *earlier)
        return rows, swap(rows, "narrow", 1)

    def branch(place, mlp, att, first_row, rows):
        kept, near, far_b, far_g, sums, columns = branch_parts(
            place, mlp[0], mlp[1], *att, weights, gain, bias, first_row, rows)
        return kept, near, (far_b, far_g), sums, columns

    first = norm_mlp(place, near, far(0, weights[0], count_x), gain, bias, up_in, b_up, up_down, 0, 0, pad_len)
    place = after(place, first[3])
    mlp_0 = norm_mlp(place, near, far(1, first[3]), gain, bias, up_in, b_up, up_down, half, half, pad_len, first)
    place = after(place, mlp_0[3])
    att_0 = attend(place, mlp_0[0], weights)
    place = after(place, att_0[0])
    mlp_1 = norm_mlp(place, near, far(2, att_0[0]), gain, bias, up_in, b_up, up_down, pad_len, 0, pad_len)
    place = after(place, mlp_1[3])
    lefts = (mlp_0[0], mlp_1[0])
    rights = (mlp_0[1], mlp_1[1])
    keep_in, send_in = weight_mlp(place, count, lefts, rights, 0)
    place = after(place, keep_in)
    x_in = swap(send_in, "wide", 1)
    hold_down, ship_down = weight_mlp(place, count, lefts, rights, 1)
    place = after(place, hold_down)
    z_down = swap(ship_down, "wide", 2)
    kept_0, near_0, sent_0, sums_0, columns_0 = branch(place, mlp_0, att_0, 0, pad_len)
    core_0 = [swap(part, "narrow", 1) for part in sent_0]
    place = after(place, sums_0)
    att_1 = attend(place, mlp_1[0], weights)
    size = keep_in.shape[1]
    x_in, z_down, count_x, *core_0 = lax.optimization_barrier((x_in, z_down, count_x, *core_0, att_1[0]))[:5]
    z_in, low_in, zz_down, low_down, chip_0 = combine(count_x, keep_in, x_in, hold_down, z_down, kept_0, core_0)
    z_in = swap(z_in, "wide", 2)
    zz_down = swap(zz_down, "wide", 4)
    y_0 = swap(chip_0, "narrow", 2)
    near_0 = swap(after(near_0, chip_0), "narrow", 1)
    place = after(place, low_in, low_down, chip_0, att_1[0])
    keep_a, send_a = weight_att(place, count, lefts, (att_0[1], att_1[1]), (att_0[0], att_1[0]))
    x_a = swap(send_a, "wide", 1)
    place = after(place, keep_a, near_0)
    kept_1, near_1, sent_1, sums_1, columns_1 = branch(place, mlp_1, att_1, 0, pad_len)
    core_1 = [swap(part, "narrow", 1) for part in sent_1]
    z_in, zz_down, y_0, sums_0, columns_0 = lax.optimization_barrier((z_in, zz_down, y_0, sums_0, columns_0, sums_1))[:5]
    count_row = count_x + unpack(z_in[2 * size :], units)[:128]
    zz_in = swap(jnp.concatenate([low_in[1] + z_in[size : 2 * size], pack(jnp.broadcast_to(count_row[:1], (units,)), units)], axis=0), "wide", 4)
    low_in = low_in[0] + z_in[:size]
    x_d = swap(low_down[1] + zz_down[1], "wide", 1)
    low_down = low_down[0] + zz_down[0]
    sums = jnp.concatenate([sums_0[:2], sums_1[:2], columns_0[:2] + columns_1[:2]], axis=1)
    sums = after(sums, y_0)
    sums = sums + swap(sums, "narrow", 1)
    core_1 = [after(part, sums, low_down, low_in) for part in core_1]
    chip_1 = add_core(kept_1, core_1)
    y_1 = swap(chip_1, "narrow", 2)
    far_sums = swap(after(sums, chip_1), "narrow", 2)
    near_1 = swap(after(near_1, chip_1), "narrow", 1)
    x_a = after(x_a, chip_1)
    z_a = swap(keep_a[2:] + x_a[2:], "wide", 2)
    low_a = keep_a[:2] + x_a[:2]
    z_a = after(z_a, low_a)
    zz_a = swap(low_a[1] + z_a[1], "wide", 4)
    low_a = low_a[0] + z_a[0]
    y_1, far_sums, near_1, zz_in = lax.optimization_barrier((y_1, far_sums, near_1, zz_in, low_a))[:4]
    count_row = count_row + unpack(zz_in[size:], units)[:128]
    per_count = groups / count_row[:1]
    scale = count * per_count
    sums = sums + far_sums
    columns = lax.dynamic_slice_in_dim(sums[:, rows_all:], column * cols, cols, 1)
    sum_up, sum_down = [after(mlp_0[k], y_1) + mlp_1[k] for k in (3, 4)]
    small = count * jnp.concatenate([columns[1] / own_gain[0], columns[0], jnp.sum(sum_up, axis=0), jnp.sum(sum_down, axis=0)])
    small = small + swap(small, "wide", 1)
    ends = finish_rows(place, scale, kept_0, near_0, y_0, inputs, cotangent, mlp_0[2], sums, own_gain, b_row, 0, 0)
    small = small + swap(small, "wide", 2)
    ends = finish_rows(place, scale, kept_1, near_1, y_1, inputs, cotangent, mlp_1[2], sums, own_gain, b_row, 1, 0, ends)
    small = per_count * (small + swap(small, "wide", 4))
    zz_a, x_d = lax.optimization_barrier((zz_a, x_d, ends[0]))[:2]
    g_in, g_down, g_qkv, g_out = finish_weights(per_count, low_in, zz_in, low_down, x_d, low_a, zz_a)
    return (
        ends[0],
        ends[1],
        small[:cols],
        small[cols : 2 * cols],
        jnp.transpose(g_qkv, (1, 0, 2)),
        g_out,
        g_in,
        small[2 * cols : 2 * cols + units],
        g_down,
        small[2 * cols + units :],
    )


def turn_tables(length):
    position = np.arange(length, dtype=np.float32)[:, None]
    frequency = (10000.0 ** (-2.0 * np.arange(ROT // 2, dtype=np.float32) / ROT)).astype(np.float32)
    angles = (position * frequency[None, :]).astype(np.float32)
    cosine = np.ones((length, HEAD_DIM), np.float32)
    sine = np.zeros((length, HEAD_DIM), np.float32)
    cosine[:, :ROT] = np.repeat(np.cos(angles), 2, axis=1)
    sine[:, 0:ROT:2] = -np.sin(angles)
    sine[:, 1:ROT:2] = np.sin(angles)
    return jnp.asarray(np.tile(cosine, (1, 2))), jnp.asarray(np.tile(sine, (1, 2)))


def solution(mesh):
    placed = (
        P("wide", "narrow"),
        P("wide", "narrow"),
        P("wide"),
        P(),
        P(),
        P(),
        P(),
        P(None, "narrow"),
        P("narrow"),
        P("narrow", None),
        P("narrow"),
    )
    paired = mesh.shape["narrow"] == 4 and mesh.shape["wide"] == 8
    return jax.shard_map(
        on_device_fast if paired else on_device,
        mesh=mesh,
        in_specs=placed,
        out_specs=(
            P("wide", "narrow"),
            P("wide", "narrow"),
            P("narrow"),
            P("narrow"),
            P("wide", None, "narrow"),
            P("narrow", "wide"),
            P("wide", "narrow"),
            P("narrow"),
            P("narrow", "wide"),
            P("narrow"),
        ),
        check_vma=False,
    )
```

profile of v0, /device:TPU:0, one launch (start us, length us, event | category | flops | bytes accessed | tf_op | source)
XLA Modules:
  0.0 195.7 jit_solution(6570386414817235695)
XLA Ops:
  0.7 1.2 fusion.8
  1.9 1.1 fusion.9
  3.0 0.8 pad_maximum_fusion.1
  3.8 3.0 %collective-permute-start.1 = (bf16[1024,256]{1,0:T(8,128)(2,1)}, bf16[1024,256]{1,0:T(8,128)(2,1)}, u32[]{:S(2)}, u32[]{:S(2)}) collective-permute-start(bf16[1024,256]{1,0:T(8,128)(2,1)} %pad_maximum_fusion.1), channel_id=1, source_target_pairs={{0,2},{1,3},{2,0},{3,1},{4,6},{5,7},{6,4},{7,5},{8,10},{9,11},{10,... | collective-permute-start | bytes 1572872 | tf_op jit(solution)/shard_map/ppermute | solution.py:847
  7.9 2.9 %collective-permute-start.2 = (f32[1]{0:T(128)}, f32[1]{0:T(128)}, u32[]{:S(2)}, u32[]{:S(2)}) collective-permute-start(f32[1]{0:T(128)} %mul_shard_map.6.scale), channel_id=1, source_target_pairs={{0,4},{4,0},{8,12},{12,8},{16,20},{20,16},{24,28},{28,24},{1,5},{5... | collective-permute-start | bytes 20 | tf_op jit(solution)/shard_map/ppermute | solution.py:847
  10.8 0.8 pad_maximum_fusion.2
  12.1 0.8 slice.140
  12.9 0.8 slice.141
  13.8 3.7 %load_weights.1 = (bf16[1024,256]{1,0:T(8,128)(2,1)S(1)}, bf16[1024,256]{1,0:T(8,128)(2,1)S(1)}, bf16[1024,256]{1,0:T(8,128)(2,1)S(1)}, bf16[256,1024]{1,0:T(8,1...) custom-call(s32[4]{0:T(128)S(1)} %pad_add_fusion.place, ...), custom_call_target="tpu_custom_call" | custom-call | flops 300000000 | bytes 1000000 | tf_op jit(solution)/shard_map/load_weights/pallas_call | solution.py:320
  18.2 1.6 collective-permute-done.1.x2.c2
  19.9 2.1 %collective-permute-start.7 = (bf16[2048,256]{1,0:T(8,128)(2,1)S(1)}, bf16[2048,256]{1,0:T(8,128)(2,1)S(1)}, u32[]{:S(2)}, u32[]{:S(2)}) collective-permute-start(bf16[2048,256]{1,0:T(8,128)(2,1)S(1)} %pad_maximum_fusion), channel_id=1, source_target_pairs={{0,2},{1,3},{2,0},{3,1},{4,6},{5,7},{6,4},{7,5},{8,10},{9,11},{10,... | collective-permute-start | bytes 3145736 | tf_op jit(solution)/shard_map/ppermute | solution.py:847
  22.1 5.9 %norm_mlp.3 = (bf16[2,1024,1024]{2,1,0:T(8,128)(2,1)S(1)}, bf16[2,1024,1024]{2,1,0:T(8,128)(2,1)S(1)}, f32[1024,128]{1,0:T(8,128)S(1)}, f32[32,1024]{1,0:T(8,128)S(1)}, f32[32,256]{1,0:T(8,128)S(1)}) custom-call(s32[4]{0:T(128)S(1)} %pad_add_fusion.place, bf16[2048,256]{1,0:T(8,128)(2,1)S(1)} %copy-done, bf16[2048,256]{1,0:T(8,128)(2,1)S(1)} %collective-permute-done.x1, ...), custom_call_target="tpu_custom_call" | custom-call | flops 512000000 | bytes 1000000 | tf_op jit(solution)/shard_map/norm_mlp/pallas_call | solution.py:399
  28.0 3.0 %collective-permute-done.5.x2.c2 = bf16[1024,256]{1,0:T(8,128)(2,1)} collective-permute-done((bf16[1024,256]{1,0:T(8,128)(2,1)}, bf16[1024,256]{1,0:T(8,128)(2,1)}, u32[]{:S(2)}, u32[]{:S(2)}) %collective-permute-start.5) | collective-permute-done | bytes 524320 | tf_op jit(solution)/shard_map/ppermute | solution.py:847
  31.1 2.1 %collective-permute-done.6.x3.c3 = bf16[1024,256]{1,0:T(8,128)(2,1)S(1)} collective-permute-done((bf16[1024,256]{1,0:T(8,128)(2,1)}, bf16[1024,256]{1,0:T(8,128)(2,1)S(1)}, u32[]{:S(2)}, u32[]{:S(2)}) %collective-permute-start.6) | collective-permute-done | bytes 524320 | tf_op jit(solution)/shard_map/ppermute | solution.py:847
  33.2 5.5 %norm_mlp.4 = (bf16[2,1024,1024]{2,1,0:T(8,128)(2,1)S(1)}, bf16[2,1024,1024]{2,1,0:T(8,128)(2,1)S(1)}, f32[1024,128]{1,0:T(8,128)S(1)}, f32[32,1024]{1,0:T(8,128)S(1)}, f32[32,256]{1,0:T(8,128)S(1)}) custom-call(s32[4]{0:T(128)S(1)} %pad_add_fusion.place, ...), custom_call_target="tpu_custom_call", output_to_operand_aliasing={{0}: (14, {}), {1}: (15, {}), {2}: (16, {}), {3}: (17, {}),... | custom-call | flops 512000000 | bytes 1000000 | tf_op jit(solution)/shard_map/norm_mlp/pallas_call | solution.py:399
  38.7 0.8 copy-done.5
  39.5 13.9 %attend.2 = (bf16[1024,256]{1,0:T(8,128)(2,1)S(1)}, bf16[1024,768]{1,0:T(8,128)(2,1)S(1)}) custom-call(s32[4]{0:T(128)S(1)} %pad_add_fusion.place, bf16[2,1024,1024]{2,1,0:T(8,128)(2,1)S(1)} %get-tuple-element.119.left.left_0, bf16[1024,256]{1,0:T(8,128)(2,1)S(1)} %get-tuple-element.106.w_q, bf16[1024,256]{1,0:T(8,128)(2,1)S(1)} %get-tuple-element.120.w_k, ...), custom_call_target="tpu_custom_call" | custom-call | flops 1433600000 | bytes 1000000 | tf_op jit(solution)/shard_map/attend/pallas_call | solution.py:536
  53.6 2.5 %collective-permute-done.8.x3.c3 = bf16[2048,256]{1,0:T(8,128)(2,1)S(1)} collective-permute-done((bf16[2048,256]{1,0:T(8,128)(2,1)S(1)}, bf16[2048,256]{1,0:T(8,128)(2,1)S(1)}, u32[]{:S(2)}, u32[]{:S(2)}) %collective-permute-start.8) | collective-permute-done | bytes 1048608 | tf_op jit(solution)/shard_map/ppermute | solution.py:847
  56.2 10.0 %norm_mlp.5 = (bf16[2,1024,1024]{2,1,0:T(8,128)(2,1)S(1)}, bf16[2,1024,1024]{2,1,0:T(8,128)(2,1)S(1)}, f32[1024,128]{1,0:T(8,128)S(1)}, f32[32,1024]{1,0:T(8,128)S(1)}, f32[32,256]{1,0:T(8,128)S(1)}) custom-call(s32[4]{0:T(128)S(1)} %pad_add_fusion.place, bf16[2048,256]{1,0:T(8,128)(2,1)S(1)} %copy-done, bf16[2048,256]{1,0:T(8,128)(2,1)S(1)} %copy-done.4, ...), custom_call_target="tpu_custom_call" | custom-call | flops 1024000000 | bytes 1000000 | tf_op jit(solution)/shard_map/norm_mlp/pallas_call | solution.py:399
  66.2 7.3 %weight_mlp.2 = (bf16[4,128,1024]{2,1,0:T(8,128)(2,1)}, bf16[4,128,1024]{2,1,0:T(8,128)(2,1)}) custom-call(s32[4]{0:T(128)S(1)} %pad_add_fusion.place, f32[1]{0:T(128)} %mul_shard_map.6.scale, bf16[2,1024,1024]{2,1,0:T(8,128)(2,1)S(1)} %get-tuple-element.119.left.left_0, bf16[2,1024,1024]{2,1,0:T(8,128)(2,1)S(1)} %get-tuple-element.130.left_1.left, ...), custom_call_target="tpu_custom_call" | custom-call | flops 665600000 | bytes 1000000 | tf_op jit(solution)/shard_map/weight_mlp/pallas_call | solution.py:626
  73.6 7.6 %weight_mlp.3 = (bf16[2,2,128,1024]{3,2,1,0:T(8,128)(2,1)}, bf16[2,2,128,1024]{3,2,1,0:T(8,128)(2,1)}) custom-call(s32[4]{0:T(128)S(1)} %pad_add_fusion.place, f32[1]{0:T(128)} %mul_shard_map.6.scale, bf16[2,1024,1024]{2,1,0:T(8,128)(2,1)S(1)} %get-tuple-element.119.left.left_0, bf16[2,1024,1024]{2,1,0:T(8,128)(2,1)S(1)} %get-tuple-element.130.left_1.left, ...), custom_call_target="tpu_custom_call" | custom-call | flops 665600000 | bytes 1000000 | tf_op jit(solution)/shard_map/weight_mlp/pallas_call | solution.py:626
  81.1 2.1 %collective-permute-start.10 = (bf16[2,2,128,1024]{3,2,1,0:T(8,128)(2,1)}, bf16[2,2,128,1024]{3,2,1,0:T(8,128)(2,1)S(1)}, u32[]{:S(2)}, u32[]{:S(2)}) collective-permute-start(bf16[2,2,128,1024]{3,2,1,0:T(8,128)(2,1)} %get-tuple-element.141), channel_id=1, source_target_pairs={{0,8},{4,12},{8,0},{12,4},{16,24},{20,28},{24,16},{28,20},{1,9},{5... | collective-permute-start | bytes 3145736 | tf_op jit(solution)/shard_map/ppermute | solution.py:847
  83.2 1.5 collective-permute-start.9
  84.7 10.6 %branch_parts.2 = (bf16[2,2,1024,256]{3,2,1,0:T(8,128)(2,1)}, bf16[2,1024,256]{2,1,0:T(8,128)(2,1)}, bf16[1024,256]{1,0:T(8,128)(2,1)}, bf16[1024,256]{1,0:T(8,1...) custom-call(s32[4]{0:T(128)S(1)} %pad_add_fusion.place, ...), custom_call_target="tpu_custom_call" | custom-call | flops 1024000000 | bytes 1000000 | tf_op jit(solution)/shard_map/branch_parts/pallas_call | solution.py:718
  95.8 13.9 %attend.3 = (bf16[1024,256]{1,0:T(8,128)(2,1)S(1)}, bf16[1024,768]{1,0:T(8,128)(2,1)S(1)}) custom-call(s32[4]{0:T(128)S(1)} %pad_add_fusion.place, bf16[2,1024,1024]{2,1,0:T(8,128)(2,1)S(1)} %get-tuple-element.130.left_1.left, bf16[1024,256]{1,0:T(8,128)(2,1)S(1)} %get-tuple-element.106.w_q, bf16[1024,256]{1,0:T(8,128)(2,1)S(1)} %get-tuple-element.120.w_k, ...), custom_call_target="tpu_custom_call" | custom-call | flops 1433600000 | bytes 1000000 | tf_op jit(solution)/shard_map/attend/pallas_call | solution.py:536
  111.4 5.0 %combine.1 = (bf16[272,1024]{1,0:T(8,128)(2,1)}, bf16[2,128,1024]{2,1,0:T(8,128)(2,1)}, bf16[2,128,1024]{2,1,0:T(8,128)(2,1)}, bf16[2,128,1024]{2,1,0:T(8,128)(2,1)}, bf16[2,1024,256]{2,1,0:T(8,128)(2,1)}) custom-call(f32[1]{0:T(128)} %add.91.count, bf16[4,128,1024]{2,1,0:T(8,128)(2,1)} %get-tuple-element.133.keep_in, bf16[4,128,1024]{2,1,0:T(8,128)(2,1)} %copy-done.21, ...), custom_call_target="tpu_custom_call" | custom-call | flops 300000000 | bytes 1000000 | tf_op jit(solution)/shard_map/combine/pallas_call | solution.py:759
  116.4 1.5 collective-permute-start.16
  118.4 2.6 %collective-permute-start.15 = (bf16[2,128,1024]{2,1,0:T(8,128)(2,1)}, bf16[2,128,1024]{2,1,0:T(8,128)(2,1)S(1)}, u32[]{:S(2)}, u32[]{:S(2)}) collective-permute-start(bf16[2,128,1024]{2,1,0:T(8,128)(2,1)} %get-tuple-element.161), channel_id=1, source_target_pairs={{0,16},{4,20},{8,24},{12,28},{16,0},{20,4},{24,8},{28,12},{1,17},{... | collective-permute-start | bytes 1572872 | tf_op jit(solution)/shard_map/ppermute | solution.py:847
  121.1 7.8 %weight_att.1 = (bf16[4,128,1024]{2,1,0:T(8,128)(2,1)}, bf16[4,128,1024]{2,1,0:T(8,128)(2,1)}) custom-call(s32[4]{0:T(128)S(1)} %pad_add_fusion.place, f32[1]{0:T(128)} %mul_shard_map.6.scale, bf16[2,1024,1024]{2,1,0:T(8,128)(2,1)S(1)} %get-tuple-element.119.left.left_0, bf16[2,1024,1024]{2,1,0:T(8,128)(2,1)S(1)} %get-tuple-element.130.left_1.left, ...), custom_call_target="tpu_custom_call" | custom-call | flops 716800000 | bytes 1000000 | tf_op jit(solution)/shard_map/weight_att/pallas_call | solution.py:650
  129.4 1.0 copy-done.18
  130.4 10.8 %branch_parts.3 = (bf16[2,2,1024,256]{3,2,1,0:T(8,128)(2,1)}, bf16[2,1024,256]{2,1,0:T(8,128)(2,1)}, bf16[1024,256]{1,0:T(8,128)(2,1)}, bf16[1024,256]{1,0:T(8,1...) custom-call(s32[4]{0:T(128)S(1)} %pad_add_fusion.place, ...), custom_call_target="tpu_custom_call" | custom-call | flops 1024000000 | bytes 1000000 | tf_op jit(solution)/shard_map/branch_parts/pallas_call | solution.py:718
  141.2 1.0 collective-permute-done.15
  142.2 1.9 collective-permute-done.14
  144.9 0.8 add_bitcast_fusion
  145.7 0.8 collective-permute-done.18
  147.1 1.1 maximum_add_fusion
  148.7 5.0 %collective-permute-done.24 = bf16[4,128,1024]{2,1,0:T(8,128)(2,1)S(1)} collective-permute-done((bf16[4,128,1024]{2,1,0:T(8,128)(2,1)}, bf16[4,128,1024]{2,1,0:T(8,128)(2,1)S(1)}, u32[]{:S(2)}, u32[]{:S(2)}) %collective-permute-start.24) | collective-permute-done | bytes 1048608 | tf_op jit(solution)/shard_map/ppermute | solution.py:847
  153.8 0.9 slice_add_fusion
  154.7 1.6 collective-permute-start.25
  158.2 0.9 maximum_maximum_fusion
  160.0 15.3 %collective-permute-done.25 = bf16[2,128,1024]{2,1,0:T(8,128)(2,1)S(1)} collective-permute-done((bf16[2,128,1024]{2,1,0:T(8,128)(2,1)}, bf16[2,128,1024]{2,1,0:T(8,128)(2,1)S(1)}, u32[]{:S(2)}, u32[]{:S(2)}) %collective-permute-start.25) | collective-permute-done | bytes 524320 | tf_op jit(solution)/shard_map/ppermute | solution.py:847
  175.9 2.1 %collective-permute-start.29 = (bf16[128,1024]{1,0:T(8,128)(2,1)S(1)}, bf16[128,1024]{1,0:T(8,128)(2,1)S(1)}, u32[]{:S(2)}, u32[]{:S(2)}) collective-permute-start(bf16[128,1024]{1,0:T(8,128)(2,1)S(1)} %get-tuple-element.210), channel_id=1, source_target_pairs={{0,16},{4,20},{8,24},{12,28},{16,0},{20,4},{24,8},{28,12},{1,17},{... | collective-permute-start | bytes 786440 | tf_op jit(solution)/shard_map/ppermute | solution.py:847
  178.0 1.1 collective-permute-done.21
  180.1 3.7 %finish_rows.2 = (bf16[2048,256]{1,0:T(8,128)(2,1)}, f32[2048,256]{1,0:T(8,128)}) custom-call(s32[4]{0:T(128)S(1)} %pad_add_fusion.place, f32[1]{0:T(128)S(6)} %mul.25.scale, bf16[2,2,1024,256]{3,2,1,0:T(8,128)(2,1)} %get-tuple-element.148.kept.keep, bf16[2,1024,256]{2,1,0:T(8,128)(2,1)} %copy-done.18, bf16[2,1024,256]{2,1,0:T(8,128)(2,1)} %copy-done.19, ...), custom_call_target="tpu_custom_call" | custom-call | flops 307200000 | bytes 1000000 | tf_op jit(solution)/shard_map/finish_rows/pallas_call | solution.py:803
  183.9 3.7 %finish_rows.3 = (bf16[2048,256]{1,0:T(8,128)(2,1)}, f32[2048,256]{1,0:T(8,128)}) custom-call(s32[4]{0:T(128)S(1)} %pad_add_fusion.place, f32[1]{0:T(128)S(6)} %mul.25.scale, bf16[2,2,1024,256]{3,2,1,0:T(8,128)(2,1)} %get-tuple-element.165.keep, bf16[2,1024,256]{2,1,0:T(8,128)(2,1)} %collective-permute-done.22.near, ...), custom_call_target="tpu_custom_call", output_to_operand_aliasing={{0}: (11, {}), {1}: (12, {})} | custom-call | flops 307200000 | bytes 1000000 | tf_op jit(solution)/shard_map/finish_rows/pallas_call | solution.py:803
  187.7 2.3 %collective-permute-done.29.far_a = bf16[128,1024]{1,0:T(8,128)(2,1)S(1)} collective-permute-done((bf16[128,1024]{1,0:T(8,128)(2,1)S(1)}, bf16[128,1024]{1,0:T(8,128)(2,1)S(1)}, u32[]{:S(2)}, u32[]{:S(2)}) %collective-permute-start.29) | collective-permute-done | bytes 262176 | tf_op jit(solution)/shard_map/ppermute | solution.py:847
  190.0 1.3 finish_weights.1
  191.3 3.2 %collective-permute-done.28 = f32[1792]{0:T(1024)S(1)} collective-permute-done((f32[1792]{0:T(1024)S(1)}, f32[1792]{0:T(1024)S(1)}, u32[]{:S(2)}, u32[]{:S(2)}) %collective-permute-start.28) | collective-permute-done | bytes 7200 | tf_op jit(solution)/shard_map/ppermute | solution.py:847
  (123 shorter events, 10.3 us)
Async XLA Ops:
  0.6 6.1 %copy-start = (bf16[2048,256]{1,0:T(8,128)(2,1)S(1)}, bf16[2048,256]{1,0:T(8,128)(2,1)}, u32[]{:S(2)}) copy-start(bf16[2048,256]{1,0:T(8,128)(2,1)} %x_ref.3) | copy-start | bytes 3145732
  0.7 6.1 %copy-start.1 = (bf16[2048,256]{1,0:T(8,128)(2,1)S(1)}, bf16[2048,256]{1,0:T(8,128)(2,1)}, u32[]{:S(2)}) copy-start(bf16[2048,256]{1,0:T(8,128)(2,1)} %cot.3) | copy-start | bytes 3145732
  3.8 16.0 %collective-permute-start.1 = (bf16[1024,256]{1,0:T(8,128)(2,1)}, bf16[1024,256]{1,0:T(8,128)(2,1)}, u32[]{:S(2)}, u32[]{:S(2)}) collective-permute-start(bf16[1024,256]{1,0:T(8,128)(2,1)} %pad_maximum_fusion.1), channel_id=1, source_target_pairs={{0,2},{1,3},{2,0},{3,1},{4,6},{5,7},{6,4},{7,5},{8,10},{9,11},{10,... | collective-permute-start | bytes 1572872 | tf_op jit(solution)/shard_map/ppermute | solution.py:847
  6.8 15.3 %collective-permute-start = (bf16[2048,256]{1,0:T(8,128)(2,1)S(1)}, bf16[2048,256]{1,0:T(8,128)(2,1)S(1)}, u32[]{:S(2)}, u32[]{:S(2)}) collective-permute-start(bf16[2048,256]{1,0:T(8,128)(2,1)S(1)} %copy-done), channel_id=1, source_target_pairs={{0,1},{1,0},{2,3},{3,2},{4,5},{5,4},{6,7},{7,6},{8,9},{9,8},{10,11... | collective-permute-start | bytes 3145736 | tf_op jit(solution)/shard_map/ppermute | solution.py:847
  6.8 15.3 %collective-permute-start.4 = (bf16[2048,256]{1,0:T(8,128)(2,1)S(1)}, bf16[2048,256]{1,0:T(8,128)(2,1)}, u32[]{:S(2)}, u32[]{:S(2)}) collective-permute-start(bf16[2048,256]{1,0:T(8,128)(2,1)S(1)} %copy-done.1), channel_id=1, source_target_pairs={{0,1},{1,0},{2,3},{3,2},{4,5},{5,4},{6,7},{7,6},{8,9},{9,8},{10,11... | collective-permute-start | bytes 3145736 | tf_op jit(solution)/shard_map/ppermute | solution.py:847
  7.9 9.7 %collective-permute-start.2 = (f32[1]{0:T(128)}, f32[1]{0:T(128)}, u32[]{:S(2)}, u32[]{:S(2)}) collective-permute-start(f32[1]{0:T(128)} %mul_shard_map.6.scale), channel_id=1, source_target_pairs={{0,4},{4,0},{8,12},{12,8},{16,20},{20,16},{24,28},{28,24},{1,5},{5... | collective-permute-start | bytes 20 | tf_op jit(solution)/shard_map/ppermute | solution.py:847
  11.6 19.4 %collective-permute-start.5 = (bf16[1024,256]{1,0:T(8,128)(2,1)}, bf16[1024,256]{1,0:T(8,128)(2,1)}, u32[]{:S(2)}, u32[]{:S(2)}) collective-permute-start(bf16[1024,256]{1,0:T(8,128)(2,1)} %pad_maximum_fusion.2), channel_id=1, source_target_pairs={{0,2},{1,3},{2,0},{3,1},{4,6},{5,7},{6,4},{7,5},{8,10},{9,11},{10,... | collective-permute-start | bytes 1572872 | tf_op jit(solution)/shard_map/ppermute | solution.py:847
  13.8 6.0 %copy-start.14 = (bf16[1024,256]{1,0:T(8,128)(2,1)S(1)}, bf16[1024,256]{1,0:T(8,128)(2,1)}, u32[]{:S(2)}) copy-start(bf16[1024,256]{1,0:T(8,128)(2,1)} %slice.140) | copy-start | bytes 1572868
  13.8 6.0 %copy-start.15 = (bf16[1024,256]{1,0:T(8,128)(2,1)S(1)}, bf16[1024,256]{1,0:T(8,128)(2,1)}, u32[]{:S(2)}) copy-start(bf16[1024,256]{1,0:T(8,128)(2,1)} %slice.141) | copy-start | bytes 1572868
  19.8 2.2 %collective-permute-start.3 = (bf16[1024,256]{1,0:T(8,128)(2,1)}, bf16[1024,256]{1,0:T(8,128)(2,1)S(1)}, u32[]{:S(2)}, u32[]{:S(2)}) collective-permute-start(bf16[1024,256]{1,0:T(8,128)(2,1)} %collective-permute-done.1.x2.c2), channel_id=1, source_target_pairs={{0,1},{1,0},{2,3},{3,2},{4,5},{5,4},{6,7},{7,6},{8,9},{9,8},{10,11... | collective-permute-start | bytes 1572872 | tf_op jit(solution)/shard_map/ppermute | solution.py:847
  19.9 33.5 %collective-permute-start.7 = (bf16[2048,256]{1,0:T(8,128)(2,1)S(1)}, bf16[2048,256]{1,0:T(8,128)(2,1)S(1)}, u32[]{:S(2)}, u32[]{:S(2)}) collective-permute-start(bf16[2048,256]{1,0:T(8,128)(2,1)S(1)} %pad_maximum_fusion), channel_id=1, source_target_pairs={{0,2},{1,3},{2,0},{3,1},{4,6},{5,7},{6,4},{7,5},{8,10},{9,11},{10,... | collective-permute-start | bytes 3145736 | tf_op jit(solution)/shard_map/ppermute | solution.py:847
  22.0 11.1 %copy-start.3 = (bf16[2048,256]{1,0:T(8,128)(2,1)}, bf16[2048,256]{1,0:T(8,128)(2,1)S(1)}, u32[]{:S(2)}) copy-start(bf16[2048,256]{1,0:T(8,128)(2,1)S(1)} %collective-permute-done.x1) | copy-start | bytes 3145732
  31.0 2.1 %collective-permute-start.6 = (bf16[1024,256]{1,0:T(8,128)(2,1)}, bf16[1024,256]{1,0:T(8,128)(2,1)S(1)}, u32[]{:S(2)}, u32[]{:S(2)}) collective-permute-start(bf16[1024,256]{1,0:T(8,128)(2,1)} %collective-permute-done.5.x2.c2), channel_id=1, source_target_pairs={{0,1},{1,0},{2,3},{3,2},{4,5},{5,4},{6,7},{7,6},{8,9},{9,8},{10,11... | collective-permute-start | bytes 1572872 | tf_op jit(solution)/shard_map/ppermute | solution.py:847
  39.5 16.7 %copy-start.2 = (bf16[2048,256]{1,0:T(8,128)(2,1)S(1)}, bf16[2048,256]{1,0:T(8,128)(2,1)}, u32[]{:S(2)}) copy-start(bf16[2048,256]{1,0:T(8,128)(2,1)} %cot.3) | copy-start | bytes 3145732
  39.5 16.7 %copy-start.4 = (bf16[2048,256]{1,0:T(8,128)(2,1)S(1)}, bf16[2048,256]{1,0:T(8,128)(2,1)}, u32[]{:S(2)}) copy-start(bf16[2048,256]{1,0:T(8,128)(2,1)} %copy-done.3) | copy-start | bytes 3145732
  53.4 2.7 %collective-permute-start.8 = (bf16[2048,256]{1,0:T(8,128)(2,1)S(1)}, bf16[2048,256]{1,0:T(8,128)(2,1)S(1)}, u32[]{:S(2)}, u32[]{:S(2)}) collective-permute-start(bf16[2048,256]{1,0:T(8,128)(2,1)S(1)} %collective-permute-done.7.x2.c2), channel_id=1, source_target_pairs={{0,1},{1,0},{2,3},{3,2},{4,5},{5,4},{6,7},{7,6},{8,9},{9,8},{10,11... | collective-permute-start | bytes 3145736 | tf_op jit(solution)/shard_map/ppermute | solution.py:847
  66.2 7.4 %copy-start.6 = (f32[1024,128]{1,0:T(8,128)}, f32[1024,128]{1,0:T(8,128)S(1)}, u32[]{:S(2)}) copy-start(f32[1024,128]{1,0:T(8,128)S(1)} %get-tuple-element.185.stats) | copy-start | bytes 1572868
  66.2 7.4 %copy-start.7 = (f32[32,1024]{1,0:T(8,128)}, f32[32,1024]{1,0:T(8,128)S(1)}, u32[]{:S(2)}) copy-start(f32[32,1024]{1,0:T(8,128)S(1)} %get-tuple-element.128) | copy-start | bytes 393220
  73.6 9.7 %copy-start.27 = (bf16[4,128,1024]{2,1,0:T(8,128)(2,1)S(1)}, bf16[4,128,1024]{2,1,0:T(8,128)(2,1)}, u32[]{:S(2)}) copy-start(bf16[4,128,1024]{2,1,0:T(8,128)(2,1)} %get-tuple-element.140) | copy-start | bytes 3145732
  81.1 28.7 %collective-permute-start.10 = (bf16[2,2,128,1024]{3,2,1,0:T(8,128)(2,1)}, bf16[2,2,128,1024]{3,2,1,0:T(8,128)(2,1)S(1)}, u32[]{:S(2)}, u32[]{:S(2)}) collective-permute-start(bf16[2,2,128,1024]{3,2,1,0:T(8,128)(2,1)} %get-tuple-element.141), channel_id=1, source_target_pairs={{0,8},{4,12},{8,0},{12,4},{16,24},{20,28},{24,16},{28,20},{1,9},{5... | collective-permute-start | bytes 3145736 | tf_op jit(solution)/shard_map/ppermute | solution.py:847
  83.2 26.6 %collective-permute-start.9 = (bf16[4,128,1024]{2,1,0:T(8,128)(2,1)S(1)}, bf16[4,128,1024]{2,1,0:T(8,128)(2,1)S(1)}, u32[]{:S(2)}, u32[]{:S(2)}) collective-permute-start(bf16[4,128,1024]{2,1,0:T(8,128)(2,1)S(1)} %copy-done.27), channel_id=1, source_target_pairs={{0,4},{4,0},{8,12},{12,8},{16,20},{20,16},{24,28},{28,24},{1,5},{5... | collective-permute-start | bytes 3145736 | tf_op jit(solution)/shard_map/ppermute | solution.py:847
  95.3 14.4 %collective-permute-start.11 = (bf16[1024,256]{1,0:T(8,128)(2,1)}, bf16[1024,256]{1,0:T(8,128)(2,1)S(1)}, u32[]{:S(2)}, u32[]{:S(2)}) collective-permute-start(bf16[1024,256]{1,0:T(8,128)(2,1)} %get-tuple-element.142), channel_id=1, source_target_pairs={{0,1},{1,0},{2,3},{3,2},{4,5},{5,4},{6,7},{7,6},{8,9},{9,8},{10,11... | collective-permute-start | bytes 1572872 | tf_op jit(solution)/shard_map/ppermute | solution.py:847
  95.3 14.5 %collective-permute-start.12 = (bf16[1024,256]{1,0:T(8,128)(2,1)}, bf16[1024,256]{1,0:T(8,128)(2,1)S(1)}, u32[]{:S(2)}, u32[]{:S(2)}) collective-permute-start(bf16[1024,256]{1,0:T(8,128)(2,1)} %get-tuple-element.143), channel_id=1, source_target_pairs={{0,1},{1,0},{2,3},{3,2},{4,5},{5,4},{6,7},{7,6},{8,9},{9,8},{10,11... | collective-permute-start | bytes 1572872 | tf_op jit(solution)/shard_map/ppermute | solution.py:847
  111.4 5.0 %copy-start.26 = (bf16[2,1024,256]{2,1,0:T(8,128)(2,1)S(1)}, bf16[2,1024,256]{2,1,0:T(8,128)(2,1)}, u32[]{:S(2)}) copy-start(bf16[2,1024,256]{2,1,0:T(8,128)(2,1)} %get-tuple-element.158) | copy-start | bytes 3145732
  116.4 13.0 %collective-permute-start.13 = (bf16[2,1024,256]{2,1,0:T(8,128)(2,1)S(1)}, bf16[2,1024,256]{2,1,0:T(8,128)(2,1)S(1)}, u32[]{:S(2)}, u32[]{:S(2)}) collective-permute-start(bf16[2,1024,256]{2,1,0:T(8,128)(2,1)S(1)} %copy-done.26), channel_id=1, source_target_pairs={{0,1},{1,0},{2,3},{3,2},{4,5},{5,4},{6,7},{7,6},{8,9},{9,8},{10,11... | collective-permute-start | bytes 3145736 | tf_op jit(solution)/shard_map/ppermute | solution.py:847
  116.4 27.7 %collective-permute-start.16 = (bf16[2,1024,256]{2,1,0:T(8,128)(2,1)}, bf16[2,1024,256]{2,1,0:T(8,128)(2,1)S(1)}, u32[]{:S(2)}, u32[]{:S(2)}) collective-permute-start(bf16[2,1024,256]{2,1,0:T(8,128)(2,1)} %get-tuple-element.153), channel_id=1, source_target_pairs={{0,2},{1,3},{2,0},{3,1},{4,6},{5,7},{6,4},{7,5},{8,10},{9,11},{10,... | collective-permute-start | bytes 3145736 | tf_op jit(solution)/shard_map/ppermute | solution.py:847
  118.0 26.1 %collective-permute-start.14 = (bf16[272,1024]{1,0:T(8,128)(2,1)}, bf16[272,1024]{1,0:T(8,128)(2,1)S(1)}, u32[]{:S(2)}, u32[]{:S(2)}) collective-permute-start(bf16[272,1024]{1,0:T(8,128)(2,1)} %get-tuple-element.160), channel_id=1, source_target_pairs={{0,8},{4,12},{8,0},{12,4},{16,24},{20,28},{24,16},{28,20},{1,9},{5... | collective-permute-start | bytes 1671176 | tf_op jit(solution)/shard_map/ppermute | solution.py:847
  118.4 23.8 %collective-permute-start.15 = (bf16[2,128,1024]{2,1,0:T(8,128)(2,1)}, bf16[2,128,1024]{2,1,0:T(8,128)(2,1)S(1)}, u32[]{:S(2)}, u32[]{:S(2)}) collective-permute-start(bf16[2,128,1024]{2,1,0:T(8,128)(2,1)} %get-tuple-element.161), channel_id=1, source_target_pairs={{0,16},{4,20},{8,24},{12,28},{16,0},{20,4},{24,8},{28,12},{1,17},{... | collective-permute-start | bytes 1572872 | tf_op jit(solution)/shard_map/ppermute | solution.py:847
  128.9 24.9 %collective-permute-start.24 = (bf16[4,128,1024]{2,1,0:T(8,128)(2,1)}, bf16[4,128,1024]{2,1,0:T(8,128)(2,1)S(1)}, u32[]{:S(2)}, u32[]{:S(2)}) collective-permute-start(bf16[4,128,1024]{2,1,0:T(8,128)(2,1)} %get-tuple-element.179), channel_id=1, source_target_pairs={{0,4},{4,0},{8,12},{12,8},{16,20},{20,16},{24,28},{28,24},{1,5},{5... | collective-permute-start | bytes 3145736 | tf_op jit(solution)/shard_map/ppermute | solution.py:847
  130.4 14.3 %copy-start.23 = (bf16[2,128,1024]{2,1,0:T(8,128)(2,1)S(1)}, bf16[2,128,1024]{2,1,0:T(8,128)(2,1)}, u32[]{:S(2)}) copy-start(bf16[2,128,1024]{2,1,0:T(8,128)(2,1)} %get-tuple-element.151) | copy-start | bytes 1572868
  130.4 14.5 %copy-start.22 = (bf16[2,128,1024]{2,1,0:T(8,128)(2,1)S(1)}, bf16[2,128,1024]{2,1,0:T(8,128)(2,1)}, u32[]{:S(2)}) copy-start(bf16[2,128,1024]{2,1,0:T(8,128)(2,1)} %get-tuple-element.152) | copy-start | bytes 1572868
  141.2 5.8 %copy-start.13 = (bf16[2,2,1024,256]{3,2,1,0:T(8,128)(2,1)S(1)}, bf16[2,2,1024,256]{3,2,1,0:T(8,128)(2,1)}, u32[]{:S(2)}) copy-start(bf16[2,2,1024,256]{3,2,1,0:T(8,128)(2,1)} %get-tuple-element.165.keep) | copy-start | bytes 6291460
  144.1 2.4 %collective-permute-start.17 = (bf16[1024,256]{1,0:T(8,128)(2,1)}, bf16[1024,256]{1,0:T(8,128)(2,1)S(1)}, u32[]{:S(2)}, u32[]{:S(2)}) collective-permute-start(bf16[1024,256]{1,0:T(8,128)(2,1)} %get-tuple-element.166), channel_id=1, source_target_pairs={{0,1},{1,0},{2,3},{3,2},{4,5},{5,4},{6,7},{7,6},{8,9},{9,8},{10,11... | collective-permute-start | bytes 1572872 | tf_op jit(solution)/shard_map/ppermute | solution.py:847
  144.2 2.9 %collective-permute-start.19 = (bf16[1024,256]{1,0:T(8,128)(2,1)}, bf16[1024,256]{1,0:T(8,128)(2,1)S(1)}, u32[]{:S(2)}, u32[]{:S(2)}) collective-permute-start(bf16[1024,256]{1,0:T(8,128)(2,1)} %get-tuple-element.174), channel_id=1, source_target_pairs={{0,1},{1,0},{2,3},{3,2},{4,5},{5,4},{6,7},{7,6},{8,9},{9,8},{10,11... | collective-permute-start | bytes 1572872 | tf_op jit(solution)/shard_map/ppermute | solution.py:847
  144.8 9.0 %copy-start.17 = (bf16[4,128,1024]{2,1,0:T(8,128)(2,1)S(1)}, bf16[4,128,1024]{2,1,0:T(8,128)(2,1)}, u32[]{:S(2)}) copy-start(bf16[4,128,1024]{2,1,0:T(8,128)(2,1)} %get-tuple-element.156) | copy-start | bytes 3145732
  144.8 1.7 collective-permute-start.18
  148.2 30.9 %collective-permute-start.20 = (bf16[2,1024,256]{2,1,0:T(8,128)(2,1)}, bf16[2,1024,256]{2,1,0:T(8,128)(2,1)S(1)}, u32[]{:S(2)}, u32[]{:S(2)}) collective-permute-start(bf16[2,1024,256]{2,1,0:T(8,128)(2,1)} %maximum_add_fusion), channel_id=1, source_target_pairs={{0,2},{1,3},{2,0},{3,1},{4,6},{5,7},{6,4},{7,5},{8,10},{9,11},{10,... | collective-permute-start | bytes 3145736 | tf_op jit(solution)/shard_map/ppermute | solution.py:847
  153.7 25.7 %copy-start.8 = (f32[32,1024]{1,0:T(8,128)S(1)}, f32[32,1024]{1,0:T(8,128)}, u32[]{:S(2)}) copy-start(f32[32,1024]{1,0:T(8,128)} %copy-done.7) | copy-start | bytes 393220
  153.7 25.3 %collective-permute-start.22 = (bf16[2,1024,256]{2,1,0:T(8,128)(2,1)}, bf16[2,1024,256]{2,1,0:T(8,128)(2,1)}, u32[]{:S(2)}, u32[]{:S(2)}) collective-permute-start(bf16[2,1024,256]{2,1,0:T(8,128)(2,1)} %get-tuple-element.178), channel_id=1, source_target_pairs={{0,1},{1,0},{2,3},{3,2},{4,5},{5,4},{6,7},{7,6},{8,9},{9,8},{10,11... | collective-permute-start | bytes 3145736 | tf_op jit(solution)/shard_map/ppermute | solution.py:847
  154.7 25.4 %copy-start.12 = (f32[256]{0:T(256)S(1)}, f32[256]{0:T(256)}, u32[]{:S(2)}) copy-start(f32[256]{0:T(256)} %param.23) | copy-start | bytes 3076
  154.7 20.6 %collective-permute-start.25 = (bf16[2,128,1024]{2,1,0:T(8,128)(2,1)}, bf16[2,128,1024]{2,1,0:T(8,128)(2,1)S(1)}, u32[]{:S(2)}, u32[]{:S(2)}) collective-permute-start(bf16[2,128,1024]{2,1,0:T(8,128)(2,1)} %get-tuple-element.204), channel_id=1, source_target_pairs={{0,8},{4,12},{8,0},{12,4},{16,24},{20,28},{24,16},{28,20},{1,9},{5... | collective-permute-start | bytes 1572872 | tf_op jit(solution)/shard_map/ppermute | solution.py:847
  159.1 16.8 %collective-permute-start.23 = (bf16[144,1024]{1,0:T(8,128)(2,1)}, bf16[144,1024]{1,0:T(8,128)(2,1)S(1)}, u32[]{:S(2)}, u32[]{:S(2)}) collective-permute-start(bf16[144,1024]{1,0:T(8,128)(2,1)} %maximum_maximum_fusion), channel_id=1, source_target_pairs={{0,16},{4,20},{8,24},{12,28},{16,0},{20,4},{24,8},{28,12},{1,17},{... | collective-permute-start | bytes 884744 | tf_op jit(solution)/shard_map/ppermute | solution.py:847
  159.5 28.2 %collective-permute-start.30 = (bf16[128,1024]{1,0:T(8,128)(2,1)}, bf16[128,1024]{1,0:T(8,128)(2,1)S(1)}, u32[]{:S(2)}, u32[]{:S(2)}) collective-permute-start(bf16[128,1024]{1,0:T(8,128)(2,1)} %get-tuple-element.208), channel_id=1, source_target_pairs={{0,4},{4,0},{8,12},{12,8},{16,20},{20,16},{24,28},{28,24},{1,5},{5... | collective-permute-start | bytes 786440 | tf_op jit(solution)/shard_map/ppermute | solution.py:847
  175.3 3.8 %collective-permute-start.21 = (f32[2,3072]{1,0:T(2,128)S(1)}, f32[2,3072]{1,0:T(2,128)S(1)}, u32[]{:S(2)}, u32[]{:S(2)}) collective-permute-start(f32[2,3072]{1,0:T(2,128)S(1)} %add.97), channel_id=1, source_target_pairs={{0,2},{1,3},{2,0},{3,1},{4,6},{5,7},{6,4},{7,5},{8,10},{9,11},{10,... | collective-permute-start | bytes 73736 | tf_op jit(solution)/shard_map/ppermute | solution.py:847
  175.9 14.0 %collective-permute-start.29 = (bf16[128,1024]{1,0:T(8,128)(2,1)S(1)}, bf16[128,1024]{1,0:T(8,128)(2,1)S(1)}, u32[]{:S(2)}, u32[]{:S(2)}) collective-permute-start(bf16[128,1024]{1,0:T(8,128)(2,1)S(1)} %get-tuple-element.210), channel_id=1, source_target_pairs={{0,16},{4,20},{8,24},{12,28},{16,0},{20,4},{24,8},{28,12},{1,17},{... | collective-permute-start | bytes 786440 | tf_op jit(solution)/shard_map/ppermute | solution.py:847
  179.5 4.3 %collective-permute-start.26 = (f32[1792]{0:T(1024)S(1)}, f32[1792]{0:T(1024)S(1)}, u32[]{:S(2)}, u32[]{:S(2)}) collective-permute-start(f32[1792]{0:T(1024)S(1)} %maximum_multiply_fusion), channel_id=1, source_target_pairs={{0,4},{4,0},{8,12},{12,8},{16,20},{20,16},{24,28},{28,24},{1,5},{5... | collective-permute-start | bytes 21512 | tf_op jit(solution)/shard_map/ppermute | solution.py:847
  183.8 6.2 %collective-permute-start.27 = (f32[1792]{0:T(1024)S(1)}, f32[1792]{0:T(1024)S(1)}, u32[]{:S(2)}, u32[]{:S(2)}) collective-permute-start(f32[1792]{0:T(1024)S(1)} %fusion.6), channel_id=1, source_target_pairs={{0,8},{4,12},{8,0},{12,4},{16,24},{20,28},{24,16},{28,20},{1,9},{5... | collective-permute-start | bytes 21512 | tf_op jit(solution)/shard_map/ppermute | solution.py:847
  190.0 4.5 %collective-permute-start.28 = (f32[1792]{0:T(1024)S(1)}, f32[1792]{0:T(1024)S(1)}, u32[]{:S(2)}, u32[]{:S(2)}) collective-permute-start(f32[1792]{0:T(1024)S(1)} %add.114), channel_id=1, source_target_pairs={{0,16},{4,20},{8,24},{12,28},{16,0},{20,4},{24,8},{28,12},{1,17},{... | collective-permute-start | bytes 21512 | tf_op jit(solution)/shard_map/ppermute | solution.py:847
  (11 other events, 28.7 us)
where the time goes:
time: 196 us
  Pallas kernels  111 us (57%)
  waiting for transfers between devices  40.4 us (21%)
  starting transfers between devices  25.5 us (13%)
  local copies, waits for them, and re-layouts  8.79 us (4%)
  other arithmetic  5.88 us (3%)
  between operations  4.3 us (2%)
    ppermute x31, waiting for transfers between devices, swap(): return lax.ppermute(value, axis, [(i, i ^ bit) for i in range(size)])  40.4 us
    pallas_call x2, Pallas kernels, attend(): pl.pallas_call(functools.partial(attend_kernel, tiles=tiles, tile=tile, p...  27.8 us
    ppermute x31, starting transfers between devices, swap(): return lax.ppermute(value, axis, [(i, i ^ bit) for i in range(size)])  25.5 us
    pallas_call x3, Pallas kernels, norm_mlp(): pl.pallas_call(functools.partial(norm_mlp_kernel, first_row=first_row), g...  21.4 us
    pallas_call x2, Pallas kernels, branch_parts(): pl.pallas_call(branch_kernel, grid_spec=pltpu.PrefetchScalarGridSpec(num_...  21.4 us
    pallas_call x2, Pallas kernels, weight_mlp(): pl.pallas_call(kernel, grid_spec=pltpu.PrefetchScalarGridSpec(num_scalar_...  14.9 us
    pallas_call x1, Pallas kernels, weight_att(): pl.pallas_call(weight_att_kernel, grid_spec=pltpu.PrefetchScalarGridSpec(...  7.81 us
    pallas_call x2, Pallas kernels, finish_rows(): pl.pallas_call(functools.partial(final_kernel, first_row=first_row), grid...  7.45 us
  transfers between devices with their start and end apart: 31, of which 14 were waited for; matrix products, arithmetic and copies ran while one was open for 4% of the time, Pallas kernels for 41%

commit v1 on v0

--- a/solution.py
+++ b/solution.py
@@ -767,6 +767,33 @@
     )(count, *[outside(value) for value in (keep_in, x_in, hold, z_down, kept, *core)])
 
 
+def relay_kernel(count, low, z_in, zz_in, kept, total):
+    size, units = kept.shape
+    kept[...] = low[0] + z_in[:size]
+    zz_in[:size] = low[1] + z_in[size : 2 * size]
+    tail = z_in[2 * size :].astype(F32)
+    value = count[0] + tail[0:1] + tail[1:2]
+    high = value.astype(BF).astype(F32)
+    row = lax.broadcasted_iota(jnp.int32, tail.shape, 0)
+    zz_in[size:] = jnp.where(row == 0, high, jnp.where(row == 1, value - high, 0.0)).astype(BF)
+    total[...] = jnp.broadcast_to(value[:, :128], total.shape)
+
+
+def relay(count, low, z_in):
+    _, size, units = low.shape
+    inner = pl.BlockSpec(memory_space=pltpu.VMEM)
+    shape = jax.ShapeDtypeStruct
+    return pl.pallas_call(
+        relay_kernel,
+        in_specs=[pl.BlockSpec(memory_space=pltpu.SMEM), inner, inner],
+        out_specs=[inner] * 3,
+        out_shape=[shape((size + 16, units), BF), shape((size, units), BF), shape((8, 128), F32)],
+        compiler_params=pltpu.CompilerParams(vmem_limit_bytes=VMEM_BYTES),
+        cost_estimate=cost(1),
+        name="relay",
+    )(count, low, z_in)
+
+
 def final_kernel(place, scale, keep, near, far, x_ref, cot, stats, sums, gain, bias_down, *refs, first_row):
     mixed, g_x = refs[-2:]
     step = pl.program_id(0)
@@ -857,13 +884,6 @@
 
 def add_core(kept, core):
     return kept[1] + jnp.stack(core)
-
-
-def pack(values, units):
-    padded = jnp.concatenate([values, jnp.zeros((-values.shape[0] % units,), F32)]).reshape(-1, units)
-    high = lax.reduce_precision(padded, 8, 7)
-    rows = jnp.concatenate([high, padded - high], axis=0).astype(BF)
-    return jnp.concatenate([rows, jnp.zeros((-rows.shape[0] % 16, units), BF)], axis=0)
 
 
 def unpack(rows, count):
@@ -943,9 +963,8 @@
     kept_1, near_1, sent_1, sums_1, columns_1 = branch(place, mlp_1, att_1, 0, pad_len)
     core_1 = [swap(part, "narrow", 1) for part in sent_1]
     z_in, zz_down, y_0, sums_0, columns_0 = lax.optimization_barrier((z_in, zz_down, y_0, sums_0, columns_0, sums_1))[:5]
-    count_row = count_x + unpack(z_in[2 * size :], units)[:128]
-    zz_in = swap(jnp.concatenate([low_in[1] + z_in[size : 2 * size], pack(jnp.broadcast_to(count_row[:1], (units,)), units)], axis=0), "wide", 4)
-    low_in = low_in[0] + z_in[:size]
+    zz_in, low_in, count_row = relay(count_x, low_in, z_in)
+    zz_in = swap(zz_in, "wide", 4)
     x_d = swap(low_down[1] + zz_down[1], "wide", 1)
     low_down = low_down[0] + zz_down[0]
     sums = jnp.concatenate([sums_0[:2], sums_1[:2], columns_0[:2] + columns_1[:2]], axis=1)
@@ -954,40 +973,46 @@
     core_1 = [after(part, sums, low_down, low_in) for part in core_1]
     chip_1 = add_core(kept_1, core_1)
     y_1 = swap(chip_1, "narrow", 2)
-    far_sums = swap(after(sums, chip_1), "narrow", 2)
-    near_1 = swap(after(near_1, chip_1), "narrow", 1)
+    far_sums = swap(after(sums[:, :rows_all], chip_1), "narrow", 2)
     x_a = after(x_a, chip_1)
     z_a = swap(keep_a[2:] + x_a[2:], "wide", 2)
     low_a = keep_a[:2] + x_a[:2]
-    z_a = after(z_a, low_a)
+    sum_up, sum_down, columns = lax.optimization_barrier((mlp_0[3], mlp_0[4], sums[:, rows_all:], low_a))[:3]
+    small = jnp.concatenate([columns.reshape(-1), jnp.sum(sum_up + mlp_1[3], axis=0), jnp.sum(sum_down + mlp_1[4], axis=0)])
+    small = count * small
+    small = small + swap(small, "wide", 1)
+    z_small = swap(small, "wide", 2)
+    zz_in = after(zz_in, small)
+    count_row = count_row[0] + unpack(zz_in[size:], units)[:128]
+    per_count = groups / count_row[:1]
+    scale = count * per_count
+    y_1, far_sums = lax.optimization_barrier((y_1, far_sums, scale))[:2]
+    sums = sums[:, :rows_all] + far_sums
+    small = small + after(z_small, sums)
+    z_a = after(z_a, small)
     zz_a = swap(low_a[1] + z_a[1], "wide", 4)
     low_a = low_a[0] + z_a[0]
-    y_1, far_sums, near_1, zz_in = lax.optimization_barrier((y_1, far_sums, near_1, zz_in, low_a))[:4]
-    count_row = count_row + unpack(zz_in[size:], units)[:128]
-    per_count = groups / count_row[:1]
-    scale = count * per_count
-    sums = sums + far_sums
-    columns = lax.dynamic_slice_in_dim(sums[:, rows_all:], column * cols, cols, 1)
-    sum_up, sum_down = [after(mlp_0[k], y_1) + mlp_1[k] for k in (3, 4)]
-    small = count * jnp.concatenate([columns[1] / own_gain[0], columns[0], jnp.sum(sum_up, axis=0), jnp.sum(sum_down, axis=0)])
-    small = small + swap(small, "wide", 1)
-    ends = finish_rows(place, scale, kept_0, near_0, y_0, inputs, cotangent, mlp_0[2], sums, own_gain, b_row, 0, 0)
-    small = small + swap(small, "wide", 2)
+    zz_small = swap(small, "wide", 4)
+    near_1 = swap(after(near_1, low_a), "narrow", 1)
+    ends = finish_rows(after(place, small), scale, kept_0, near_0, y_0, inputs, cotangent, mlp_0[2], sums, own_gain, b_row, 0, 0)
     ends = finish_rows(place, scale, kept_1, near_1, y_1, inputs, cotangent, mlp_1[2], sums, own_gain, b_row, 1, 0, ends)
-    small = per_count * (small + swap(small, "wide", 4))
-    zz_a, x_d = lax.optimization_barrier((zz_a, x_d, ends[0]))[:2]
+    small = per_count * (small + after(zz_small, ends[0]))
+    columns = small[: 2 * width].reshape(2, width)
+    far_columns = swap(columns, "narrow", 2)
+    zz_a, x_d, far_columns = lax.optimization_barrier((zz_a, x_d, far_columns, ends[0]))[:3]
+    columns = lax.dynamic_slice_in_dim(columns + far_columns, column * cols, cols, 1)
     g_in, g_down, g_qkv, g_out = finish_weights(per_count, low_in, zz_in, low_down, x_d, low_a, zz_a)
     return (
         ends[0],
         ends[1],
-        small[:cols],
-        small[cols : 2 * cols],
+        columns[1] / own_gain[0],
+        columns[0],
         jnp.transpose(g_qkv, (1, 0, 2)),
         g_out,
         g_in,
-        small[2 * cols : 2 * cols + units],
+        small[2 * width : 2 * width + units],
         g_down,
-        small[2 * cols + units :],
+        small[2 * width + units :],
     )
 
 

time: 196 us -> 193 us (0.985)
  starting transfers between devices: 25.5 us -> 30 us
  other arithmetic: 5.88 us -> 2.94 us
  waiting for transfers between devices: 40.4 us -> 38.1 us
    ppermute x31 -> x32, starting transfers between devices: 25.5 us -> 30 us  [swap(): return lax.ppermute(value, axis, [(i, i ^ bit) for i in range(size)])]
    ppermute x31 -> x32, waiting for transfers between devices: 40.4 us -> 38.1 us  [swap(): return lax.ppermute(value, axis, [(i, i ^ bit) for i in range(size)])]
  transfers between devices with their start and end apart: 31 -> 32, of which waited for: 14 -> 12; matrix products, arithmetic and copies ran while one was open for 4% -> 2% of each run, Pallas kernels for 41% -> 41%
where the time goes in v1:
time: 193 us
  Pallas kernels  111 us (58%)
  waiting for transfers between devices  38.1 us (20%)
  starting transfers between devices  30 us (16%)
  local copies, waits for them, and re-layouts  8.25 us (4%)
  other arithmetic  2.94 us (2%)
  between operations  2.52 us (1%)
    ppermute x32, waiting for transfers between devices, swap(): return lax.ppermute(value, axis, [(i, i ^ bit) for i in range(size)])  38.1 us
    ppermute x32, starting transfers between devices, swap(): return lax.ppermute(value, axis, [(i, i ^ bit) for i in range(size)])  30 us
    pallas_call x2, Pallas kernels, attend(): pl.pallas_call(functools.partial(attend_kernel, tiles=tiles, tile=tile, p...  27.7 us
    pallas_call x3, Pallas kernels, norm_mlp(): pl.pallas_call(functools.partial(norm_mlp_kernel, first_row=first_row), g...  21.5 us
    pallas_call x2, Pallas kernels, branch_parts(): pl.pallas_call(branch_kernel, grid_spec=pltpu.PrefetchScalarGridSpec(num_...  21.4 us
    pallas_call x2, Pallas kernels, weight_mlp(): pl.pallas_call(kernel, grid_spec=pltpu.PrefetchScalarGridSpec(num_scalar_...  15.1 us
    pallas_call x1, Pallas kernels, weight_att(): pl.pallas_call(weight_att_kernel, grid_spec=pltpu.PrefetchScalarGridSpec(...  7.8 us
    pallas_call x2, Pallas kernels, finish_rows(): pl.pallas_call(functools.partial(final_kernel, first_row=first_row), grid...  7.46 us
  transfers between devices with their start and end apart: 32, of which 12 were waited for; matrix products, arithmetic and copies ran while one was open for 2% of the time, Pallas kernels for 41%

profile of v1, /device:TPU:0, one launch (start us, length us, event | category | flops | bytes accessed | tf_op | source)
XLA Modules:
  0.0 192.7 jit_solution(14514869282861363752)
XLA Ops:
  0.7 1.2 fusion.5
  1.9 1.1 fusion.6
  3.0 0.8 pad_maximum_fusion.1
  3.8 3.0 %collective-permute-start.1 = (bf16[1024,256]{1,0:T(8,128)(2,1)}, bf16[1024,256]{1,0:T(8,128)(2,1)}, u32[]{:S(2)}, u32[]{:S(2)}) collective-permute-start(bf16[1024,256]{1,0:T(8,128)(2,1)} %pad_maximum_fusion.1), channel_id=1, source_target_pairs={{0,2},{1,3},{2,0},{3,1},{4,6},{5,7},{6,4},{7,5},{8,10},{9,11},{10,... | collective-permute-start | bytes 1572872 | tf_op jit(solution)/shard_map/ppermute | solution.py:874
  7.9 2.9 %collective-permute-start.2 = (f32[1]{0:T(128)}, f32[1]{0:T(128)}, u32[]{:S(2)}, u32[]{:S(2)}) collective-permute-start(f32[1]{0:T(128)} %mul_shard_map.6.scale), channel_id=1, source_target_pairs={{0,4},{4,0},{8,12},{12,8},{16,20},{20,16},{24,28},{28,24},{1,5},{5... | collective-permute-start | bytes 20 | tf_op jit(solution)/shard_map/ppermute | solution.py:874
  10.8 0.8 pad_maximum_fusion.2
  12.1 0.8 slice.115
  12.9 0.8 slice.116
  13.8 3.7 %load_weights.1 = (bf16[1024,256]{1,0:T(8,128)(2,1)S(1)}, bf16[1024,256]{1,0:T(8,128)(2,1)S(1)}, bf16[1024,256]{1,0:T(8,128)(2,1)S(1)}, bf16[256,1024]{1,0:T(8,1...) custom-call(s32[4]{0:T(128)S(1)} %pad_add_fusion.place, ...), custom_call_target="tpu_custom_call" | custom-call | flops 300000000 | bytes 1000000 | tf_op jit(solution)/shard_map/load_weights/pallas_call | solution.py:320
  18.2 1.6 collective-permute-done.1.x2.c2
  19.9 2.1 %collective-permute-start.7 = (bf16[2048,256]{1,0:T(8,128)(2,1)S(1)}, bf16[2048,256]{1,0:T(8,128)(2,1)S(1)}, u32[]{:S(2)}, u32[]{:S(2)}) collective-permute-start(bf16[2048,256]{1,0:T(8,128)(2,1)S(1)} %pad_maximum_fusion), channel_id=1, source_target_pairs={{0,2},{1,3},{2,0},{3,1},{4,6},{5,7},{6,4},{7,5},{8,10},{9,11},{10,... | collective-permute-start | bytes 3145736 | tf_op jit(solution)/shard_map/ppermute | solution.py:874
  22.1 5.9 %norm_mlp.3 = (bf16[2,1024,1024]{2,1,0:T(8,128)(2,1)S(1)}, bf16[2,1024,1024]{2,1,0:T(8,128)(2,1)S(1)}, f32[1024,128]{1,0:T(8,128)S(1)}, f32[32,1024]{1,0:T(8,128)S(1)}, f32[32,256]{1,0:T(8,128)S(1)}) custom-call(s32[4]{0:T(128)S(1)} %pad_add_fusion.place, bf16[2048,256]{1,0:T(8,128)(2,1)S(1)} %copy-done, bf16[2048,256]{1,0:T(8,128)(2,1)S(1)} %collective-permute-done.x1, ...), custom_call_target="tpu_custom_call" | custom-call | flops 512000000 | bytes 1000000 | tf_op jit(solution)/shard_map/norm_mlp/pallas_call | solution.py:399
  28.0 3.0 %collective-permute-done.5.x2.c2 = bf16[1024,256]{1,0:T(8,128)(2,1)} collective-permute-done((bf16[1024,256]{1,0:T(8,128)(2,1)}, bf16[1024,256]{1,0:T(8,128)(2,1)}, u32[]{:S(2)}, u32[]{:S(2)}) %collective-permute-start.5) | collective-permute-done | bytes 524320 | tf_op jit(solution)/shard_map/ppermute | solution.py:874
  31.1 2.1 %collective-permute-done.6.x3.c3 = bf16[1024,256]{1,0:T(8,128)(2,1)S(1)} collective-permute-done((bf16[1024,256]{1,0:T(8,128)(2,1)}, bf16[1024,256]{1,0:T(8,128)(2,1)S(1)}, u32[]{:S(2)}, u32[]{:S(2)}) %collective-permute-start.6) | collective-permute-done | bytes 524320 | tf_op jit(solution)/shard_map/ppermute | solution.py:874
  33.2 5.5 %norm_mlp.4 = (bf16[2,1024,1024]{2,1,0:T(8,128)(2,1)S(1)}, bf16[2,1024,1024]{2,1,0:T(8,128)(2,1)S(1)}, f32[1024,128]{1,0:T(8,128)S(1)}, f32[32,1024]{1,0:T(8,128)S(1)}, f32[32,256]{1,0:T(8,128)S(1)}) custom-call(s32[4]{0:T(128)S(1)} %pad_add_fusion.place, ...), custom_call_target="tpu_custom_call", output_to_operand_aliasing={{0}: (14, {}), {1}: (15, {}), {2}: (16, {}), {3}: (17, {}),... | custom-call | flops 512000000 | bytes 1000000 | tf_op jit(solution)/shard_map/norm_mlp/pallas_call | solution.py:399
  38.7 0.8 copy-done.5
  39.5 13.9 %attend.2 = (bf16[1024,256]{1,0:T(8,128)(2,1)S(1)}, bf16[1024,768]{1,0:T(8,128)(2,1)S(1)}) custom-call(s32[4]{0:T(128)S(1)} %pad_add_fusion.place, bf16[2,1024,1024]{2,1,0:T(8,128)(2,1)S(1)} %get-tuple-element.126.left.left_0, bf16[1024,256]{1,0:T(8,128)(2,1)S(1)} %get-tuple-element.113.w_q, bf16[1024,256]{1,0:T(8,128)(2,1)S(1)} %get-tuple-element.127.w_k, ...), custom_call_target="tpu_custom_call" | custom-call | flops 1433600000 | bytes 1000000 | tf_op jit(solution)/shard_map/attend/pallas_call | solution.py:536
  53.6 2.5 %collective-permute-done.8.x3.c3 = bf16[2048,256]{1,0:T(8,128)(2,1)S(1)} collective-permute-done((bf16[2048,256]{1,0:T(8,128)(2,1)S(1)}, bf16[2048,256]{1,0:T(8,128)(2,1)S(1)}, u32[]{:S(2)}, u32[]{:S(2)}) %collective-permute-start.8) | collective-permute-done | bytes 1048608 | tf_op jit(solution)/shard_map/ppermute | solution.py:874
  56.1 10.0 %norm_mlp.5 = (bf16[2,1024,1024]{2,1,0:T(8,128)(2,1)S(1)}, bf16[2,1024,1024]{2,1,0:T(8,128)(2,1)S(1)}, f32[1024,128]{1,0:T(8,128)S(1)}, f32[32,1024]{1,0:T(8,128)S(1)}, f32[32,256]{1,0:T(8,128)S(1)}) custom-call(s32[4]{0:T(128)S(1)} %pad_add_fusion.place, bf16[2048,256]{1,0:T(8,128)(2,1)S(1)} %copy-done, bf16[2048,256]{1,0:T(8,128)(2,1)S(1)} %copy-done.4, ...), custom_call_target="tpu_custom_call" | custom-call | flops 1024000000 | bytes 1000000 | tf_op jit(solution)/shard_map/norm_mlp/pallas_call | solution.py:399
  66.1 7.4 %weight_mlp.2 = (bf16[4,128,1024]{2,1,0:T(8,128)(2,1)}, bf16[4,128,1024]{2,1,0:T(8,128)(2,1)}) custom-call(s32[4]{0:T(128)S(1)} %pad_add_fusion.place, f32[1]{0:T(128)} %mul_shard_map.6.scale, bf16[2,1024,1024]{2,1,0:T(8,128)(2,1)S(1)} %get-tuple-element.126.left.left_0, bf16[2,1024,1024]{2,1,0:T(8,128)(2,1)S(1)} %get-tuple-element.137.left_1.left, ...), custom_call_target="tpu_custom_call" | custom-call | flops 665600000 | bytes 1000000 | tf_op jit(solution)/shard_map/weight_mlp/pallas_call | solution.py:626
  73.6 7.6 %weight_mlp.3 = (bf16[2,2,128,1024]{3,2,1,0:T(8,128)(2,1)}, bf16[2,2,128,1024]{3,2,1,0:T(8,128)(2,1)}) custom-call(s32[4]{0:T(128)S(1)} %pad_add_fusion.place, f32[1]{0:T(128)} %mul_shard_map.6.scale, bf16[2,1024,1024]{2,1,0:T(8,128)(2,1)S(1)} %get-tuple-element.126.left.left_0, bf16[2,1024,1024]{2,1,0:T(8,128)(2,1)S(1)} %get-tuple-element.137.left_1.left, ...), custom_call_target="tpu_custom_call" | custom-call | flops 665600000 | bytes 1000000 | tf_op jit(solution)/shard_map/weight_mlp/pallas_call | solution.py:626
  81.2 2.1 %collective-permute-start.10 = (bf16[2,2,128,1024]{3,2,1,0:T(8,128)(2,1)}, bf16[2,2,128,1024]{3,2,1,0:T(8,128)(2,1)S(1)}, u32[]{:S(2)}, u32[]{:S(2)}) collective-permute-start(bf16[2,2,128,1024]{3,2,1,0:T(8,128)(2,1)} %get-tuple-element.148), channel_id=1, source_target_pairs={{0,8},{4,12},{8,0},{12,4},{16,24},{20,28},{24,16},{28,20},{1,9},{5... | collective-permute-start | bytes 3145736 | tf_op jit(solution)/shard_map/ppermute | solution.py:874
  83.3 1.5 collective-permute-start.9
  84.8 10.6 %branch_parts.2 = (bf16[2,2,1024,256]{3,2,1,0:T(8,128)(2,1)}, bf16[2,1024,256]{2,1,0:T(8,128)(2,1)}, bf16[1024,256]{1,0:T(8,128)(2,1)}, bf16[1024,256]{1,0:T(8,1...) custom-call(s32[4]{0:T(128)S(1)} %pad_add_fusion.place, ...), custom_call_target="tpu_custom_call" | custom-call | flops 1024000000 | bytes 1000000 | tf_op jit(solution)/shard_map/branch_parts/pallas_call | solution.py:718
  95.9 13.9 %attend.3 = (bf16[1024,256]{1,0:T(8,128)(2,1)S(1)}, bf16[1024,768]{1,0:T(8,128)(2,1)S(1)}) custom-call(s32[4]{0:T(128)S(1)} %pad_add_fusion.place, bf16[2,1024,1024]{2,1,0:T(8,128)(2,1)S(1)} %get-tuple-element.137.left_1.left, bf16[1024,256]{1,0:T(8,128)(2,1)S(1)} %get-tuple-element.113.w_q, bf16[1024,256]{1,0:T(8,128)(2,1)S(1)} %get-tuple-element.127.w_k, ...), custom_call_target="tpu_custom_call" | custom-call | flops 1433600000 | bytes 1000000 | tf_op jit(solution)/shard_map/attend/pallas_call | solution.py:536
  109.9 0.7 copy-done.22
  111.5 5.0 %combine.1 = (bf16[272,1024]{1,0:T(8,128)(2,1)}, bf16[2,128,1024]{2,1,0:T(8,128)(2,1)}, bf16[2,128,1024]{2,1,0:T(8,128)(2,1)}, bf16[2,128,1024]{2,1,0:T(8,128)(2,1)}, bf16[2,1024,256]{2,1,0:T(8,128)(2,1)}) custom-call(f32[1]{0:T(128)S(6)} %add.72.count, bf16[4,128,1024]{2,1,0:T(8,128)(2,1)} %get-tuple-element.140.keep_in, bf16[4,128,1024]{2,1,0:T(8,128)(2,1)} %copy-done.20, ...), custom_call_target="tpu_custom_call" | custom-call | flops 300000000 | bytes 1000000 | tf_op jit(solution)/shard_map/combine/pallas_call | solution.py:759
  116.4 1.6 collective-permute-start.16
  118.4 2.6 %collective-permute-start.15 = (bf16[2,128,1024]{2,1,0:T(8,128)(2,1)}, bf16[2,128,1024]{2,1,0:T(8,128)(2,1)S(1)}, u32[]{:S(2)}, u32[]{:S(2)}) collective-permute-start(bf16[2,128,1024]{2,1,0:T(8,128)(2,1)} %get-tuple-element.168), channel_id=1, source_target_pairs={{0,16},{4,20},{8,24},{12,28},{16,0},{20,4},{24,8},{28,12},{1,17},{... | collective-permute-start | bytes 1572872 | tf_op jit(solution)/shard_map/ppermute | solution.py:874
  121.0 7.8 %weight_att.1 = (bf16[4,128,1024]{2,1,0:T(8,128)(2,1)}, bf16[4,128,1024]{2,1,0:T(8,128)(2,1)}) custom-call(s32[4]{0:T(128)S(1)} %pad_add_fusion.place, f32[1]{0:T(128)} %mul_shard_map.6.scale, bf16[2,1024,1024]{2,1,0:T(8,128)(2,1)S(1)} %get-tuple-element.126.left.left_0, bf16[2,1024,1024]{2,1,0:T(8,128)(2,1)S(1)} %get-tuple-element.137.left_1.left, ...), custom_call_target="tpu_custom_call" | custom-call | flops 716800000 | bytes 1000000 | tf_op jit(solution)/shard_map/weight_att/pallas_call | solution.py:650
  129.4 10.8 %branch_parts.3 = (bf16[2,2,1024,256]{3,2,1,0:T(8,128)(2,1)}, bf16[2,1024,256]{2,1,0:T(8,128)(2,1)}, bf16[1024,256]{1,0:T(8,128)(2,1)}, bf16[1024,256]{1,0:T(8,1...) custom-call(s32[4]{0:T(128)S(1)} %pad_add_fusion.place, ...), custom_call_target="tpu_custom_call" | custom-call | flops 1024000000 | bytes 1000000 | tf_op jit(solution)/shard_map/branch_parts/pallas_call | solution.py:718
  140.2 2.0 %collective-permute-done.15 = bf16[2,128,1024]{2,1,0:T(8,128)(2,1)S(1)} collective-permute-done((bf16[2,128,1024]{2,1,0:T(8,128)(2,1)}, bf16[2,128,1024]{2,1,0:T(8,128)(2,1)S(1)}, u32[]{:S(2)}, u32[]{:S(2)}) %collective-permute-start.15) | collective-permute-done | bytes 524320 | tf_op jit(solution)/shard_map/ppermute | solution.py:874
  142.2 1.9 collective-permute-done.14.z_in
  145.1 1.5 collective-permute-start.17
  147.9 5.8 %collective-permute-done.19 = bf16[4,128,1024]{2,1,0:T(8,128)(2,1)S(1)} collective-permute-done((bf16[4,128,1024]{2,1,0:T(8,128)(2,1)}, bf16[4,128,1024]{2,1,0:T(8,128)(2,1)S(1)}, u32[]{:S(2)}, u32[]{:S(2)}) %collective-permute-start.19) | collective-permute-done | bytes 1048608 | tf_op jit(solution)/shard_map/ppermute | solution.py:874
  155.0 1.6 collective-permute-start.23
  156.6 1.1 collective-permute-done.22
  157.7 1.6 collective-permute-start.24
  159.3 2.5 %collective-permute-done.17.far_in = bf16[144,1024]{1,0:T(8,128)(2,1)S(1)} collective-permute-done((bf16[144,1024]{1,0:T(8,128)(2,1)S(1)}, bf16[144,1024]{1,0:T(8,128)(2,1)S(1)}, u32[]{:S(2)}, u32[]{:S(2)}) %collective-permute-start.17) | collective-permute-done | bytes 294944 | tf_op jit(solution)/shard_map/ppermute | solution.py:874
  161.9 11.0 %collective-permute-done.26 = f32[2,2048]{1,0:T(2,128)S(1)} collective-permute-done((f32[2,2048]{1,0:T(2,128)S(1)}, f32[2,2048]{1,0:T(2,128)S(1)}, u32[]{:S(2)}, u32[]{:S(2)}) %collective-permute-start.26) | collective-permute-done | bytes 16416 | tf_op jit(solution)/shard_map/ppermute | solution.py:874
  173.7 1.5 collective-permute-start.28
  175.2 1.5 collective-permute-start.29
  176.6 3.7 %finish_rows.2 = (bf16[2048,256]{1,0:T(8,128)(2,1)}, f32[2048,256]{1,0:T(8,128)}) custom-call(s32[4]{0:T(128)S(1)} %pad_add_fusion.place, f32[1]{0:T(128)S(6)} %mul.27.scale, bf16[2,2,1024,256]{3,2,1,0:T(8,128)(2,1)} %get-tuple-element.155.kept.keep, bf16[2,1024,256]{2,1,0:T(8,128)(2,1)} %copy-done.17, bf16[2,1024,256]{2,1,0:T(8,128)(2,1)} %copy-done.18, ...), custom_call_target="tpu_custom_call" | custom-call | flops 307200000 | bytes 1000000 | tf_op jit(solution)/shard_map/finish_rows/pallas_call | solution.py:830
  180.4 3.7 %finish_rows.3 = (bf16[2048,256]{1,0:T(8,128)(2,1)}, f32[2048,256]{1,0:T(8,128)}) custom-call(s32[4]{0:T(128)S(1)} %pad_add_fusion.place, f32[1]{0:T(128)S(6)} %mul.27.scale, bf16[2,2,1024,256]{3,2,1,0:T(8,128)(2,1)} %get-tuple-element.181.keep, bf16[2,1024,256]{2,1,0:T(8,128)(2,1)} %collective-permute-done.27.near, ...), custom_call_target="tpu_custom_call", output_to_operand_aliasing={{0}: (11, {}), {1}: (12, {})} | custom-call | flops 307200000 | bytes 1000000 | tf_op jit(solution)/shard_map/finish_rows/pallas_call | solution.py:830
  184.1 1.0 collective-permute-start.31
  186.3 3.9 %collective-permute-done.29.far_a = bf16[128,1024]{1,0:T(8,128)(2,1)S(1)} collective-permute-done((bf16[128,1024]{1,0:T(8,128)(2,1)S(1)}, bf16[128,1024]{1,0:T(8,128)(2,1)S(1)}, u32[]{:S(2)}, u32[]{:S(2)}) %collective-permute-start.29) | collective-permute-done | bytes 262176 | tf_op jit(solution)/shard_map/ppermute | solution.py:874
  190.8 0.6 dynamic-slice_divide_fusion
  191.4 1.3 finish_weights.1
  (121 shorter events, 9.8 us)
Async XLA Ops:
  0.6 6.1 %copy-start = (bf16[2048,256]{1,0:T(8,128)(2,1)S(1)}, bf16[2048,256]{1,0:T(8,128)(2,1)}, u32[]{:S(2)}) copy-start(bf16[2048,256]{1,0:T(8,128)(2,1)} %x_ref.3) | copy-start | bytes 3145732
  0.7 6.1 %copy-start.1 = (bf16[2048,256]{1,0:T(8,128)(2,1)S(1)}, bf16[2048,256]{1,0:T(8,128)(2,1)}, u32[]{:S(2)}) copy-start(bf16[2048,256]{1,0:T(8,128)(2,1)} %cot.3) | copy-start | bytes 3145732
  3.8 16.0 %collective-permute-start.1 = (bf16[1024,256]{1,0:T(8,128)(2,1)}, bf16[1024,256]{1,0:T(8,128)(2,1)}, u32[]{:S(2)}, u32[]{:S(2)}) collective-permute-start(bf16[1024,256]{1,0:T(8,128)(2,1)} %pad_maximum_fusion.1), channel_id=1, source_target_pairs={{0,2},{1,3},{2,0},{3,1},{4,6},{5,7},{6,4},{7,5},{8,10},{9,11},{10,... | collective-permute-start | bytes 1572872 | tf_op jit(solution)/shard_map/ppermute | solution.py:874
  6.8 15.3 %collective-permute-start = (bf16[2048,256]{1,0:T(8,128)(2,1)S(1)}, bf16[2048,256]{1,0:T(8,128)(2,1)S(1)}, u32[]{:S(2)}, u32[]{:S(2)}) collective-permute-start(bf16[2048,256]{1,0:T(8,128)(2,1)S(1)} %copy-done), channel_id=1, source_target_pairs={{0,1},{1,0},{2,3},{3,2},{4,5},{5,4},{6,7},{7,6},{8,9},{9,8},{10,11... | collective-permute-start | bytes 3145736 | tf_op jit(solution)/shard_map/ppermute | solution.py:874
  6.8 15.3 %collective-permute-start.4 = (bf16[2048,256]{1,0:T(8,128)(2,1)S(1)}, bf16[2048,256]{1,0:T(8,128)(2,1)}, u32[]{:S(2)}, u32[]{:S(2)}) collective-permute-start(bf16[2048,256]{1,0:T(8,128)(2,1)S(1)} %copy-done.1), channel_id=1, source_target_pairs={{0,1},{1,0},{2,3},{3,2},{4,5},{5,4},{6,7},{7,6},{8,9},{9,8},{10,11... | collective-permute-start | bytes 3145736 | tf_op jit(solution)/shard_map/ppermute | solution.py:874
  7.9 9.7 %collective-permute-start.2 = (f32[1]{0:T(128)}, f32[1]{0:T(128)}, u32[]{:S(2)}, u32[]{:S(2)}) collective-permute-start(f32[1]{0:T(128)} %mul_shard_map.6.scale), channel_id=1, source_target_pairs={{0,4},{4,0},{8,12},{12,8},{16,20},{20,16},{24,28},{28,24},{1,5},{5... | collective-permute-start | bytes 20 | tf_op jit(solution)/shard_map/ppermute | solution.py:874
  11.6 19.4 %collective-permute-start.5 = (bf16[1024,256]{1,0:T(8,128)(2,1)}, bf16[1024,256]{1,0:T(8,128)(2,1)}, u32[]{:S(2)}, u32[]{:S(2)}) collective-permute-start(bf16[1024,256]{1,0:T(8,128)(2,1)} %pad_maximum_fusion.2), channel_id=1, source_target_pairs={{0,2},{1,3},{2,0},{3,1},{4,6},{5,7},{6,4},{7,5},{8,10},{9,11},{10,... | collective-permute-start | bytes 1572872 | tf_op jit(solution)/shard_map/ppermute | solution.py:874
  13.8 6.0 %copy-start.13 = (bf16[1024,256]{1,0:T(8,128)(2,1)S(1)}, bf16[1024,256]{1,0:T(8,128)(2,1)}, u32[]{:S(2)}) copy-start(bf16[1024,256]{1,0:T(8,128)(2,1)} %slice.115) | copy-start | bytes 1572868
  13.8 6.0 %copy-start.14 = (bf16[1024,256]{1,0:T(8,128)(2,1)S(1)}, bf16[1024,256]{1,0:T(8,128)(2,1)}, u32[]{:S(2)}) copy-start(bf16[1024,256]{1,0:T(8,128)(2,1)} %slice.116) | copy-start | bytes 1572868
  19.8 2.2 %collective-permute-start.3 = (bf16[1024,256]{1,0:T(8,128)(2,1)}, bf16[1024,256]{1,0:T(8,128)(2,1)S(1)}, u32[]{:S(2)}, u32[]{:S(2)}) collective-permute-start(bf16[1024,256]{1,0:T(8,128)(2,1)} %collective-permute-done.1.x2.c2), channel_id=1, source_target_pairs={{0,1},{1,0},{2,3},{3,2},{4,5},{5,4},{6,7},{7,6},{8,9},{9,8},{10,11... | collective-permute-start | bytes 1572872 | tf_op jit(solution)/shard_map/ppermute | solution.py:874
  19.9 33.5 %collective-permute-start.7 = (bf16[2048,256]{1,0:T(8,128)(2,1)S(1)}, bf16[2048,256]{1,0:T(8,128)(2,1)S(1)}, u32[]{:S(2)}, u32[]{:S(2)}) collective-permute-start(bf16[2048,256]{1,0:T(8,128)(2,1)S(1)} %pad_maximum_fusion), channel_id=1, source_target_pairs={{0,2},{1,3},{2,0},{3,1},{4,6},{5,7},{6,4},{7,5},{8,10},{9,11},{10,... | collective-permute-start | bytes 3145736 | tf_op jit(solution)/shard_map/ppermute | solution.py:874
  22.0 11.1 %copy-start.3 = (bf16[2048,256]{1,0:T(8,128)(2,1)}, bf16[2048,256]{1,0:T(8,128)(2,1)S(1)}, u32[]{:S(2)}) copy-start(bf16[2048,256]{1,0:T(8,128)(2,1)S(1)} %collective-permute-done.x1) | copy-start | bytes 3145732
  31.0 2.1 %collective-permute-start.6 = (bf16[1024,256]{1,0:T(8,128)(2,1)}, bf16[1024,256]{1,0:T(8,128)(2,1)S(1)}, u32[]{:S(2)}, u32[]{:S(2)}) collective-permute-start(bf16[1024,256]{1,0:T(8,128)(2,1)} %collective-permute-done.5.x2.c2), channel_id=1, source_target_pairs={{0,1},{1,0},{2,3},{3,2},{4,5},{5,4},{6,7},{7,6},{8,9},{9,8},{10,11... | collective-permute-start | bytes 1572872 | tf_op jit(solution)/shard_map/ppermute | solution.py:874
  39.5 16.6 %copy-start.2 = (bf16[2048,256]{1,0:T(8,128)(2,1)S(1)}, bf16[2048,256]{1,0:T(8,128)(2,1)}, u32[]{:S(2)}) copy-start(bf16[2048,256]{1,0:T(8,128)(2,1)} %cot.3) | copy-start | bytes 3145732
  39.5 16.6 %copy-start.4 = (bf16[2048,256]{1,0:T(8,128)(2,1)S(1)}, bf16[2048,256]{1,0:T(8,128)(2,1)}, u32[]{:S(2)}) copy-start(bf16[2048,256]{1,0:T(8,128)(2,1)} %copy-done.3) | copy-start | bytes 3145732
  53.4 2.7 %collective-permute-start.8 = (bf16[2048,256]{1,0:T(8,128)(2,1)S(1)}, bf16[2048,256]{1,0:T(8,128)(2,1)S(1)}, u32[]{:S(2)}, u32[]{:S(2)}) collective-permute-start(bf16[2048,256]{1,0:T(8,128)(2,1)S(1)} %collective-permute-done.7.x2.c2), channel_id=1, source_target_pairs={{0,1},{1,0},{2,3},{3,2},{4,5},{5,4},{6,7},{7,6},{8,9},{9,8},{10,11... | collective-permute-start | bytes 3145736 | tf_op jit(solution)/shard_map/ppermute | solution.py:874
  66.1 7.4 %copy-start.6 = (f32[1024,128]{1,0:T(8,128)}, f32[1024,128]{1,0:T(8,128)S(1)}, u32[]{:S(2)}) copy-start(f32[1024,128]{1,0:T(8,128)S(1)} %get-tuple-element.201.stats) | copy-start | bytes 1572868
  73.6 9.7 %copy-start.25 = (bf16[4,128,1024]{2,1,0:T(8,128)(2,1)S(1)}, bf16[4,128,1024]{2,1,0:T(8,128)(2,1)}, u32[]{:S(2)}) copy-start(bf16[4,128,1024]{2,1,0:T(8,128)(2,1)} %get-tuple-element.147) | copy-start | bytes 3145732
  81.2 28.6 %collective-permute-start.10 = (bf16[2,2,128,1024]{3,2,1,0:T(8,128)(2,1)}, bf16[2,2,128,1024]{3,2,1,0:T(8,128)(2,1)S(1)}, u32[]{:S(2)}, u32[]{:S(2)}) collective-permute-start(bf16[2,2,128,1024]{3,2,1,0:T(8,128)(2,1)} %get-tuple-element.148), channel_id=1, source_target_pairs={{0,8},{4,12},{8,0},{12,4},{16,24},{20,28},{24,16},{28,20},{1,9},{5... | collective-permute-start | bytes 3145736 | tf_op jit(solution)/shard_map/ppermute | solution.py:874
  83.3 26.5 %collective-permute-start.9 = (bf16[4,128,1024]{2,1,0:T(8,128)(2,1)S(1)}, bf16[4,128,1024]{2,1,0:T(8,128)(2,1)S(1)}, u32[]{:S(2)}, u32[]{:S(2)}) collective-permute-start(bf16[4,128,1024]{2,1,0:T(8,128)(2,1)S(1)} %copy-done.25), channel_id=1, source_target_pairs={{0,4},{4,0},{8,12},{12,8},{16,20},{20,16},{24,28},{28,24},{1,5},{5... | collective-permute-start | bytes 3145736 | tf_op jit(solution)/shard_map/ppermute | solution.py:874
  95.4 14.4 %collective-permute-start.11 = (bf16[1024,256]{1,0:T(8,128)(2,1)}, bf16[1024,256]{1,0:T(8,128)(2,1)S(1)}, u32[]{:S(2)}, u32[]{:S(2)}) collective-permute-start(bf16[1024,256]{1,0:T(8,128)(2,1)} %get-tuple-element.149), channel_id=1, source_target_pairs={{0,1},{1,0},{2,3},{3,2},{4,5},{5,4},{6,7},{7,6},{8,9},{9,8},{10,11... | collective-permute-start | bytes 1572872 | tf_op jit(solution)/shard_map/ppermute | solution.py:874
  95.4 14.4 %collective-permute-start.12 = (bf16[1024,256]{1,0:T(8,128)(2,1)}, bf16[1024,256]{1,0:T(8,128)(2,1)S(1)}, u32[]{:S(2)}, u32[]{:S(2)}) collective-permute-start(bf16[1024,256]{1,0:T(8,128)(2,1)} %get-tuple-element.150), channel_id=1, source_target_pairs={{0,1},{1,0},{2,3},{3,2},{4,5},{5,4},{6,7},{7,6},{8,9},{9,8},{10,11... | collective-permute-start | bytes 1572872 | tf_op jit(solution)/shard_map/ppermute | solution.py:874
  116.4 13.0 %collective-permute-start.13 = (bf16[2,1024,256]{2,1,0:T(8,128)(2,1)S(1)}, bf16[2,1024,256]{2,1,0:T(8,128)(2,1)S(1)}, u32[]{:S(2)}, u32[]{:S(2)}) collective-permute-start(bf16[2,1024,256]{2,1,0:T(8,128)(2,1)S(1)} %copy-done.24), channel_id=1, source_target_pairs={{0,1},{1,0},{2,3},{3,2},{4,5},{5,4},{6,7},{7,6},{8,9},{9,8},{10,11... | collective-permute-start | bytes 3145736 | tf_op jit(solution)/shard_map/ppermute | solution.py:874
  116.4 27.7 %collective-permute-start.16 = (bf16[2,1024,256]{2,1,0:T(8,128)(2,1)}, bf16[2,1024,256]{2,1,0:T(8,128)(2,1)S(1)}, u32[]{:S(2)}, u32[]{:S(2)}) collective-permute-start(bf16[2,1024,256]{2,1,0:T(8,128)(2,1)} %get-tuple-element.160), channel_id=1, source_target_pairs={{0,2},{1,3},{2,0},{3,1},{4,6},{5,7},{6,4},{7,5},{8,10},{9,11},{10,... | collective-permute-start | bytes 3145736 | tf_op jit(solution)/shard_map/ppermute | solution.py:874
  118.0 26.1 %collective-permute-start.14 = (bf16[272,1024]{1,0:T(8,128)(2,1)}, bf16[272,1024]{1,0:T(8,128)(2,1)S(1)}, u32[]{:S(2)}, u32[]{:S(2)}) collective-permute-start(bf16[272,1024]{1,0:T(8,128)(2,1)} %get-tuple-element.167), channel_id=1, source_target_pairs={{0,8},{4,12},{8,0},{12,4},{16,24},{20,28},{24,16},{28,20},{1,9},{5... | collective-permute-start | bytes 1671176 | tf_op jit(solution)/shard_map/ppermute | solution.py:874
  118.4 23.8 %collective-permute-start.15 = (bf16[2,128,1024]{2,1,0:T(8,128)(2,1)}, bf16[2,128,1024]{2,1,0:T(8,128)(2,1)S(1)}, u32[]{:S(2)}, u32[]{:S(2)}) collective-permute-start(bf16[2,128,1024]{2,1,0:T(8,128)(2,1)} %get-tuple-element.168), channel_id=1, source_target_pairs={{0,16},{4,20},{8,24},{12,28},{16,0},{20,4},{24,8},{28,12},{1,17},{... | collective-permute-start | bytes 1572872 | tf_op jit(solution)/shard_map/ppermute | solution.py:874
  128.8 24.9 %collective-permute-start.19 = (bf16[4,128,1024]{2,1,0:T(8,128)(2,1)}, bf16[4,128,1024]{2,1,0:T(8,128)(2,1)S(1)}, u32[]{:S(2)}, u32[]{:S(2)}) collective-permute-start(bf16[4,128,1024]{2,1,0:T(8,128)(2,1)} %get-tuple-element.180), channel_id=1, source_target_pairs={{0,4},{4,0},{8,12},{12,8},{16,20},{20,16},{24,28},{28,24},{1,5},{5... | collective-permute-start | bytes 3145736 | tf_op jit(solution)/shard_map/ppermute | solution.py:874
  129.4 10.8 %copy-start.17 = (bf16[2,1024,256]{2,1,0:T(8,128)(2,1)}, bf16[2,1024,256]{2,1,0:T(8,128)(2,1)S(1)}, u32[]{:S(2)}) copy-start(bf16[2,1024,256]{2,1,0:T(8,128)(2,1)S(1)} %collective-permute-done.13.near) | copy-start | bytes 3145732
  129.4 15.5 %copy-start.21 = (bf16[2,128,1024]{2,1,0:T(8,128)(2,1)S(1)}, bf16[2,128,1024]{2,1,0:T(8,128)(2,1)}, u32[]{:S(2)}) copy-start(bf16[2,128,1024]{2,1,0:T(8,128)(2,1)} %get-tuple-element.159) | copy-start | bytes 1572868
  129.4 15.6 %copy-start.7 = (bf16[2,128,1024]{2,1,0:T(8,128)(2,1)S(1)}, bf16[2,128,1024]{2,1,0:T(8,128)(2,1)}, u32[]{:S(2)}) copy-start(bf16[2,128,1024]{2,1,0:T(8,128)(2,1)} %get-tuple-element.158.low) | copy-start | bytes 1572868
  140.2 6.9 %copy-start.12 = (bf16[2,2,1024,256]{3,2,1,0:T(8,128)(2,1)S(1)}, bf16[2,2,1024,256]{3,2,1,0:T(8,128)(2,1)}, u32[]{:S(2)}) copy-start(bf16[2,2,1024,256]{3,2,1,0:T(8,128)(2,1)} %get-tuple-element.181.keep) | copy-start | bytes 6291460
  144.1 2.5 %collective-permute-start.20 = (bf16[1024,256]{1,0:T(8,128)(2,1)}, bf16[1024,256]{1,0:T(8,128)(2,1)S(1)}, u32[]{:S(2)}, u32[]{:S(2)}) collective-permute-start(bf16[1024,256]{1,0:T(8,128)(2,1)} %get-tuple-element.182), channel_id=1, source_target_pairs={{0,1},{1,0},{2,3},{3,2},{4,5},{5,4},{6,7},{7,6},{8,9},{9,8},{10,11... | collective-permute-start | bytes 1572872 | tf_op jit(solution)/shard_map/ppermute | solution.py:874
  144.2 2.9 %collective-permute-start.21 = (bf16[1024,256]{1,0:T(8,128)(2,1)}, bf16[1024,256]{1,0:T(8,128)(2,1)S(1)}, u32[]{:S(2)}, u32[]{:S(2)}) collective-permute-start(bf16[1024,256]{1,0:T(8,128)(2,1)} %get-tuple-element.186), channel_id=1, source_target_pairs={{0,1},{1,0},{2,3},{3,2},{4,5},{5,4},{6,7},{7,6},{8,9},{9,8},{10,11... | collective-permute-start | bytes 1572872 | tf_op jit(solution)/shard_map/ppermute | solution.py:874
  144.7 1.9 collective-permute-start.18
  145.0 8.7 %copy-start.16 = (bf16[4,128,1024]{2,1,0:T(8,128)(2,1)S(1)}, bf16[4,128,1024]{2,1,0:T(8,128)(2,1)}, u32[]{:S(2)}) copy-start(bf16[4,128,1024]{2,1,0:T(8,128)(2,1)} %get-tuple-element.163) | copy-start | bytes 3145732
  145.1 16.8 %collective-permute-start.17 = (bf16[144,1024]{1,0:T(8,128)(2,1)S(1)}, bf16[144,1024]{1,0:T(8,128)(2,1)S(1)}, u32[]{:S(2)}, u32[]{:S(2)}) collective-permute-start(bf16[144,1024]{1,0:T(8,128)(2,1)S(1)} %get-tuple-element.173), channel_id=1, source_target_pairs={{0,16},{4,20},{8,24},{12,28},{16,0},{20,4},{24,8},{28,12},{1,17},{... | collective-permute-start | bytes 884744 | tf_op jit(solution)/shard_map/ppermute | solution.py:874
  147.3 29.4 %copy-start.11 = (f32[256]{0:T(256)S(1)}, f32[256]{0:T(256)}, u32[]{:S(2)}) copy-start(f32[256]{0:T(256)} %param.23) | copy-start | bytes 3076
  147.3 25.6 %collective-permute-start.25 = (bf16[2,1024,256]{2,1,0:T(8,128)(2,1)S(1)}, bf16[2,1024,256]{2,1,0:T(8,128)(2,1)S(1)}, u32[]{:S(2)}, u32[]{:S(2)}) collective-permute-start(bf16[2,1024,256]{2,1,0:T(8,128)(2,1)S(1)} %maximum_add_fusion), channel_id=1, source_target_pairs={{0,2},{1,3},{2,0},{3,1},{4,6},{5,7},{6,4},{7,5},{8,10},{9,11},{10,... | collective-permute-start | bytes 3145736 | tf_op jit(solution)/shard_map/ppermute | solution.py:874
  153.9 3.8 %collective-permute-start.22 = (f32[3328]{0:T(1024)S(1)}, f32[3328]{0:T(1024)S(1)}, u32[]{:S(2)}, u32[]{:S(2)}) collective-permute-start(f32[3328]{0:T(1024)S(1)} %maximum_multiply_fusion), channel_id=1, source_target_pairs={{0,4},{4,0},{8,12},{12,8},{16,20},{20,16},{24,28},{28,24},{1,5},{5... | collective-permute-start | bytes 39944 | tf_op jit(solution)/shard_map/ppermute | solution.py:874
  154.5 18.4 %collective-permute-start.26 = (f32[2,2048]{1,0:T(2,128)S(1)}, f32[2,2048]{1,0:T(2,128)S(1)}, u32[]{:S(2)}, u32[]{:S(2)}) collective-permute-start(f32[2,2048]{1,0:T(2,128)S(1)} %slice.150), channel_id=1, source_target_pairs={{0,2},{1,3},{2,0},{3,1},{4,6},{5,7},{6,4},{7,5},{8,10},{9,11},{10,... | collective-permute-start | bytes 49160 | tf_op jit(solution)/shard_map/ppermute | solution.py:874
  155.0 17.9 %collective-permute-start.23 = (bf16[2,128,1024]{2,1,0:T(8,128)(2,1)S(1)}, bf16[2,128,1024]{2,1,0:T(8,128)(2,1)S(1)}, u32[]{:S(2)}, u32[]{:S(2)}) collective-permute-start(bf16[2,128,1024]{2,1,0:T(8,128)(2,1)S(1)} %get-tuple-element.216), channel_id=1, source_target_pairs={{0,8},{4,12},{8,0},{12,4},{16,24},{20,28},{24,16},{28,20},{1,9},{5... | collective-permute-start | bytes 1572872 | tf_op jit(solution)/shard_map/ppermute | solution.py:874
  157.7 15.2 %collective-permute-start.24 = (f32[3328]{0:T(1024)S(1)}, f32[3328]{0:T(1024)S(1)}, u32[]{:S(2)}, u32[]{:S(2)}) collective-permute-start(f32[3328]{0:T(1024)S(1)} %fusion.4), channel_id=1, source_target_pairs={{0,8},{4,12},{8,0},{12,4},{16,24},{20,28},{24,16},{28,20},{1,9},{5... | collective-permute-start | bytes 39944 | tf_op jit(solution)/shard_map/ppermute | solution.py:874
  172.9 7.5 %copy-start.15 = (bf16[2,1024,256]{2,1,0:T(8,128)(2,1)}, bf16[2,1024,256]{2,1,0:T(8,128)(2,1)S(1)}, u32[]{:S(2)}) copy-start(bf16[2,1024,256]{2,1,0:T(8,128)(2,1)S(1)} %collective-permute-done.25.far) | copy-start | bytes 3145732
  173.0 7.4 %collective-permute-start.27 = (bf16[2,1024,256]{2,1,0:T(8,128)(2,1)}, bf16[2,1024,256]{2,1,0:T(8,128)(2,1)}, u32[]{:S(2)}, u32[]{:S(2)}) collective-permute-start(bf16[2,1024,256]{2,1,0:T(8,128)(2,1)} %get-tuple-element.199), channel_id=1, source_target_pairs={{0,1},{1,0},{2,3},{3,2},{4,5},{5,4},{6,7},{7,6},{8,9},{9,8},{10,11... | collective-permute-start | bytes 3145736 | tf_op jit(solution)/shard_map/ppermute | solution.py:874
  173.2 13.1 %collective-permute-start.30 = (bf16[128,1024]{1,0:T(8,128)(2,1)S(1)}, bf16[128,1024]{1,0:T(8,128)(2,1)S(1)}, u32[]{:S(2)}, u32[]{:S(2)}) collective-permute-start(bf16[128,1024]{1,0:T(8,128)(2,1)S(1)} %get-tuple-element.218), channel_id=1, source_target_pairs={{0,4},{4,0},{8,12},{12,8},{16,20},{20,16},{24,28},{28,24},{1,5},{5... | collective-permute-start | bytes 786440 | tf_op jit(solution)/shard_map/ppermute | solution.py:874
  173.7 10.4 %collective-permute-start.28 = (f32[3328]{0:T(1024)S(1)}, f32[3328]{0:T(1024)S(1)}, u32[]{:S(2)}, u32[]{:S(2)}) collective-permute-start(f32[3328]{0:T(1024)S(1)} %add.86), channel_id=1, source_target_pairs={{0,16},{4,20},{8,24},{12,28},{16,0},{20,4},{24,8},{28,12},{1,17},{... | collective-permute-start | bytes 39944 | tf_op jit(solution)/shard_map/ppermute | solution.py:874
  175.2 15.0 %collective-permute-start.29 = (bf16[128,1024]{1,0:T(8,128)(2,1)S(1)}, bf16[128,1024]{1,0:T(8,128)(2,1)S(1)}, u32[]{:S(2)}, u32[]{:S(2)}) collective-permute-start(bf16[128,1024]{1,0:T(8,128)(2,1)S(1)} %get-tuple-element.220), channel_id=1, source_target_pairs={{0,16},{4,20},{8,24},{12,28},{16,0},{20,4},{24,8},{28,12},{1,17},{... | collective-permute-start | bytes 786440 | tf_op jit(solution)/shard_map/ppermute | solution.py:874
  184.1 6.0 %collective-permute-start.31 = (f32[2,1024]{1,0:T(2,128)S(1)}, f32[2,1024]{1,0:T(2,128)S(1)}, u32[]{:S(2)}, u32[]{:S(2)}) collective-permute-start(f32[2,1024]{1,0:T(2,128)S(1)} %reshape.64), channel_id=1, source_target_pairs={{0,2},{1,3},{2,0},{3,1},{4,6},{5,7},{6,4},{7,5},{8,10},{9,11},{10,... | collective-permute-start | bytes 24584 | tf_op jit(solution)/shard_map/ppermute | solution.py:874
  (10 other events, 27.0 us)

commit v2 on v1

--- a/solution.py
+++ b/solution.py
@@ -913,10 +913,12 @@
     own_gain = lax.dynamic_slice_in_dim(ln_gain, column * cols, cols, 0).reshape(1, cols)
     b_row = b_down.reshape(1, cols)
 
-    across = [swap(jnp.concatenate([inputs[low:high], cotangent[low:high]], axis=0), "narrow", 2) for low, high in cuts]
-    near = (inputs, swap(inputs, "narrow", 1), cotangent, swap(cotangent, "narrow", 1))
     count = (2.0 * jnp.sum(lengths.astype(F32))).reshape(1)
     count_x = count + swap(count, "wide", 1)
+    later = lax.optimization_barrier((inputs, cotangent, count_x))[:2]
+    sources = [(inputs, cotangent)] + [later] * (len(cuts) - 1)
+    across = [swap(jnp.concatenate([a[low:high], b[low:high]], axis=0), "narrow", 2) for (a, b), (low, high) in zip(sources, cuts)]
+    near = (inputs, swap(inputs, "narrow", 1), cotangent, swap(cotangent, "narrow", 1))
     weights = load_weights(place, w_qkv, w_out, w_in, w_down, *turn_tables(pad_len))
     up_in, up_down = weights[4:6]
 
@@ -986,7 +988,7 @@
     count_row = count_row[0] + unpack(zz_in[size:], units)[:128]
     per_count = groups / count_row[:1]
     scale = count * per_count
-    y_1, far_sums = lax.optimization_barrier((y_1, far_sums, scale))[:2]
+    y_1, far_sums, x_d = lax.optimization_barrier((y_1, far_sums, x_d, scale))[:3]
     sums = sums[:, :rows_all] + far_sums
     small = small + after(z_small, sums)
     z_a = after(z_a, small)
@@ -999,7 +1001,7 @@
     small = per_count * (small + after(zz_small, ends[0]))
     columns = small[: 2 * width].reshape(2, width)
     far_columns = swap(columns, "narrow", 2)
-    zz_a, x_d, far_columns = lax.optimization_barrier((zz_a, x_d, far_columns, ends[0]))[:3]
+    zz_a, far_columns = lax.optimization_barrier((zz_a, far_columns, ends[0]))[:2]
     columns = lax.dynamic_slice_in_dim(columns + far_columns, column * cols, cols, 1)
     g_in, g_down, g_qkv, g_out = finish_weights(per_count, low_in, zz_in, low_down, x_d, low_a, zz_a)
     return (

time: 193 us -> 191 us (0.990)
  waiting for transfers between devices: 38.1 us -> 41.4 us
  local copies, waits for them, and re-layouts: 8.25 us -> 5.58 us
    ppermute x32, waiting for transfers between devices: 38.1 us -> 41.4 us  [swap(): return lax.ppermute(value, axis, [(i, i ^ bit) for i in range(size)])]
    slice x4 -> x6, local copies, waits for them, and re-layouts: 3.93 us -> 2.05 us  [the longest x3 1.02 us: on_device_fast(): b[low:high]]
  transfers between devices with their start and end apart: 32 -> 32, of which waited for: 12 -> 14; matrix products, arithmetic and copies ran while one was open for 2% -> 1% of each run, Pallas kernels for 41% -> 42%
where the time goes in v2:
time: 191 us; the launch traced here: 190 us
  Pallas kernels  110 us (58%)
  waiting for transfers between devices  41.4 us (22%)
  starting transfers between devices  28.6 us (15%)
  local copies, waits for them, and re-layouts  5.58 us (3%)
  between operations  2.56 us (1%)
  other arithmetic  2.26 us (1%)
    ppermute x32, waiting for transfers between devices, swap(): return lax.ppermute(value, axis, [(i, i ^ bit) for i in range(size)])  41.4 us
    ppermute x32, starting transfers between devices, swap(): return lax.ppermute(value, axis, [(i, i ^ bit) for i in range(size)])  28.6 us
    pallas_call x2, Pallas kernels, attend(): pl.pallas_call(functools.partial(attend_kernel, tiles=tiles, tile=tile, p...  27.8 us
    pallas_call x2, Pallas kernels, branch_parts(): pl.pallas_call(branch_kernel, grid_spec=pltpu.PrefetchScalarGridSpec(num_...  21.5 us
    pallas_call x3, Pallas kernels, norm_mlp(): pl.pallas_call(functools.partial(norm_mlp_kernel, first_row=first_row), g...  20.4 us
    pallas_call x2, Pallas kernels, weight_mlp(): pl.pallas_call(kernel, grid_spec=pltpu.PrefetchScalarGridSpec(num_scalar_...  14.9 us
    pallas_call x1, Pallas kernels, weight_att(): pl.pallas_call(weight_att_kernel, grid_spec=pltpu.PrefetchScalarGridSpec(...  7.82 us
    pallas_call x2, Pallas kernels, finish_rows(): pl.pallas_call(functools.partial(final_kernel, first_row=first_row), grid...  7.45 us
  transfers between devices with their start and end apart: 32, of which 14 were waited for; matrix products, arithmetic and copies ran while one was open for 1% of the time, Pallas kernels for 42%

profile of v2, /device:TPU:0, one launch (start us, length us, event | category | flops | bytes accessed | tf_op | source)
XLA Modules:
  0.0 190.5 jit_solution(5989149260711955449)
XLA Ops:
  0.6 1.0 slice.111
  1.6 1.0 slice.112
  2.6 0.8 pad_maximum_fusion.1
  3.4 3.0 %collective-permute-start.1 = (bf16[1024,256]{1,0:T(8,128)(2,1)}, bf16[1024,256]{1,0:T(8,128)(2,1)}, u32[]{:S(2)}, u32[]{:S(2)}) collective-permute-start(bf16[1024,256]{1,0:T(8,128)(2,1)} %pad_maximum_fusion.1), channel_id=1, source_target_pairs={{0,2},{1,3},{2,0},{3,1},{4,6},{5,7},{6,4},{7,5},{8,10},{9,11},{10,... | collective-permute-start | bytes 1572872 | tf_op jit(solution)/shard_map/ppermute | solution.py:874
  7.5 2.9 %collective-permute-start.2 = (f32[1]{0:T(128)}, f32[1]{0:T(128)}, u32[]{:S(2)}, u32[]{:S(2)}) collective-permute-start(f32[1]{0:T(128)} %mul_shard_map.6.scale), channel_id=1, source_target_pairs={{0,4},{4,0},{8,12},{12,8},{16,20},{20,16},{24,28},{28,24},{1,5},{5... | collective-permute-start | bytes 20 | tf_op jit(solution)/shard_map/ppermute | solution.py:874
  10.5 3.8 %load_weights.1 = (bf16[1024,256]{1,0:T(8,128)(2,1)S(1)}, bf16[1024,256]{1,0:T(8,128)(2,1)S(1)}, bf16[1024,256]{1,0:T(8,128)(2,1)S(1)}, bf16[256,1024]{1,0:T(8,1...) custom-call(s32[4]{0:T(128)S(1)} %pad_add_fusion.place, ...), custom_call_target="tpu_custom_call" | custom-call | flops 300000000 | bytes 1000000 | tf_op jit(solution)/shard_map/load_weights/pallas_call | solution.py:320
  15.8 3.7 %collective-permute-done.1.x2.c2 = bf16[1024,256]{1,0:T(8,128)(2,1)} collective-permute-done((bf16[1024,256]{1,0:T(8,128)(2,1)}, bf16[1024,256]{1,0:T(8,128)(2,1)}, u32[]{:S(2)}, u32[]{:S(2)}) %collective-permute-start.1) | collective-permute-done | bytes 524320 | tf_op jit(solution)/shard_map/ppermute | solution.py:874
  19.5 2.1 %collective-permute-start.7 = (bf16[2048,256]{1,0:T(8,128)(2,1)S(1)}, bf16[2048,256]{1,0:T(8,128)(2,1)S(1)}, u32[]{:S(2)}, u32[]{:S(2)}) collective-permute-start(bf16[2048,256]{1,0:T(8,128)(2,1)S(1)} %pad_maximum_fusion), channel_id=1, source_target_pairs={{0,2},{1,3},{2,0},{3,1},{4,6},{5,7},{6,4},{7,5},{8,10},{9,11},{10,... | collective-permute-start | bytes 3145736 | tf_op jit(solution)/shard_map/ppermute | solution.py:874
  21.7 5.8 %norm_mlp.3 = (bf16[2,1024,1024]{2,1,0:T(8,128)(2,1)S(1)}, bf16[2,1024,1024]{2,1,0:T(8,128)(2,1)S(1)}, f32[1024,128]{1,0:T(8,128)S(1)}, f32[32,1024]{1,0:T(8,128)S(1)}, f32[32,256]{1,0:T(8,128)S(1)}) custom-call(s32[4]{0:T(128)S(1)} %pad_add_fusion.place, bf16[2048,256]{1,0:T(8,128)(2,1)S(1)} %copy-done, bf16[2048,256]{1,0:T(8,128)(2,1)S(1)} %collective-permute-done.x1, ...), custom_call_target="tpu_custom_call" | custom-call | flops 512000000 | bytes 1000000 | tf_op jit(solution)/shard_map/norm_mlp/pallas_call | solution.py:399
  27.6 3.0 %collective-permute-done.5.x2.c2 = bf16[1024,256]{1,0:T(8,128)(2,1)S(1)} collective-permute-done((bf16[1024,256]{1,0:T(8,128)(2,1)S(1)}, bf16[1024,256]{1,0:T(8,128)(2,1)S(1)}, u32[]{:S(2)}, u32[]{:S(2)}) %collective-permute-start.5) | collective-permute-done | bytes 524320 | tf_op jit(solution)/shard_map/ppermute | solution.py:874
  30.6 1.9 %collective-permute-done.6.x3.c3 = bf16[1024,256]{1,0:T(8,128)(2,1)S(1)} collective-permute-done((bf16[1024,256]{1,0:T(8,128)(2,1)S(1)}, bf16[1024,256]{1,0:T(8,128)(2,1)S(1)}, u32[]{:S(2)}, u32[]{:S(2)}) %collective-permute-start.6) | collective-permute-done | bytes 524320 | tf_op jit(solution)/shard_map/ppermute | solution.py:874
  32.5 5.0 %norm_mlp.4 = (bf16[2,1024,1024]{2,1,0:T(8,128)(2,1)S(1)}, bf16[2,1024,1024]{2,1,0:T(8,128)(2,1)S(1)}, f32[1024,128]{1,0:T(8,128)S(1)}, f32[32,1024]{1,0:T(8,128)S(1)}, f32[32,256]{1,0:T(8,128)S(1)}) custom-call(s32[4]{0:T(128)S(1)} %pad_add_fusion.place, ...), custom_call_target="tpu_custom_call", output_to_operand_aliasing={{0}: (14, {}), {1}: (15, {}), {2}: (16, {}), {3}: (17, {}),... | custom-call | flops 512000000 | bytes 1000000 | tf_op jit(solution)/shard_map/norm_mlp/pallas_call | solution.py:399
  37.6 13.9 %attend.2 = (bf16[1024,256]{1,0:T(8,128)(2,1)S(1)}, bf16[1024,768]{1,0:T(8,128)(2,1)S(1)}) custom-call(s32[4]{0:T(128)S(1)} %pad_add_fusion.place, bf16[2,1024,1024]{2,1,0:T(8,128)(2,1)S(1)} %get-tuple-element.130.left.left_0, bf16[1024,256]{1,0:T(8,128)(2,1)S(1)} %get-tuple-element.115.w_q, bf16[1024,256]{1,0:T(8,128)(2,1)S(1)} %get-tuple-element.131.w_k, ...), custom_call_target="tpu_custom_call" | custom-call | flops 1433600000 | bytes 1000000 | tf_op jit(solution)/shard_map/attend/pallas_call | solution.py:536
  51.5 0.7 collective-permute-done.7.x2.c2
  52.2 2.7 %collective-permute-done.8.x3.c3 = bf16[2048,256]{1,0:T(8,128)(2,1)S(1)} collective-permute-done((bf16[2048,256]{1,0:T(8,128)(2,1)S(1)}, bf16[2048,256]{1,0:T(8,128)(2,1)S(1)}, u32[]{:S(2)}, u32[]{:S(2)}) %collective-permute-start.8) | collective-permute-done | bytes 1048608 | tf_op jit(solution)/shard_map/ppermute | solution.py:874
  54.9 9.5 %norm_mlp.5 = (bf16[2,1024,1024]{2,1,0:T(8,128)(2,1)S(1)}, bf16[2,1024,1024]{2,1,0:T(8,128)(2,1)S(1)}, f32[1024,128]{1,0:T(8,128)S(1)}, f32[32,1024]{1,0:T(8,128)S(1)}, f32[32,256]{1,0:T(8,128)S(1)}) custom-call(s32[4]{0:T(128)S(1)} %pad_add_fusion.place, bf16[2048,256]{1,0:T(8,128)(2,1)S(1)} %copy-done, bf16[2048,256]{1,0:T(8,128)(2,1)S(1)} %copy-done.3, ...), custom_call_target="tpu_custom_call" | custom-call | flops 1024000000 | bytes 1000000 | tf_op jit(solution)/shard_map/norm_mlp/pallas_call | solution.py:399
  64.4 7.4 %weight_mlp.2 = (bf16[4,128,1024]{2,1,0:T(8,128)(2,1)}, bf16[4,128,1024]{2,1,0:T(8,128)(2,1)}) custom-call(s32[4]{0:T(128)S(1)} %pad_add_fusion.place, f32[1]{0:T(128)} %mul_shard_map.6.scale, bf16[2,1024,1024]{2,1,0:T(8,128)(2,1)S(1)} %get-tuple-element.130.left.left_0, bf16[2,1024,1024]{2,1,0:T(8,128)(2,1)S(1)} %get-tuple-element.141.left_1.left, ...), custom_call_target="tpu_custom_call" | custom-call | flops 665600000 | bytes 1000000 | tf_op jit(solution)/shard_map/weight_mlp/pallas_call | solution.py:626
  71.8 7.5 %weight_mlp.3 = (bf16[2,2,128,1024]{3,2,1,0:T(8,128)(2,1)}, bf16[2,2,128,1024]{3,2,1,0:T(8,128)(2,1)}) custom-call(s32[4]{0:T(128)S(1)} %pad_add_fusion.place, f32[1]{0:T(128)} %mul_shard_map.6.scale, bf16[2,1024,1024]{2,1,0:T(8,128)(2,1)S(1)} %get-tuple-element.130.left.left_0, bf16[2,1024,1024]{2,1,0:T(8,128)(2,1)S(1)} %get-tuple-element.141.left_1.left, ...), custom_call_target="tpu_custom_call" | custom-call | flops 665600000 | bytes 1000000 | tf_op jit(solution)/shard_map/weight_mlp/pallas_call | solution.py:626
  79.3 1.8 collective-permute-start.10
  81.2 1.5 collective-permute-start.9
  82.7 10.6 %branch_parts.2 = (bf16[2,2,1024,256]{3,2,1,0:T(8,128)(2,1)}, bf16[2,1024,256]{2,1,0:T(8,128)(2,1)}, bf16[1024,256]{1,0:T(8,128)(2,1)}, bf16[1024,256]{1,0:T(8,1...) custom-call(s32[4]{0:T(128)S(1)} %pad_add_fusion.place, ...), custom_call_target="tpu_custom_call" | custom-call | flops 1024000000 | bytes 1000000 | tf_op jit(solution)/shard_map/branch_parts/pallas_call | solution.py:718
  93.8 13.9 %attend.3 = (bf16[1024,256]{1,0:T(8,128)(2,1)S(1)}, bf16[1024,768]{1,0:T(8,128)(2,1)S(1)}) custom-call(s32[4]{0:T(128)S(1)} %pad_add_fusion.place, bf16[2,1024,1024]{2,1,0:T(8,128)(2,1)S(1)} %get-tuple-element.141.left_1.left, bf16[1024,256]{1,0:T(8,128)(2,1)S(1)} %get-tuple-element.115.w_q, bf16[1024,256]{1,0:T(8,128)(2,1)S(1)} %get-tuple-element.131.w_k, ...), custom_call_target="tpu_custom_call" | custom-call | flops 1433600000 | bytes 1000000 | tf_op jit(solution)/shard_map/attend/pallas_call | solution.py:536
  107.8 0.7 copy-done.21
  109.4 5.0 %combine.1 = (bf16[272,1024]{1,0:T(8,128)(2,1)}, bf16[2,128,1024]{2,1,0:T(8,128)(2,1)}, bf16[2,128,1024]{2,1,0:T(8,128)(2,1)}, bf16[2,128,1024]{2,1,0:T(8,128)(2,1)}, bf16[2,1024,256]{2,1,0:T(8,128)(2,1)}) custom-call(f32[1]{0:T(128)S(6)} %add.72.count, bf16[4,128,1024]{2,1,0:T(8,128)(2,1)} %get-tuple-element.144.keep_in, bf16[4,128,1024]{2,1,0:T(8,128)(2,1)} %copy-done.19, ...), custom_call_target="tpu_custom_call" | custom-call | flops 300000000 | bytes 1000000 | tf_op jit(solution)/shard_map/combine/pallas_call | solution.py:759
  114.3 1.6 collective-permute-start.16
  116.4 2.6 %collective-permute-start.15 = (bf16[2,128,1024]{2,1,0:T(8,128)(2,1)}, bf16[2,128,1024]{2,1,0:T(8,128)(2,1)S(1)}, u32[]{:S(2)}, u32[]{:S(2)}) collective-permute-start(bf16[2,128,1024]{2,1,0:T(8,128)(2,1)} %get-tuple-element.172), channel_id=1, source_target_pairs={{0,16},{4,20},{8,24},{12,28},{16,0},{20,4},{24,8},{28,12},{1,17},{... | collective-permute-start | bytes 1572872 | tf_op jit(solution)/shard_map/ppermute | solution.py:874
  118.9 7.8 %weight_att.1 = (bf16[4,128,1024]{2,1,0:T(8,128)(2,1)}, bf16[4,128,1024]{2,1,0:T(8,128)(2,1)}) custom-call(s32[4]{0:T(128)S(1)} %pad_add_fusion.place, f32[1]{0:T(128)} %mul_shard_map.6.scale, bf16[2,1024,1024]{2,1,0:T(8,128)(2,1)S(1)} %get-tuple-element.130.left.left_0, bf16[2,1024,1024]{2,1,0:T(8,128)(2,1)S(1)} %get-tuple-element.141.left_1.left, ...), custom_call_target="tpu_custom_call" | custom-call | flops 716800000 | bytes 1000000 | tf_op jit(solution)/shard_map/weight_att/pallas_call | solution.py:650
  127.3 10.8 %branch_parts.3 = (bf16[2,2,1024,256]{3,2,1,0:T(8,128)(2,1)}, bf16[2,1024,256]{2,1,0:T(8,128)(2,1)}, bf16[1024,256]{1,0:T(8,128)(2,1)}, bf16[1024,256]{1,0:T(8,1...) custom-call(s32[4]{0:T(128)S(1)} %pad_add_fusion.place, ...), custom_call_target="tpu_custom_call" | custom-call | flops 1024000000 | bytes 1000000 | tf_op jit(solution)/shard_map/branch_parts/pallas_call | solution.py:718
  138.2 2.0 %collective-permute-done.15 = bf16[2,128,1024]{2,1,0:T(8,128)(2,1)S(1)} collective-permute-done((bf16[2,128,1024]{2,1,0:T(8,128)(2,1)}, bf16[2,128,1024]{2,1,0:T(8,128)(2,1)S(1)}, u32[]{:S(2)}, u32[]{:S(2)}) %collective-permute-start.15) | collective-permute-done | bytes 524320 | tf_op jit(solution)/shard_map/ppermute | solution.py:874
  140.2 1.9 collective-permute-done.14.z_in
  143.0 1.5 collective-permute-start.17
  145.3 0.6 collective-permute-start.25
  145.8 5.8 %collective-permute-done.19 = bf16[4,128,1024]{2,1,0:T(8,128)(2,1)S(1)} collective-permute-done((bf16[4,128,1024]{2,1,0:T(8,128)(2,1)}, bf16[4,128,1024]{2,1,0:T(8,128)(2,1)S(1)}, u32[]{:S(2)}, u32[]{:S(2)}) %collective-permute-start.19) | collective-permute-done | bytes 1048608 | tf_op jit(solution)/shard_map/ppermute | solution.py:874
  151.9 0.6 collective-permute-start.22
  152.5 1.5 collective-permute-start.27
  154.5 1.4 collective-permute-done.22
  155.9 1.6 collective-permute-start.23
  157.5 2.2 %collective-permute-done.17.far_in = bf16[144,1024]{1,0:T(8,128)(2,1)S(1)} collective-permute-done((bf16[144,1024]{1,0:T(8,128)(2,1)S(1)}, bf16[144,1024]{1,0:T(8,128)(2,1)S(1)}, u32[]{:S(2)}, u32[]{:S(2)}) %collective-permute-start.17) | collective-permute-done | bytes 294944 | tf_op jit(solution)/shard_map/ppermute | solution.py:874
  159.9 11.0 %collective-permute-done.26 = f32[2,2048]{1,0:T(2,128)S(1)} collective-permute-done((f32[2,2048]{1,0:T(2,128)S(1)}, f32[2,2048]{1,0:T(2,128)S(1)}, u32[]{:S(2)}, u32[]{:S(2)}) %collective-permute-start.26) | collective-permute-done | bytes 16416 | tf_op jit(solution)/shard_map/ppermute | solution.py:874
  171.5 1.2 collective-permute-start.29
  172.6 1.8 collective-permute-start.30
  174.4 3.7 %finish_rows.2 = (bf16[2048,256]{1,0:T(8,128)(2,1)}, f32[2048,256]{1,0:T(8,128)}) custom-call(s32[4]{0:T(128)S(1)} %pad_add_fusion.place, f32[1]{0:T(128)S(6)} %mul.27.scale, bf16[2,2,1024,256]{3,2,1,0:T(8,128)(2,1)} %get-tuple-element.159.kept.keep, bf16[2,1024,256]{2,1,0:T(8,128)(2,1)} %copy-done.16, bf16[2,1024,256]{2,1,0:T(8,128)(2,1)} %copy-done.17, ...), custom_call_target="tpu_custom_call" | custom-call | flops 307200000 | bytes 1000000 | tf_op jit(solution)/shard_map/finish_rows/pallas_call | solution.py:830
  178.1 3.7 %finish_rows.3 = (bf16[2048,256]{1,0:T(8,128)(2,1)}, f32[2048,256]{1,0:T(8,128)}) custom-call(s32[4]{0:T(128)S(1)} %pad_add_fusion.place, f32[1]{0:T(128)S(6)} %mul.27.scale, bf16[2,2,1024,256]{3,2,1,0:T(8,128)(2,1)} %get-tuple-element.185.keep, bf16[2,1024,256]{2,1,0:T(8,128)(2,1)} %collective-permute-done.28.near, ...), custom_call_target="tpu_custom_call", output_to_operand_aliasing={{0}: (11, {}), {1}: (12, {})} | custom-call | flops 307200000 | bytes 1000000 | tf_op jit(solution)/shard_map/finish_rows/pallas_call | solution.py:830
  181.9 0.6 collective-permute-start.31
  182.5 0.6 slice.155
  183.6 4.3 %collective-permute-done.30.far_a = bf16[128,1024]{1,0:T(8,128)(2,1)S(1)} collective-permute-done((bf16[128,1024]{1,0:T(8,128)(2,1)S(1)}, bf16[128,1024]{1,0:T(8,128)(2,1)S(1)}, u32[]{:S(2)}, u32[]{:S(2)}) %collective-permute-start.30) | collective-permute-done | bytes 262176 | tf_op jit(solution)/shard_map/ppermute | solution.py:874
  188.5 0.6 dynamic-slice_divide_fusion
  189.1 1.3 finish_weights.1
  (121 shorter events, 8.0 us)
Async XLA Ops:
  3.4 16.0 %collective-permute-start.1 = (bf16[1024,256]{1,0:T(8,128)(2,1)}, bf16[1024,256]{1,0:T(8,128)(2,1)}, u32[]{:S(2)}, u32[]{:S(2)}) collective-permute-start(bf16[1024,256]{1,0:T(8,128)(2,1)} %pad_maximum_fusion.1), channel_id=1, source_target_pairs={{0,2},{1,3},{2,0},{3,1},{4,6},{5,7},{6,4},{7,5},{8,10},{9,11},{10,... | collective-permute-start | bytes 1572872 | tf_op jit(solution)/shard_map/ppermute | solution.py:874
  6.4 15.3 %collective-permute-start = (bf16[2048,256]{1,0:T(8,128)(2,1)}, bf16[2048,256]{1,0:T(8,128)(2,1)S(1)}, u32[]{:S(2)}, u32[]{:S(2)}) collective-permute-start(bf16[2048,256]{1,0:T(8,128)(2,1)} %x_ref.3), channel_id=1, source_target_pairs={{0,1},{1,0},{2,3},{3,2},{4,5},{5,4},{6,7},{7,6},{8,9},{9,8},{10,11... | collective-permute-start | bytes 3145736 | tf_op jit(solution)/shard_map/ppermute | solution.py:874
  6.4 15.3 %collective-permute-start.4 = (bf16[2048,256]{1,0:T(8,128)(2,1)}, bf16[2048,256]{1,0:T(8,128)(2,1)S(1)}, u32[]{:S(2)}, u32[]{:S(2)}) collective-permute-start(bf16[2048,256]{1,0:T(8,128)(2,1)} %cot.3), channel_id=1, source_target_pairs={{0,1},{1,0},{2,3},{3,2},{4,5},{5,4},{6,7},{7,6},{8,9},{9,8},{10,11... | collective-permute-start | bytes 3145736 | tf_op jit(solution)/shard_map/ppermute | solution.py:874
  7.5 6.7 %collective-permute-start.2 = (f32[1]{0:T(128)}, f32[1]{0:T(128)}, u32[]{:S(2)}, u32[]{:S(2)}) collective-permute-start(f32[1]{0:T(128)} %mul_shard_map.6.scale), channel_id=1, source_target_pairs={{0,4},{4,0},{8,12},{12,8},{16,20},{20,16},{24,28},{28,24},{1,5},{5... | collective-permute-start | bytes 20 | tf_op jit(solution)/shard_map/ppermute | solution.py:874
  15.1 6.6 %copy-start.9 = (f32[1024]{0:T(1024)S(1)}, f32[1024]{0:T(1024)}, u32[]{:S(2)}) copy-start(f32[1024]{0:T(1024)} %param.16) | copy-start | bytes 12292
  15.1 6.6 %copy-start.10 = (f32[1024]{0:T(1024)S(1)}, f32[1024]{0:T(1024)}, u32[]{:S(2)}) copy-start(f32[1024]{0:T(1024)} %param.17) | copy-start | bytes 12292
  15.2 15.4 %collective-permute-start.5 = (bf16[1024,256]{1,0:T(8,128)(2,1)S(1)}, bf16[1024,256]{1,0:T(8,128)(2,1)S(1)}, u32[]{:S(2)}, u32[]{:S(2)}) collective-permute-start(bf16[1024,256]{1,0:T(8,128)(2,1)S(1)} %pad_maximum_fusion.2), channel_id=1, source_target_pairs={{0,2},{1,3},{2,0},{3,1},{4,6},{5,7},{6,4},{7,5},{8,10},{9,11},{10,... | collective-permute-start | bytes 1572872 | tf_op jit(solution)/shard_map/ppermute | solution.py:874
  19.4 2.2 %collective-permute-start.3 = (bf16[1024,256]{1,0:T(8,128)(2,1)}, bf16[1024,256]{1,0:T(8,128)(2,1)S(1)}, u32[]{:S(2)}, u32[]{:S(2)}) collective-permute-start(bf16[1024,256]{1,0:T(8,128)(2,1)} %collective-permute-done.1.x2.c2), channel_id=1, source_target_pairs={{0,1},{1,0},{2,3},{3,2},{4,5},{5,4},{6,7},{7,6},{8,9},{9,8},{10,11... | collective-permute-start | bytes 1572872 | tf_op jit(solution)/shard_map/ppermute | solution.py:874
  19.5 32.7 %collective-permute-start.7 = (bf16[2048,256]{1,0:T(8,128)(2,1)S(1)}, bf16[2048,256]{1,0:T(8,128)(2,1)S(1)}, u32[]{:S(2)}, u32[]{:S(2)}) collective-permute-start(bf16[2048,256]{1,0:T(8,128)(2,1)S(1)} %pad_maximum_fusion), channel_id=1, source_target_pairs={{0,2},{1,3},{2,0},{3,1},{4,6},{5,7},{6,4},{7,5},{8,10},{9,11},{10,... | collective-permute-start | bytes 3145736 | tf_op jit(solution)/shard_map/ppermute | solution.py:874
  21.7 10.8 %copy-start.2 = (bf16[2048,256]{1,0:T(8,128)(2,1)}, bf16[2048,256]{1,0:T(8,128)(2,1)S(1)}, u32[]{:S(2)}) copy-start(bf16[2048,256]{1,0:T(8,128)(2,1)S(1)} %collective-permute-done.x1) | copy-start | bytes 3145732
  21.7 10.8 %copy-start.4 = (bf16[2048,256]{1,0:T(8,128)(2,1)}, bf16[2048,256]{1,0:T(8,128)(2,1)S(1)}, u32[]{:S(2)}) copy-start(bf16[2048,256]{1,0:T(8,128)(2,1)S(1)} %collective-permute-done.4.c1) | copy-start | bytes 3145732
  30.6 1.9 %collective-permute-start.6 = (bf16[1024,256]{1,0:T(8,128)(2,1)S(1)}, bf16[1024,256]{1,0:T(8,128)(2,1)S(1)}, u32[]{:S(2)}, u32[]{:S(2)}) collective-permute-start(bf16[1024,256]{1,0:T(8,128)(2,1)S(1)} %collective-permute-done.5.x2.c2), channel_id=1, source_target_pairs={{0,1},{1,0},{2,3},{3,2},{4,5},{5,4},{6,7},{7,6},{8,9},{9,8},{10,11... | collective-permute-start | bytes 1572872 | tf_op jit(solution)/shard_map/ppermute | solution.py:874
  37.5 14.0 %copy-start.6 = (f32[1024,128]{1,0:T(8,128)}, f32[1024,128]{1,0:T(8,128)S(1)}, u32[]{:S(2)}) copy-start(f32[1024,128]{1,0:T(8,128)S(1)} %get-tuple-element.207.stats) | copy-start | bytes 1572868
  37.6 17.3 %copy-start.3 = (bf16[2048,256]{1,0:T(8,128)(2,1)S(1)}, bf16[2048,256]{1,0:T(8,128)(2,1)}, u32[]{:S(2)}) copy-start(bf16[2048,256]{1,0:T(8,128)(2,1)} %copy-done.2) | copy-start | bytes 3145732
  37.6 17.3 %copy-start.5 = (bf16[2048,256]{1,0:T(8,128)(2,1)S(1)}, bf16[2048,256]{1,0:T(8,128)(2,1)}, u32[]{:S(2)}) copy-start(bf16[2048,256]{1,0:T(8,128)(2,1)} %copy-done.4) | copy-start | bytes 3145732
  52.2 2.7 %collective-permute-start.8 = (bf16[2048,256]{1,0:T(8,128)(2,1)S(1)}, bf16[2048,256]{1,0:T(8,128)(2,1)S(1)}, u32[]{:S(2)}, u32[]{:S(2)}) collective-permute-start(bf16[2048,256]{1,0:T(8,128)(2,1)S(1)} %collective-permute-done.7.x2.c2), channel_id=1, source_target_pairs={{0,1},{1,0},{2,3},{3,2},{4,5},{5,4},{6,7},{7,6},{8,9},{9,8},{10,11... | collective-permute-start | bytes 3145736 | tf_op jit(solution)/shard_map/ppermute | solution.py:874
  64.4 7.4 %copy-start.7 = (f32[1024,128]{1,0:T(8,128)}, f32[1024,128]{1,0:T(8,128)S(1)}, u32[]{:S(2)}) copy-start(f32[1024,128]{1,0:T(8,128)S(1)} %get-tuple-element.205.stats) | copy-start | bytes 1572868
  71.8 9.4 %copy-start.24 = (bf16[4,128,1024]{2,1,0:T(8,128)(2,1)S(1)}, bf16[4,128,1024]{2,1,0:T(8,128)(2,1)}, u32[]{:S(2)}) copy-start(bf16[4,128,1024]{2,1,0:T(8,128)(2,1)} %get-tuple-element.151) | copy-start | bytes 3145732
  79.3 28.4 %collective-permute-start.10 = (bf16[2,2,128,1024]{3,2,1,0:T(8,128)(2,1)}, bf16[2,2,128,1024]{3,2,1,0:T(8,128)(2,1)S(1)}, u32[]{:S(2)}, u32[]{:S(2)}) collective-permute-start(bf16[2,2,128,1024]{3,2,1,0:T(8,128)(2,1)} %get-tuple-element.152), channel_id=1, source_target_pairs={{0,8},{4,12},{8,0},{12,4},{16,24},{20,28},{24,16},{28,20},{1,9},{5... | collective-permute-start | bytes 3145736 | tf_op jit(solution)/shard_map/ppermute | solution.py:874
  81.2 26.6 %collective-permute-start.9 = (bf16[4,128,1024]{2,1,0:T(8,128)(2,1)S(1)}, bf16[4,128,1024]{2,1,0:T(8,128)(2,1)S(1)}, u32[]{:S(2)}, u32[]{:S(2)}) collective-permute-start(bf16[4,128,1024]{2,1,0:T(8,128)(2,1)S(1)} %copy-done.24), channel_id=1, source_target_pairs={{0,4},{4,0},{8,12},{12,8},{16,20},{20,16},{24,28},{28,24},{1,5},{5... | collective-permute-start | bytes 3145736 | tf_op jit(solution)/shard_map/ppermute | solution.py:874
  93.3 14.4 %collective-permute-start.11 = (bf16[1024,256]{1,0:T(8,128)(2,1)}, bf16[1024,256]{1,0:T(8,128)(2,1)S(1)}, u32[]{:S(2)}, u32[]{:S(2)}) collective-permute-start(bf16[1024,256]{1,0:T(8,128)(2,1)} %get-tuple-element.153), channel_id=1, source_target_pairs={{0,1},{1,0},{2,3},{3,2},{4,5},{5,4},{6,7},{7,6},{8,9},{9,8},{10,11... | collective-permute-start | bytes 1572872 | tf_op jit(solution)/shard_map/ppermute | solution.py:874
  93.3 14.5 %collective-permute-start.12 = (bf16[1024,256]{1,0:T(8,128)(2,1)}, bf16[1024,256]{1,0:T(8,128)(2,1)S(1)}, u32[]{:S(2)}, u32[]{:S(2)}) collective-permute-start(bf16[1024,256]{1,0:T(8,128)(2,1)} %get-tuple-element.154), channel_id=1, source_target_pairs={{0,1},{1,0},{2,3},{3,2},{4,5},{5,4},{6,7},{7,6},{8,9},{9,8},{10,11... | collective-permute-start | bytes 1572872 | tf_op jit(solution)/shard_map/ppermute | solution.py:874
  114.3 13.0 %collective-permute-start.13 = (bf16[2,1024,256]{2,1,0:T(8,128)(2,1)S(1)}, bf16[2,1024,256]{2,1,0:T(8,128)(2,1)S(1)}, u32[]{:S(2)}, u32[]{:S(2)}) collective-permute-start(bf16[2,1024,256]{2,1,0:T(8,128)(2,1)S(1)} %copy-done.23), channel_id=1, source_target_pairs={{0,1},{1,0},{2,3},{3,2},{4,5},{5,4},{6,7},{7,6},{8,9},{9,8},{10,11... | collective-permute-start | bytes 3145736 | tf_op jit(solution)/shard_map/ppermute | solution.py:874
  114.3 27.7 %collective-permute-start.16 = (bf16[2,1024,256]{2,1,0:T(8,128)(2,1)}, bf16[2,1024,256]{2,1,0:T(8,128)(2,1)S(1)}, u32[]{:S(2)}, u32[]{:S(2)}) collective-permute-start(bf16[2,1024,256]{2,1,0:T(8,128)(2,1)} %get-tuple-element.164), channel_id=1, source_target_pairs={{0,2},{1,3},{2,0},{3,1},{4,6},{5,7},{6,4},{7,5},{8,10},{9,11},{10,... | collective-permute-start | bytes 3145736 | tf_op jit(solution)/shard_map/ppermute | solution.py:874
  115.9 26.1 %collective-permute-start.14 = (bf16[272,1024]{1,0:T(8,128)(2,1)}, bf16[272,1024]{1,0:T(8,128)(2,1)S(1)}, u32[]{:S(2)}, u32[]{:S(2)}) collective-permute-start(bf16[272,1024]{1,0:T(8,128)(2,1)} %get-tuple-element.171), channel_id=1, source_target_pairs={{0,8},{4,12},{8,0},{12,4},{16,24},{20,28},{24,16},{28,20},{1,9},{5... | collective-permute-start | bytes 1671176 | tf_op jit(solution)/shard_map/ppermute | solution.py:874
  116.4 23.8 %collective-permute-start.15 = (bf16[2,128,1024]{2,1,0:T(8,128)(2,1)}, bf16[2,128,1024]{2,1,0:T(8,128)(2,1)S(1)}, u32[]{:S(2)}, u32[]{:S(2)}) collective-permute-start(bf16[2,128,1024]{2,1,0:T(8,128)(2,1)} %get-tuple-element.172), channel_id=1, source_target_pairs={{0,16},{4,20},{8,24},{12,28},{16,0},{20,4},{24,8},{28,12},{1,17},{... | collective-permute-start | bytes 1572872 | tf_op jit(solution)/shard_map/ppermute | solution.py:874
  126.8 24.9 %collective-permute-start.19 = (bf16[4,128,1024]{2,1,0:T(8,128)(2,1)}, bf16[4,128,1024]{2,1,0:T(8,128)(2,1)S(1)}, u32[]{:S(2)}, u32[]{:S(2)}) collective-permute-start(bf16[4,128,1024]{2,1,0:T(8,128)(2,1)} %get-tuple-element.184), channel_id=1, source_target_pairs={{0,4},{4,0},{8,12},{12,8},{16,20},{20,16},{24,28},{28,24},{1,5},{5... | collective-permute-start | bytes 3145736 | tf_op jit(solution)/shard_map/ppermute | solution.py:874
  127.3 10.9 %copy-start.16 = (bf16[2,1024,256]{2,1,0:T(8,128)(2,1)}, bf16[2,1024,256]{2,1,0:T(8,128)(2,1)S(1)}, u32[]{:S(2)}) copy-start(bf16[2,1024,256]{2,1,0:T(8,128)(2,1)S(1)} %collective-permute-done.13.near) | copy-start | bytes 3145732
  127.3 15.5 %copy-start.20 = (bf16[2,128,1024]{2,1,0:T(8,128)(2,1)S(1)}, bf16[2,128,1024]{2,1,0:T(8,128)(2,1)}, u32[]{:S(2)}) copy-start(bf16[2,128,1024]{2,1,0:T(8,128)(2,1)} %get-tuple-element.163) | copy-start | bytes 1572868
  127.3 15.6 %copy-start.8 = (bf16[2,128,1024]{2,1,0:T(8,128)(2,1)S(1)}, bf16[2,128,1024]{2,1,0:T(8,128)(2,1)}, u32[]{:S(2)}) copy-start(bf16[2,128,1024]{2,1,0:T(8,128)(2,1)} %get-tuple-element.162.low) | copy-start | bytes 1572868
  138.2 6.9 %copy-start.13 = (bf16[2,2,1024,256]{3,2,1,0:T(8,128)(2,1)S(1)}, bf16[2,2,1024,256]{3,2,1,0:T(8,128)(2,1)}, u32[]{:S(2)}) copy-start(bf16[2,2,1024,256]{3,2,1,0:T(8,128)(2,1)} %get-tuple-element.185.keep) | copy-start | bytes 6291460
  142.1 2.5 %collective-permute-start.20 = (bf16[1024,256]{1,0:T(8,128)(2,1)}, bf16[1024,256]{1,0:T(8,128)(2,1)S(1)}, u32[]{:S(2)}, u32[]{:S(2)}) collective-permute-start(bf16[1024,256]{1,0:T(8,128)(2,1)} %get-tuple-element.186), channel_id=1, source_target_pairs={{0,1},{1,0},{2,3},{3,2},{4,5},{5,4},{6,7},{7,6},{8,9},{9,8},{10,11... | collective-permute-start | bytes 1572872 | tf_op jit(solution)/shard_map/ppermute | solution.py:874
  142.1 2.9 %collective-permute-start.21 = (bf16[1024,256]{1,0:T(8,128)(2,1)}, bf16[1024,256]{1,0:T(8,128)(2,1)S(1)}, u32[]{:S(2)}, u32[]{:S(2)}) collective-permute-start(bf16[1024,256]{1,0:T(8,128)(2,1)} %get-tuple-element.190), channel_id=1, source_target_pairs={{0,1},{1,0},{2,3},{3,2},{4,5},{5,4},{6,7},{7,6},{8,9},{9,8},{10,11... | collective-permute-start | bytes 1572872 | tf_op jit(solution)/shard_map/ppermute | solution.py:874
  142.7 1.8 collective-permute-start.18
  142.9 8.8 %copy-start.15 = (bf16[4,128,1024]{2,1,0:T(8,128)(2,1)S(1)}, bf16[4,128,1024]{2,1,0:T(8,128)(2,1)}, u32[]{:S(2)}) copy-start(bf16[4,128,1024]{2,1,0:T(8,128)(2,1)} %get-tuple-element.167) | copy-start | bytes 3145732
  143.0 16.7 %collective-permute-start.17 = (bf16[144,1024]{1,0:T(8,128)(2,1)S(1)}, bf16[144,1024]{1,0:T(8,128)(2,1)S(1)}, u32[]{:S(2)}, u32[]{:S(2)}) collective-permute-start(bf16[144,1024]{1,0:T(8,128)(2,1)S(1)} %get-tuple-element.177), channel_id=1, source_target_pairs={{0,16},{4,20},{8,24},{12,28},{16,0},{20,4},{24,8},{28,12},{1,17},{... | collective-permute-start | bytes 884744 | tf_op jit(solution)/shard_map/ppermute | solution.py:874
  145.2 29.1 %copy-start.12 = (f32[256]{0:T(256)S(1)}, f32[256]{0:T(256)}, u32[]{:S(2)}) copy-start(f32[256]{0:T(256)} %param.23) | copy-start | bytes 3076
  145.3 25.6 %collective-permute-start.25 = (bf16[2,1024,256]{2,1,0:T(8,128)(2,1)S(1)}, bf16[2,1024,256]{2,1,0:T(8,128)(2,1)S(1)}, u32[]{:S(2)}, u32[]{:S(2)}) collective-permute-start(bf16[2,1024,256]{2,1,0:T(8,128)(2,1)S(1)} %maximum_add_fusion), channel_id=1, source_target_pairs={{0,2},{1,3},{2,0},{3,1},{4,6},{5,7},{6,4},{7,5},{8,10},{9,11},{10,... | collective-permute-start | bytes 3145736 | tf_op jit(solution)/shard_map/ppermute | solution.py:874
  151.9 4.0 %collective-permute-start.22 = (f32[3328]{0:T(1024)S(1)}, f32[3328]{0:T(1024)S(1)}, u32[]{:S(2)}, u32[]{:S(2)}) collective-permute-start(f32[3328]{0:T(1024)S(1)} %maximum_multiply_fusion), channel_id=1, source_target_pairs={{0,4},{4,0},{8,12},{12,8},{16,20},{20,16},{24,28},{28,24},{1,5},{5... | collective-permute-start | bytes 39944 | tf_op jit(solution)/shard_map/ppermute | solution.py:874
  152.5 7.4 %collective-permute-start.27 = (bf16[128,1024]{1,0:T(8,128)(2,1)S(1)}, bf16[128,1024]{1,0:T(8,128)(2,1)S(1)}, u32[]{:S(2)}, u32[]{:S(2)}) collective-permute-start(bf16[128,1024]{1,0:T(8,128)(2,1)S(1)} %get-tuple-element.224), channel_id=1, source_target_pairs={{0,4},{4,0},{8,12},{12,8},{16,20},{20,16},{24,28},{28,24},{1,5},{5... | collective-permute-start | bytes 786440 | tf_op jit(solution)/shard_map/ppermute | solution.py:874
  154.0 16.9 %collective-permute-start.26 = (f32[2,2048]{1,0:T(2,128)S(1)}, f32[2,2048]{1,0:T(2,128)S(1)}, u32[]{:S(2)}, u32[]{:S(2)}) collective-permute-start(f32[2,2048]{1,0:T(2,128)S(1)} %slice.150), channel_id=1, source_target_pairs={{0,2},{1,3},{2,0},{3,1},{4,6},{5,7},{6,4},{7,5},{8,10},{9,11},{10,... | collective-permute-start | bytes 49160 | tf_op jit(solution)/shard_map/ppermute | solution.py:874
  155.9 15.3 %collective-permute-start.23 = (bf16[2,128,1024]{2,1,0:T(8,128)(2,1)S(1)}, bf16[2,128,1024]{2,1,0:T(8,128)(2,1)S(1)}, u32[]{:S(2)}, u32[]{:S(2)}) collective-permute-start(bf16[2,128,1024]{2,1,0:T(8,128)(2,1)S(1)} %get-tuple-element.220), channel_id=1, source_target_pairs={{0,8},{4,12},{8,0},{12,4},{16,24},{20,28},{24,16},{28,20},{1,9},{5... | collective-permute-start | bytes 1572872 | tf_op jit(solution)/shard_map/ppermute | solution.py:874
  159.7 11.5 %collective-permute-start.24 = (f32[3328]{0:T(1024)S(1)}, f32[3328]{0:T(1024)S(1)}, u32[]{:S(2)}, u32[]{:S(2)}) collective-permute-start(f32[3328]{0:T(1024)S(1)} %fusion.4), channel_id=1, source_target_pairs={{0,8},{4,12},{8,0},{12,4},{16,24},{20,28},{24,16},{28,20},{1,9},{5... | collective-permute-start | bytes 39944 | tf_op jit(solution)/shard_map/ppermute | solution.py:874
  170.9 7.2 %copy-start.14 = (bf16[2,1024,256]{2,1,0:T(8,128)(2,1)}, bf16[2,1024,256]{2,1,0:T(8,128)(2,1)S(1)}, u32[]{:S(2)}) copy-start(bf16[2,1024,256]{2,1,0:T(8,128)(2,1)S(1)} %collective-permute-done.25.far) | copy-start | bytes 3145732
  171.3 6.8 %collective-permute-start.28 = (bf16[2,1024,256]{2,1,0:T(8,128)(2,1)}, bf16[2,1024,256]{2,1,0:T(8,128)(2,1)}, u32[]{:S(2)}, u32[]{:S(2)}) collective-permute-start(bf16[2,1024,256]{2,1,0:T(8,128)(2,1)} %get-tuple-element.203), channel_id=1, source_target_pairs={{0,1},{1,0},{2,3},{3,2},{4,5},{5,4},{6,7},{7,6},{8,9},{9,8},{10,11... | collective-permute-start | bytes 3145736 | tf_op jit(solution)/shard_map/ppermute | solution.py:874
  171.5 10.4 %collective-permute-start.29 = (f32[3328]{0:T(1024)S(1)}, f32[3328]{0:T(1024)S(1)}, u32[]{:S(2)}, u32[]{:S(2)}) collective-permute-start(f32[3328]{0:T(1024)S(1)} %add.88), channel_id=1, source_target_pairs={{0,16},{4,20},{8,24},{12,28},{16,0},{20,4},{24,8},{28,12},{1,17},{... | collective-permute-start | bytes 39944 | tf_op jit(solution)/shard_map/ppermute | solution.py:874
  172.6 15.3 %collective-permute-start.30 = (bf16[128,1024]{1,0:T(8,128)(2,1)S(1)}, bf16[128,1024]{1,0:T(8,128)(2,1)S(1)}, u32[]{:S(2)}, u32[]{:S(2)}) collective-permute-start(bf16[128,1024]{1,0:T(8,128)(2,1)S(1)} %get-tuple-element.222), channel_id=1, source_target_pairs={{0,16},{4,20},{8,24},{12,28},{16,0},{20,4},{24,8},{28,12},{1,17},{... | collective-permute-start | bytes 786440 | tf_op jit(solution)/shard_map/ppermute | solution.py:874
  181.9 6.0 %collective-permute-start.31 = (f32[2,1024]{1,0:T(2,128)S(1)}, f32[2,1024]{1,0:T(2,128)S(1)}, u32[]{:S(2)}, u32[]{:S(2)}) collective-permute-start(f32[2,1024]{1,0:T(2,128)S(1)} %reshape.64), channel_id=1, source_target_pairs={{0,2},{1,3},{2,0},{3,1},{4,6},{5,7},{6,4},{7,5},{8,10},{9,11},{10,... | collective-permute-start | bytes 24584 | tf_op jit(solution)/shard_map/ppermute | solution.py:874
  (9 other events, 28.4 us)
